TPU v7x, 32 devices: a whole 2x2x4 slice. The times are simulated.
32 devices in a mesh: seq: 4 (over x, core), fsdp: 4 (over z), tensor: 2 (over y).
Axes of the slice: x: 2, y: 2, z: 4, core: 2. Of those that a mesh axis runs over, the one named last changes fastest.
Arguments:
- layer_input: bfloat16 [4096, 2304], P(('seq', 'fsdp')), may hold values from -6 to 6
- positions: int32 [4096], P(('seq', 'fsdp')), may hold values from 0 to 3839, as said below
- gain_attn_in: bfloat16 [2304], P(('seq', 'fsdp')), may hold values from 0.25 to 1.75
- w_query: bfloat16 [2304, 2048], P(('seq', 'fsdp'), 'tensor'), may hold values from -0.21875 to 0.21875
- w_key: bfloat16 [2304, 1024], P(('seq', 'fsdp'), 'tensor'), may hold values from -0.21875 to 0.21875
- w_value: bfloat16 [2304, 1024], P(('seq', 'fsdp'), 'tensor'), may hold values from -0.125 to 0.125
- w_out: bfloat16 [2048, 2304], P('tensor', ('seq', 'fsdp')), may hold values from -0.125 to 0.125
- gain_attn_out: bfloat16 [2304], P(('seq', 'fsdp')), may hold values from 0.25 to 1.75
- gain_ffn_in: bfloat16 [2304], P(('seq', 'fsdp')), may hold values from 0.25 to 1.75
- w_gate: bfloat16 [2304, 9216], P(None, ('fsdp', 'tensor')), may hold values from -0.125 to 0.125
- w_up: bfloat16 [2304, 9216], P(None, ('fsdp', 'tensor')), may hold values from -0.125 to 0.125
- w_down: bfloat16 [9216, 2304], P(('fsdp', 'tensor')), may hold values from -0.0625 to 0.0625
- gain_ffn_out: bfloat16 [2304], P(('seq', 'fsdp')), may hold values from 0.25 to 1.75
- cotangent: bfloat16 [4096, 2304], P(('seq', 'fsdp', 'tensor')), may hold values from -6 to 6
Outputs:
- output: bfloat16 [4096, 2304], P(('seq', 'fsdp', 'tensor'))
- grad_input: float32 [4096, 2304], P(('seq', 'fsdp', 'tensor'))
- grad_gain_attn_in: float32 [2304], P(('seq', 'fsdp'))
- grad_w_query: float32 [2304, 2048], P(('seq', 'fsdp'), 'tensor')
- grad_w_key: float32 [2304, 1024], P(('seq', 'fsdp'), 'tensor')
- grad_w_value: float32 [2304, 1024], P(('seq', 'fsdp'), 'tensor')
- grad_w_out: float32 [2048, 2304], P('tensor', ('seq', 'fsdp'))
- grad_gain_attn_out: float32 [2304], P(('seq', 'fsdp'))
- grad_gain_ffn_in: float32 [2304], P(('seq', 'fsdp'))
- grad_w_gate: float32 [2304, 9216], P(None, ('fsdp', 'tensor'))
- grad_w_up: float32 [2304, 9216], P(None, ('fsdp', 'tensor'))
- grad_w_down: float32 [9216, 2304], P(('fsdp', 'tensor'))
- grad_gain_ffn_out: float32 [2304], P(('seq', 'fsdp'))
Inputs may be any that keep to these rules, and one draw needn't show every extreme that they name: `positions`: positions restart at 0 at each document's first token and rise by one per token. One document holds exactly 3840 tokens and starts within the first 256 tokens; the tokens before it and after it form further documents, each shorter than 256 tokens.
All inputs are finite; a program needn't handle non-finite values.
Results may differ from a plain program's by a relative error of at most 0.02.
Values may be sent and summed in bfloat16 or wider, within the bound.
No kernel may reach another device: no remote copies, remote signals or barrier semaphores. Data moves between devices by JAX's collectives and lax.ppermute only.
A program may use at most 320 MiB of HBM per device.

v0:
```python
import jax
import jax.numpy as jnp
from jax import lax
from jax.sharding import PartitionSpec as P

HEAD = 256
WINDOW = 4096


epsilon = 1e-06
soft_cap = 50.0
rotary_base = 10000.0


def passed_along(x, axis, by):
    length = lax.axis_size(axis)
    pairs = [(i, i + by) for i in range(length) if 0 <= i + by < length]
    return lax.ppermute(x, axis, pairs)


def normalize(values):
    return values * lax.rsqrt(jnp.mean(values * values, axis=-1, keepdims=True) + epsilon)


def normalize_back(values, gain, incoming):
    scale = lax.rsqrt(jnp.mean(values * values, axis=-1, keepdims=True) + epsilon)
    unit = values * scale
    weighted = incoming * gain
    grad_values = scale * (weighted - unit * jnp.mean(weighted * unit, axis=-1, keepdims=True))
    return (grad_values, jnp.sum(incoming * unit, axis=0))


def rotary_tables(positions):
    freqs = rotary_base ** (-2.0 * jnp.arange(HEAD // 2, dtype=jnp.float32) / HEAD)
    angles = positions.astype(jnp.float32)[:, None] * freqs[None, :]
    return (jnp.cos(angles), jnp.sin(angles))


def rotate(values, cosine_table, sine_table):
    half_width = values.shape[-1] // 2
    front_half = values[..., :half_width]
    back_half = values[..., half_width:]
    cosine_part = cosine_table[:, None, :]
    sine_part = sine_table[:, None, :]
    return jnp.concatenate(
        [
            front_half * cosine_part - back_half * sine_part,
            back_half * cosine_part + front_half * sine_part,
        ],
        axis=-1,
    )


def rotate_back(values, cosine_table, sine_table):
    half_width = values.shape[-1] // 2
    front_half = values[..., :half_width]
    back_half = values[..., half_width:]
    cosine_part = cosine_table[:, None, :]
    sine_part = sine_table[:, None, :]
    return jnp.concatenate(
        [
            front_half * cosine_part + back_half * sine_part,
            back_half * cosine_part - front_half * sine_part,
        ],
        axis=-1,
    )


def gated_gelu(gate, up_proj):
    return jax.nn.gelu(gate, approximate=True) * up_proj


def attend(query_slice, key_slice, value_slice, visible):
    attention_scores = jnp.einsum(
        "ofx,hx->ofh", query_slice, key_slice, preferred_element_type=jnp.float32
    )
    capped = soft_cap * jnp.tanh(attention_scores / soft_cap)
    capped = jnp.where(visible[None], capped, -1e30)
    top_score = jnp.max(capped, axis=-1, keepdims=True)
    weights = jnp.exp(capped - top_score)
    total = jnp.sum(weights, axis=-1, keepdims=True)
    attention_output = (weights / total).astype(jnp.bfloat16)
    final_output = jnp.einsum(
        "qah,he->qae", attention_output, value_slice, preferred_element_type=jnp.float32
    )
    return (final_output, top_score[..., 0] + jnp.log(total[..., 0]))


def attend_back(query_slice, key_slice, value_slice, gradient_slice, log_total, visible):
    attention_scores = jnp.einsum(
        "ofx,hx->ofh", query_slice, key_slice, preferred_element_type=jnp.float32
    )
    bent = jnp.tanh(attention_scores / soft_cap)
    capped = soft_cap * bent
    exponent = jnp.where(visible[None], capped - log_total[..., None], -1e30)
    attention_output = jnp.exp(exponent)
    grad_attention = jnp.einsum(
        "ofx,hx->ofh", gradient_slice, value_slice, preferred_element_type=jnp.float32
    )
    inner = jnp.sum(attention_output * grad_attention, axis=-1, keepdims=True)
    score_gradient = (attention_output * (grad_attention - inner) * (1.0 - bent * bent)).astype(
        jnp.bfloat16
    )
    grad_query = jnp.einsum(
        "qah,he->qae", score_gradient, key_slice, preferred_element_type=jnp.float32
    )
    grad_key = jnp.einsum(
        "hlo,hle->oe", score_gradient, query_slice, preferred_element_type=jnp.float32
    )
    grad_value = jnp.einsum(
        "hlo,hle->oe",
        attention_output.astype(jnp.bfloat16),
        gradient_slice,
        preferred_element_type=jnp.float32,
    )
    return (grad_query, grad_key, grad_value)


def fetch_block(key_rows, value_rows, key_places):
    return (
        lax.all_gather(key_rows, "fsdp", axis=0, tiled=True),
        lax.all_gather(value_rows, "fsdp", axis=0, tiled=True),
        lax.all_gather(key_places, "fsdp", axis=0, tiled=True),
    )


def fetch_earlier(key_rows, value_rows, key_places, offset):
    return passed_along((key_rows, value_rows, key_places), "seq", offset)


def return_rows(grad_keys, grad_values):
    return (
        lax.psum_scatter(
            grad_keys.astype(jnp.bfloat16), "fsdp", scatter_dimension=0, tiled=True
        ).astype(jnp.float32),
        lax.psum_scatter(
            grad_values.astype(jnp.bfloat16), "fsdp", scatter_dimension=0, tiled=True
        ).astype(jnp.float32),
    )


def return_earlier(grad_keys, grad_values, offset):
    return (
        passed_along(grad_keys.astype(jnp.bfloat16), "seq", -offset).astype(grad_keys.dtype),
        passed_along(grad_values.astype(jnp.bfloat16), "seq", -offset).astype(grad_values.dtype),
    )


def contract_rows(left, right):
    return lax.dot_general(
        left, right, (((0,), (0,)), ((), ())), preferred_element_type=jnp.float32
    )


def contract_cols(left, right):
    return lax.dot_general(
        left, right, (((1,), (1,)), ((), ())), preferred_element_type=jnp.float32
    )


def per_device(
    layer_input,
    positions,
    gain_attn_in,
    w_query,
    w_key,
    w_value,
    w_out,
    gain_attn_out,
    gain_ffn_in,
    w_gate,
    w_up,
    w_down,
    gain_ffn_out,
    cotangent,
):
    rows = layer_input.shape[0]
    half_rows = cotangent.shape[0]
    seq_count = lax.axis_size("seq")
    fsdp_count = lax.axis_size("fsdp")
    block = rows * fsdp_count
    seq_place = lax.axis_index("seq")
    fsdp_place = lax.axis_index("fsdp")
    tensor_place = lax.axis_index("tensor")
    query_w, key_w, value_w, out_w, gain_one, gain_two, gain_three, gain_four = (
        lax.all_gather(w_query, ("seq", "fsdp"), axis=0, tiled=True),
        lax.all_gather(w_key, ("seq", "fsdp"), axis=0, tiled=True),
        lax.all_gather(w_value, ("seq", "fsdp"), axis=0, tiled=True),
        lax.all_gather(w_out, ("seq", "fsdp"), axis=1, tiled=True),
        lax.all_gather(gain_attn_in, ("seq", "fsdp"), axis=0, tiled=True),
        lax.all_gather(gain_attn_out, ("seq", "fsdp"), axis=0, tiled=True),
        lax.all_gather(gain_ffn_in, ("seq", "fsdp"), axis=0, tiled=True),
        lax.all_gather(gain_ffn_out, ("seq", "fsdp"), axis=0, tiled=True),
    )
    gain_one = gain_one.astype(jnp.float32)
    gain_two = gain_two.astype(jnp.float32)
    gain_three = gain_three.astype(jnp.float32)
    gain_four = gain_four.astype(jnp.float32)
    local_heads = query_w.shape[1] // HEAD
    local_kv = key_w.shape[1] // HEAD
    group_size = local_heads // local_kv
    scale = HEAD ** (-0.5)
    inputs = layer_input.astype(jnp.float32)
    normed = (normalize(inputs) * gain_one).astype(jnp.bfloat16)
    query_raw = jnp.dot(normed, query_w, preferred_element_type=jnp.float32)
    key_raw = jnp.dot(normed, key_w, preferred_element_type=jnp.float32)
    value_rows = jnp.dot(normed, value_w, preferred_element_type=jnp.float32).astype(jnp.bfloat16)
    cosine_table, sine_table = rotary_tables(positions)
    queries = (
        rotate(query_raw.reshape(rows, local_heads, HEAD), cosine_table, sine_table) * scale
    ).astype(jnp.bfloat16)
    key_rows = rotate(key_raw.reshape(rows, local_kv, HEAD), cosine_table, sine_table).astype(
        jnp.bfloat16
    )
    key_rows = key_rows.reshape(rows, local_kv * HEAD)
    reach = min(seq_count - 1, (WINDOW - 2 + block) // block)
    own_block = fetch_block(key_rows, value_rows, positions)
    earlier = []
    for offset in range(reach, 0, -1):
        earlier.append(fetch_earlier(own_block[0], own_block[1], own_block[2], offset))
    pieces = earlier + [own_block]
    key_all = jnp.concatenate([piece[0] for piece in pieces], axis=0)
    value_all = jnp.concatenate([piece[1] for piece in pieces], axis=0)
    key_places = jnp.concatenate([piece[2] for piece in pieces], axis=0)
    key_index = jnp.concatenate(
        [
            (seq_place - offset) * block + jnp.arange(block, dtype=jnp.int32)
            for offset in range(reach, -1, -1)
        ]
    )
    key_count = key_all.shape[0]
    query_index = seq_place * block + fsdp_place * rows + jnp.arange(rows, dtype=jnp.int32)
    place_apart = positions[:, None] - key_places[None, :]
    index_apart = query_index[:, None] - key_index[None, :]
    visible = (place_apart == index_apart) & (place_apart >= 0) & (place_apart < WINDOW)
    key_heads = key_all.reshape(key_count, local_kv, HEAD).transpose(1, 0, 2)
    value_heads = value_all.reshape(key_count, local_kv, HEAD).transpose(1, 0, 2)
    query_heads = queries.reshape(rows, local_kv, group_size, HEAD).transpose(1, 2, 0, 3)

    def forward_head(operands):
        return attend(operands[0], operands[1], operands[2], visible)

    head_out, log_total = lax.map(forward_head, (query_heads, key_heads, value_heads))
    attended = head_out.transpose(2, 0, 1, 3).reshape(rows, local_heads * HEAD).astype(jnp.bfloat16)
    branch_part = jnp.dot(attended, out_w, preferred_element_type=jnp.float32)
    branch = lax.psum_scatter(branch_part, "tensor", scatter_dimension=0, tiled=True)
    input_half = lax.dynamic_slice_in_dim(inputs, tensor_place * half_rows, half_rows, 0)
    middle = input_half + normalize(branch) * gain_two
    ffn_in = (normalize(middle) * gain_three).astype(jnp.bfloat16)
    ffn_rows = lax.all_gather(ffn_in, ("fsdp", "tensor"), axis=0, tiled=True)
    gate = jnp.dot(ffn_rows, w_gate, preferred_element_type=jnp.float32)
    up_proj = jnp.dot(ffn_rows, w_up, preferred_element_type=jnp.float32)
    hidden = gated_gelu(gate, up_proj).astype(jnp.bfloat16)
    ffn_out = lax.psum_scatter(
        jnp.dot(hidden, w_down, preferred_element_type=jnp.float32),
        ("fsdp", "tensor"),
        scatter_dimension=0,
        tiled=True,
    )
    output = middle + normalize(ffn_out) * gain_four
    incoming = cotangent.astype(jnp.float32)
    grad_ffn_out, grad_gain_four = normalize_back(ffn_out, gain_four, incoming)
    ffn_cot = lax.all_gather(
        grad_ffn_out.astype(jnp.bfloat16), ("fsdp", "tensor"), axis=0, tiled=True
    )
    grad_hidden = contract_cols(ffn_cot, w_down)
    grad_down = contract_rows(hidden, ffn_cot)
    _, gelu_pullback = jax.vjp(gated_gelu, gate, up_proj)
    grad_gate, grad_up = gelu_pullback(grad_hidden)
    grad_gate = grad_gate.astype(jnp.bfloat16)
    grad_up = grad_up.astype(jnp.bfloat16)
    grad_gate_w = contract_rows(ffn_rows, grad_gate)
    grad_up_w = contract_rows(ffn_rows, grad_up)
    grad_ffn_in = lax.psum_scatter(
        contract_cols(grad_gate, w_gate) + contract_cols(grad_up, w_up),
        ("fsdp", "tensor"),
        scatter_dimension=0,
        tiled=True,
    )
    grad_mid_norm, grad_gain_three = normalize_back(middle, gain_three, grad_ffn_in)
    grad_middle = incoming + grad_mid_norm
    grad_branch, grad_gain_two = normalize_back(branch, gain_two, grad_middle)
    branch_cot = lax.all_gather(grad_branch.astype(jnp.bfloat16), "tensor", axis=0, tiled=True)
    grad_attended = contract_cols(branch_cot, out_w).astype(jnp.bfloat16)
    grad_out_w = contract_rows(attended, branch_cot)
    grad_heads = grad_attended.reshape(rows, local_kv, group_size, HEAD).transpose(1, 2, 0, 3)

    def backward_head(operands):
        return attend_back(operands[0], operands[1], operands[2], operands[3], operands[4], visible)

    grad_query_heads, grad_key_heads, grad_value_heads = lax.map(
        backward_head, (query_heads, key_heads, value_heads, grad_heads, log_total)
    )
    grad_key_all = grad_key_heads.transpose(1, 0, 2).reshape(key_count, local_kv * HEAD)
    grad_value_all = grad_value_heads.transpose(1, 0, 2).reshape(key_count, local_kv * HEAD)
    own_keys = grad_key_all[reach * block :]
    own_values = grad_value_all[reach * block :]
    for offset in range(1, reach + 1):
        first_row = (reach - offset) * block
        back = return_earlier(
            grad_key_all[first_row : first_row + block],
            grad_value_all[first_row : first_row + block],
            offset,
        )
        own_keys = own_keys + back[0]
        own_values = own_values + back[1]
    grad_keys, grad_values = return_rows(own_keys, own_values)
    grad_key_raw = rotate_back(grad_keys.reshape(rows, local_kv, HEAD), cosine_table, sine_table)
    grad_key_raw = grad_key_raw.reshape(rows, local_kv * HEAD).astype(jnp.bfloat16)
    grad_value_low = grad_values.astype(jnp.bfloat16)
    grad_queries = grad_query_heads.transpose(2, 0, 1, 3).reshape(rows, local_heads, HEAD)
    grad_query_raw = rotate_back(grad_queries * scale, cosine_table, sine_table)
    grad_query_raw = grad_query_raw.reshape(rows, local_heads * HEAD).astype(jnp.bfloat16)
    grad_query_w = contract_rows(normed, grad_query_raw)
    grad_key_w = contract_rows(normed, grad_key_raw)
    grad_value_w = contract_rows(normed, grad_value_low)
    grad_normed = (
        contract_cols(grad_query_raw, query_w)
        + contract_cols(grad_key_raw, key_w)
        + contract_cols(grad_value_low, value_w)
    )
    grad_normed, grad_gain_two, grad_gain_three, grad_gain_four = (
        lax.psum(grad_normed.astype(jnp.bfloat16), "tensor").astype(jnp.float32),
        lax.psum(grad_gain_two.astype(jnp.bfloat16), "tensor").astype(jnp.float32),
        lax.psum(grad_gain_three.astype(jnp.bfloat16), "tensor").astype(jnp.float32),
        lax.psum(grad_gain_four.astype(jnp.bfloat16), "tensor").astype(jnp.float32),
    )
    grad_input_norm, grad_gain_one = normalize_back(inputs, gain_one, grad_normed)
    grad_input = grad_middle + lax.dynamic_slice_in_dim(
        grad_input_norm, tensor_place * half_rows, half_rows, 0
    )
    summed_grads = (
        lax.psum_scatter(grad_query_w, ("seq", "fsdp"), scatter_dimension=0, tiled=True),
        lax.psum_scatter(grad_key_w, ("seq", "fsdp"), scatter_dimension=0, tiled=True),
        lax.psum_scatter(grad_value_w, ("seq", "fsdp"), scatter_dimension=0, tiled=True),
        lax.psum_scatter(grad_out_w, ("seq", "fsdp"), scatter_dimension=1, tiled=True),
        lax.psum_scatter(grad_gain_one, ("seq", "fsdp"), scatter_dimension=0, tiled=True),
        lax.psum_scatter(grad_gain_two, ("seq", "fsdp"), scatter_dimension=0, tiled=True),
        lax.psum_scatter(grad_gain_three, ("seq", "fsdp"), scatter_dimension=0, tiled=True),
        lax.psum_scatter(grad_gain_four, ("seq", "fsdp"), scatter_dimension=0, tiled=True),
    )
    ffn_summed = (
        lax.psum(grad_gate_w.astype(jnp.bfloat16), "seq").astype(jnp.float32),
        lax.psum(grad_up_w.astype(jnp.bfloat16), "seq").astype(jnp.float32),
        lax.psum(grad_down.astype(jnp.bfloat16), "seq").astype(jnp.float32),
    )
    return (
        output.astype(jnp.bfloat16),
        grad_input,
        summed_grads[4],
        summed_grads[0],
        summed_grads[1],
        summed_grads[2],
        summed_grads[3],
        summed_grads[5],
        summed_grads[6],
        ffn_summed[0],
        ffn_summed[1],
        ffn_summed[2],
        summed_grads[7],
    )


def solution(mesh):
    placed = (
        P(("seq", "fsdp"), None),
        P(("seq", "fsdp")),
        P(("seq", "fsdp")),
        P(("seq", "fsdp"), "tensor"),
        P(("seq", "fsdp"), "tensor"),
        P(("seq", "fsdp"), "tensor"),
        P("tensor", ("seq", "fsdp")),
        P(("seq", "fsdp")),
        P(("seq", "fsdp")),
        P(None, ("fsdp", "tensor")),
        P(None, ("fsdp", "tensor")),
        P(("fsdp", "tensor"), None),
        P(("seq", "fsdp")),
        P(("seq", "fsdp", "tensor"), None),
    )
    return jax.shard_map(
        per_device,
        mesh=mesh,
        in_specs=placed,
        out_specs=(
            P(("seq", "fsdp", "tensor"), None),
            P(("seq", "fsdp", "tensor"), None),
            P(("seq", "fsdp")),
            P(("seq", "fsdp"), "tensor"),
            P(("seq", "fsdp"), "tensor"),
            P(("seq", "fsdp"), "tensor"),
            P("tensor", ("seq", "fsdp")),
            P(("seq", "fsdp")),
            P(("seq", "fsdp")),
            P(None, ("fsdp", "tensor")),
            P(None, ("fsdp", "tensor")),
            P(("fsdp", "tensor"), None),
            P(("seq", "fsdp")),
        ),
        check_vma=False,
    )
```

profile of v0, /device:TPU:0, one launch (start us, length us, event | category | flops | bytes accessed | tf_op | source)
XLA Modules:
  0.0 1881.7 jit_solution(3673737329369897031)
XLA Ops:
  14.1 64.0 %all-reduce.9 = (bf16[2304]{0:T(1024)(128)(2,1)S(1)}, bf16[2304]{0:T(1024)(128)(2,1)S(1)}, bf16[2304]{0:T(1024)(128)(2,1)S(1)}, bf16[2304]{0:T(1024)(128)(2,1)}) all-reduce(bf16[2304]{0:T(1024)(128)(2,1)S(1)} %dynamic-update-slice, bf16[2304]{0:T(1024)(128)(2,1)S(1)} %dynamic-update-slice.1, ...), channel_id=1, replica_groups=mesh['seq'=4,'fsdp'=4,'tensor'=2] {'seq','fsdp'}, use_global_device_ids=true, to_apply=%add | all-reduce | flops 9216 | bytes 36864
  86.0 12.8 all-gather.17.cloned.1.call-done
  102.7 27.3 %all-gather.15.cloned.1.call-done = bf16[1024,512]{0,1:T(8,128)(2,1)} async-done(((bf16[256,512]{0,1:T(8,128)(2,1)}), bf16[1024,512]{0,1:T(8,128)(2,1)}) %all-gather.15.cloned.1.call-update) | async-done | bytes 1048592 | tf_op jit(solution)/shard_map/all_gather | solution.py:121
  150.6 30.8 %collective-permute-done.1 = s32[1024]{0:T(1024)S(1)} collective-permute-done((s32[1024]{0:T(1024)S(1)}, s32[1024]{0:T(1024)S(1)}, u32[]{:S(2)}, u32[]{:S(2)}) %collective-permute-start.1) | collective-permute-done | bytes 4128 | tf_op jit(solution)/shard_map/ppermute | solution.py:18
  201.5 22.7 %collective-permute-done.7 = bf16[1024,512]{1,0:T(8,128)(2,1)} collective-permute-done((bf16[1024,512]{1,0:T(8,128)(2,1)}, bf16[1024,512]{1,0:T(8,128)(2,1)}, u32[]{:S(2)}, u32[]{:S(2)}) %collective-permute-start.7) | collective-permute-done | bytes 1048608 | tf_op jit(solution)/shard_map/ppermute | solution.py:18
  224.2 23.1 %collective-permute-done.6 = bf16[1024,512]{1,0:T(8,128)(2,1)} collective-permute-done((bf16[1024,512]{1,0:T(8,128)(2,1)}, bf16[1024,512]{1,0:T(8,128)(2,1)}, u32[]{:S(2)}, u32[]{:S(2)}) %collective-permute-start.6) | collective-permute-done | bytes 1048608 | tf_op jit(solution)/shard_map/ppermute | solution.py:18
  258.6 19.7 %while.28 = (s32[]{:T(128)}, bf16[2,2,256,256]{2,3,1,0:T(8,128)(2,1)S(1)}, f32[2,2,256]{2,1,0:T(2,128)S(1)}, bf16[2,2,256,256]{3,2,1,0:T(8,128)(2,1)S(1)}, bf16[...) while((s32[]{:T(128)}, ...), condition=%wide.region_4.5_spmd.clone, body=%wide.region_1.4_spmd.clone.sunk | while | flops 2173697536 | bytes 49074324 | solution.py:243
  291.4 31.8 %reduce-scatter.10.cloned.1.call-done = f32[128,2304]{1,0:T(8,128)} async-done(((f32[256,2304]{1,0:T(8,128)}), f32[128,2304]{1,0:T(8,128)}) %reduce-scatter.10.cloned.1.call-update) | async-done | bytes 1179664 | tf_op jit(solution)/shard_map/reduce_scatter | solution.py:246
  328.2 79.5 %all-gather.23.cloned.1.call-done = bf16[1024,2304]{1,0:T(8,128)(2,1)} async-done(((bf16[128,2304]{1,0:T(8,128)(2,1)}), bf16[1024,2304]{1,0:T(8,128)(2,1)}) %all-gather.23.cloned.1.call-update) | async-done | bytes 4718608 | tf_op jit(solution)/shard_map/all_gather | solution.py:250
  417.5 12.6 multiply_convert_fusion.2
  440.9 161.1 %reduce-scatter.12.cloned.1.call-done = f32[128,2304]{1,0:T(8,128)} async-done(((f32[1024,2304]{1,0:T(8,128)}), f32[128,2304]{1,0:T(8,128)}) %reduce-scatter.12.cloned.1.call-update) | async-done | bytes 1179664 | tf_op jit(solution)/shard_map/reduce_scatter | solution.py:254
  608.6 78.9 %all-gather.25.cloned.1.call-done = bf16[1024,2304]{1,0:T(8,128)(2,1)} async-done(((bf16[128,2304]{1,0:T(8,128)(2,1)}), bf16[1024,2304]{1,0:T(8,128)(2,1)}) %all-gather.25.cloned.1.call-update) | async-done | bytes 4718608 | tf_op jit(solution)/shard_map/all_gather | solution.py:263
  687.5 15.0 multiply_convert_fusion.1
  702.5 10.5 fusion.152
  713.1 11.3 convolution_add_fusion
  724.5 161.5 %reduce-scatter.14.cloned.1.call-done = f32[128,2304]{1,0:T(8,128)} async-done(((f32[1024,2304]{1,0:T(8,128)}), f32[128,2304]{1,0:T(8,128)}) %reduce-scatter.14.cloned.1.call-update) | async-done | bytes 1179664 | tf_op jit(solution)/shard_map/reduce_scatter | solution.py:274
  893.0 22.0 %all-gather.27.cloned.1.call-done = bf16[256,2304]{1,0:T(8,128)(2,1)} async-done(((bf16[128,2304]{1,0:T(8,128)(2,1)}), bf16[256,2304]{1,0:T(8,128)(2,1)}) %all-gather.27.cloned.1.call-update) | async-done | bytes 1179664 | tf_op jit(solution)/shard_map/all_gather | solution.py:283
  919.5 108.7 %while.29 = (s32[]{:T(128)}, f32[2,2,256,256]{3,2,1,0:T(8,128)}, f32[2,4096,256]{1,2,0:T(8,128)}, f32[2,4096,256]{1,2,0:T(8,128)}, bf16[2,2,256,256]{3,2,1,0:T(8...) while((s32[]{:T(128)}, f32[2,2,256,256]{3,2,1,0:T(8,128)}, ...), condition=%wide.region_16.17_spmd.clone, body=%wide.region_14.16_spmd.clone.sunk | while | flops 5449458688 | bytes 131650728 | solution.py:291
  932.5 15.8 fusion.230
  948.2 16.8 fusion.231
  986.4 16.0 fusion.230
  1002.4 16.8 fusion.231
  1044.6 17.4 collective-permute-done.11
  1080.9 26.0 %collective-permute-done.14 = bf16[1024,512]{0,1:T(8,128)(2,1)S(1)} collective-permute-done((bf16[1024,512]{0,1:T(8,128)(2,1)}, bf16[1024,512]{0,1:T(8,128)(2,1)S(1)}, u32[]{:S(2)}, u32[]{:S(2)}) %collective-permute-start.14) | collective-permute-done | bytes 1048608 | tf_op jit(solution)/shard_map/ppermute | solution.py:18
  1114.0 10.6 convolution_convert_fusion
  1148.9 11.6 reduce-scatter.18.cloned.1.call-done
  1186.3 251.8 %all-reduce.17.cloned.1.call-done = (bf16[2304,1152]{1,0:T(8,128)(2,1)}, bf16[2304,1152]{1,0:T(8,128)(2,1)}, bf16[1152,2304]{1,0:T(8,128)(2,1)}) async-done(((bf16[2304,1152]{1,0:T(8,128)(2,1)}, bf16[2304,1152]{1,0:T(8,128)(2,1)}, bf16[1152,2304]{1,0:T(8,128)(2,1)}), (bf16[2304,1152]{1,0:T(8,128)(2,1)}, bf16[2304,1152]{1,0:T(8,128)(2,1)}, bf16[1152,2304]{1,0:T(8,128)(2,1)})) %all-reduce.17.cloned.1.call-update) | async-done | bytes 15925264 | tf_op jit(solution)/shard_map/psum | solution.py:343
  1464.6 18.9 %all-reduce.15.cloned.1.call-done = bf16[256,2304]{1,0:T(8,128)(2,1)} async-done(((bf16[256,2304]{1,0:T(8,128)(2,1)}), bf16[256,2304]{1,0:T(8,128)(2,1)}) %all-reduce.15.cloned.1.call-update) | async-done | bytes 1179664 | tf_op jit(solution)/shard_map/psum | solution.py:323
  1487.9 62.9 %all-reduce.8 = (f32[2304]{0:T(1024)S(1)}, f32[2304]{0:T(1024)S(1)}, f32[2304]{0:T(1024)S(1)}, f32[2304]{0:T(1024)S(1)}) all-reduce(f32[2304]{0:T(1024)S(1)} %get-tuple-element.214, bf16[2304]{0:T(1024)(128)(2,1)S(1)} %get-tuple-element.279, ...), channel_id=7, replica_groups=mesh['seq'=4,'fsdp'=4,'tensor'=2] {'seq','fsdp'}, use_global_device_ids=true, to_apply=%region_22.23.clone | all-reduce | flops 9216 | bytes 59904
  1564.4 78.9 %reduce-scatter.24.cloned.1.call-done = f32[144,512]{1,0:T(8,128)} async-done(((f32[2304,512]{1,0:T(8,128)}), f32[144,512]{1,0:T(8,128)}) %reduce-scatter.24.cloned.1.call-update) | async-done | bytes 294928 | tf_op jit(solution)/shard_map/reduce_scatter | solution.py:335
  1643.3 115.7 %reduce-scatter.20.cloned.1.call-done = f32[144,1024]{1,0:T(8,128)} async-done(((f32[2304,1024]{1,0:T(8,128)}), f32[144,1024]{1,0:T(8,128)}) %reduce-scatter.20.cloned.1.call-update) | async-done | bytes 589840 | tf_op jit(solution)/shard_map/reduce_scatter | solution.py:333
  1759.0 115.6 %reduce-scatter.26.cloned.1.call-done = f32[1024,144]{0,1:T(8,128)} async-done(((f32[1024,2304]{0,1:T(8,128)}), f32[1024,144]{0,1:T(8,128)}) %reduce-scatter.26.cloned.1.call-update) | async-done | bytes 589840 | tf_op jit(solution)/shard_map/reduce_scatter | solution.py:336
  (292 shorter events, 324.7 us)
Async XLA Ops:
  7.2 73.8 %all-gather.13.cloned.1.call-start = ((), (), s32[]{:S(2)}) async-start(), calls=%async_computation.10 | async-start | bytes 2506752 | tf_op jit(solution)/shard_map/all_gather | solution.py:187
  7.9 91.0 %all-gather.17.cloned.1.call-start = ((), (), s32[]{:S(2)}) async-start(), calls=%async_computation.12 | async-start | bytes 2506752 | tf_op jit(solution)/shard_map/all_gather | solution.py:188
  8.7 121.4 %all-gather.15.cloned.1.call-start = ((), (), s32[]{:S(2)}) async-start(), calls=%async_computation.11 | async-start | bytes 1310720 | tf_op jit(solution)/shard_map/all_gather | solution.py:121
  86.0 95.4 %all-gather.19.cloned.1.call-start = ((), (), s32[]{:S(2)}) async-start(), calls=%async_computation.13 | async-start | bytes 1310720 | tf_op jit(solution)/shard_map/all_gather | solution.py:122
  102.1 149.5 %all-gather.11.cloned.1.call-start = ((), (), s32[]{:S(2)}) async-start(), calls=%async_computation.9 | async-start | bytes 5013504 | tf_op jit(solution)/shard_map/all_gather | solution.py:186
  102.7 181.9 %all-gather.21.cloned.1.call-start = ((), (), s32[]{:S(2)}) async-start(), calls=%async_computation.14 | async-start | bytes 5013504 | tf_op jit(solution)/shard_map/all_gather | solution.py:189
  130.0 58.6 %collective-permute-start.5 = (bf16[1024,512]{0,1:T(8,128)(2,1)}, bf16[1024,512]{0,1:T(8,128)(2,1)S(1)}, u32[]{:S(2)}, u32[]{:S(2)}) collective-permute-start(bf16[1024,512]{0,1:T(8,128)(2,1)} %all-gather.15.cloned.1.call-done), channel_id=1, source_target_pairs={{0,8},{8,16},{16,24},{1,9},{9,17},{17,25},{2,10},{10,18},{18,26},{... | collective-permute-start | bytes 3145736 | tf_op jit(solution)/shard_map/ppermute | solution.py:18
  131.4 59.9 %collective-permute-start.4 = (bf16[1024,512]{0,1:T(8,128)(2,1)}, bf16[1024,512]{0,1:T(8,128)(2,1)}, u32[]{:S(2)}, u32[]{:S(2)}) collective-permute-start(bf16[1024,512]{0,1:T(8,128)(2,1)} %all-gather.15.cloned.1.call-done), channel_id=1, source_target_pairs={{0,16},{8,24},{1,17},{9,25},{2,18},{10,26},{3,19},{11,27},{4,20},{... | collective-permute-start | bytes 3145736 | tf_op jit(solution)/shard_map/ppermute | solution.py:18
  135.4 55.9 %collective-permute-start.3 = (bf16[1024,512]{0,1:T(8,128)(2,1)}, bf16[1024,512]{0,1:T(8,128)(2,1)}, u32[]{:S(2)}, u32[]{:S(2)}) collective-permute-start(bf16[1024,512]{0,1:T(8,128)(2,1)} %all-gather.15.cloned.1.call-done), channel_id=1, source_target_pairs={{0,24},{1,25},{2,26},{3,27},{4,28},{5,29},{6,30},{7,31}} | collective-permute-start | bytes 3145736 | tf_op jit(solution)/shard_map/ppermute | solution.py:18
  147.9 33.4 %collective-permute-start.1 = (s32[1024]{0:T(1024)S(1)}, s32[1024]{0:T(1024)S(1)}, u32[]{:S(2)}, u32[]{:S(2)}) collective-permute-start(s32[1024]{0:T(1024)S(1)} %bitcast.225), channel_id=1, source_target_pairs={{0,16},{8,24},{1,17},{9,25},{2,18},{10,26},{3,19},{11,27},{4,20},{... | collective-permute-start | bytes 12296 | tf_op jit(solution)/shard_map/ppermute | solution.py:18
  149.3 34.5 %collective-permute-start = (s32[1024]{0:T(1024)S(1)}, s32[1024]{0:T(1024)S(1)}, u32[]{:S(2)}, u32[]{:S(2)}) collective-permute-start(s32[1024]{0:T(1024)S(1)} %bitcast.226), channel_id=1, source_target_pairs={{0,24},{1,25},{2,26},{3,27},{4,28},{5,29},{6,30},{7,31}} | collective-permute-start | bytes 12296 | tf_op jit(solution)/shard_map/ppermute | solution.py:18
  150.6 172.6 %reduce-scatter.10.cloned.1.call-start = ((), (), s32[]{:S(2)}) async-start(), calls=%async_computation.15 | async-start | bytes 3538944 | tf_op jit(solution)/shard_map/reduce_scatter | solution.py:246
  183.8 40.4 %collective-permute-start.7 = (bf16[1024,512]{1,0:T(8,128)(2,1)}, bf16[1024,512]{1,0:T(8,128)(2,1)}, u32[]{:S(2)}, u32[]{:S(2)}) collective-permute-start(bf16[1024,512]{1,0:T(8,128)(2,1)} %all-gather.19.cloned.1.call-done), channel_id=1, source_target_pairs={{0,16},{8,24},{1,17},{9,25},{2,18},{10,26},{3,19},{11,27},{4,20},{... | collective-permute-start | bytes 3145736 | tf_op jit(solution)/shard_map/ppermute | solution.py:18
  188.6 58.6 %collective-permute-start.6 = (bf16[1024,512]{1,0:T(8,128)(2,1)}, bf16[1024,512]{1,0:T(8,128)(2,1)}, u32[]{:S(2)}, u32[]{:S(2)}) collective-permute-start(bf16[1024,512]{1,0:T(8,128)(2,1)} %all-gather.19.cloned.1.call-done), channel_id=1, source_target_pairs={{0,24},{1,25},{2,26},{3,27},{4,28},{5,29},{6,30},{7,31}} | collective-permute-start | bytes 3145736 | tf_op jit(solution)/shard_map/ppermute | solution.py:18
  289.8 117.9 %all-gather.23.cloned.1.call-start = ((), (), s32[]{:S(2)}) async-start(), calls=%async_computation.16 | async-start | bytes 5308416 | tf_op jit(solution)/shard_map/all_gather | solution.py:250
  327.6 274.3 %reduce-scatter.12.cloned.1.call-start = ((), (), s32[]{:S(2)}) async-start(), calls=%async_computation.17 | async-start | bytes 10616832 | tf_op jit(solution)/shard_map/reduce_scatter | solution.py:254
  440.2 247.3 %all-gather.25.cloned.1.call-start = ((), (), s32[]{:S(2)}) async-start(), calls=%async_computation.18 | async-start | bytes 5308416 | tf_op jit(solution)/shard_map/all_gather | solution.py:263
  608.4 277.6 %reduce-scatter.14.cloned.1.call-start = ((), (), s32[]{:S(2)}) async-start(), calls=%async_computation.19 | async-start | bytes 10616832 | tf_op jit(solution)/shard_map/reduce_scatter | solution.py:274
  724.4 190.6 %all-gather.27.cloned.1.call-start = ((), (), s32[]{:S(2)}) async-start(), calls=%async_computation.20 | async-start | bytes 1769472 | tf_op jit(solution)/shard_map/all_gather | solution.py:283
  893.0 250.1 %reduce-scatter.16.cloned.1.call-start = ((), (), s32[]{:S(2)}) async-start(), calls=%async_computation.21 | async-start | bytes 1310720 | tf_op jit(solution)/shard_map/reduce_scatter | solution.py:133
  1037.4 28.0 %collective-permute-start.10 = (bf16[1024,512]{0,1:T(8,128)(2,1)S(1)}, bf16[1024,512]{0,1:T(8,128)(2,1)S(1)}, u32[]{:S(2)}, u32[]{:S(2)}) collective-permute-start(bf16[1024,512]{0,1:T(8,128)(2,1)S(1)} %bitcast.220), channel_id=1, source_target_pairs={{16,0},{24,8},{17,1},{25,9},{18,2},{26,10},{19,3},{27,11},{20,4},{... | collective-permute-start | bytes 3145736 | tf_op jit(solution)/shard_map/ppermute | solution.py:18
  1038.7 26.7 %collective-permute-start.9 = (bf16[1024,512]{0,1:T(8,128)(2,1)S(1)}, bf16[1024,512]{0,1:T(8,128)(2,1)}, u32[]{:S(2)}, u32[]{:S(2)}) collective-permute-start(bf16[1024,512]{0,1:T(8,128)(2,1)S(1)} %bitcast.219), channel_id=1, source_target_pairs={{8,0},{16,8},{24,16},{9,1},{17,9},{25,17},{10,2},{18,10},{26,18},{... | collective-permute-start | bytes 3145736 | tf_op jit(solution)/shard_map/ppermute | solution.py:18
  1042.0 64.9 %collective-permute-start.14 = (bf16[1024,512]{0,1:T(8,128)(2,1)}, bf16[1024,512]{0,1:T(8,128)(2,1)S(1)}, u32[]{:S(2)}, u32[]{:S(2)}) collective-permute-start(bf16[1024,512]{0,1:T(8,128)(2,1)} %bitcast.28), channel_id=1, source_target_pairs={{24,0},{25,1},{26,2},{27,3},{28,4},{29,5},{30,6},{31,7}} | collective-permute-start | bytes 3145736 | tf_op jit(solution)/shard_map/ppermute | solution.py:18
  1043.3 67.2 %collective-permute-start.13 = (bf16[1024,512]{0,1:T(8,128)(2,1)S(1)}, bf16[1024,512]{0,1:T(8,128)(2,1)}, u32[]{:S(2)}, u32[]{:S(2)}) collective-permute-start(bf16[1024,512]{0,1:T(8,128)(2,1)S(1)} %bitcast.218), channel_id=1, source_target_pairs={{16,0},{24,8},{17,1},{25,9},{18,2},{26,10},{19,3},{27,11},{20,4},{... | collective-permute-start | bytes 3145736 | tf_op jit(solution)/shard_map/ppermute | solution.py:18
  1062.0 48.5 %collective-permute-start.12 = (bf16[1024,512]{0,1:T(8,128)(2,1)S(1)}, bf16[1024,512]{0,1:T(8,128)(2,1)}, u32[]{:S(2)}, u32[]{:S(2)}) collective-permute-start(bf16[1024,512]{0,1:T(8,128)(2,1)S(1)} %bitcast.217), channel_id=1, source_target_pairs={{8,0},{16,8},{24,16},{9,1},{17,9},{25,17},{10,2},{18,10},{26,18},{... | collective-permute-start | bytes 3145736 | tf_op jit(solution)/shard_map/ppermute | solution.py:18
  1068.6 91.9 %reduce-scatter.18.cloned.1.call-start = ((), (), s32[]{:S(2)}) async-start(), calls=%async_computation.22 | async-start | bytes 1310720 | tf_op jit(solution)/shard_map/reduce_scatter | solution.py:136
  1113.9 324.1 %all-reduce.17.cloned.1.call-start = ((), (), s32[]{:S(2)}) async-start(), calls=%async_computation.28 | async-start | bytes 31850496 | tf_op jit(solution)/shard_map/psum | solution.py:343
  1134.4 349.2 %all-reduce.15.cloned.1.call-start = ((), (), s32[]{:S(2)}) async-start(), calls=%async_computation.23 | async-start | bytes 2359296 | tf_op jit(solution)/shard_map/psum | solution.py:323
  1164.2 400.2 %reduce-scatter.22.cloned.1.call-start = ((), (), s32[]{:S(2)}) async-start(), calls=%async_computation.25 | async-start | bytes 5013504 | tf_op jit(solution)/shard_map/reduce_scatter | solution.py:334
  1168.7 474.6 %reduce-scatter.24.cloned.1.call-start = ((), (), s32[]{:S(2)}) async-start(), calls=%async_computation.26 | async-start | bytes 5013504 | tf_op jit(solution)/shard_map/reduce_scatter | solution.py:335
  1172.8 586.1 %reduce-scatter.20.cloned.1.call-start = ((), (), s32[]{:S(2)}) async-start(), calls=%async_computation.24 | async-start | bytes 10027008 | tf_op jit(solution)/shard_map/reduce_scatter | solution.py:333
  1179.1 695.6 %reduce-scatter.26.cloned.1.call-start = ((), (), s32[]{:S(2)}) async-start(), calls=%async_computation.27 | async-start | bytes 10027008 | tf_op jit(solution)/shard_map/reduce_scatter | solution.py:336
  (48 other events, 1541.1 us)
Sparse Core Ops, SparseCore 0:
  10.3 44.9 all-gather.12
  57.6 41.1 all-gather.16
  101.0 28.9 all-gather.14
  132.0 26.2 all-gather.18
  160.5 55.4 all-gather.10
  218.2 66.3 all-gather.20
  289.9 33.2 reduce-scatter.9
  327.8 79.8 all-gather.22
  440.3 161.5 reduce-scatter.11
  608.5 78.9 all-gather.24
  724.5 161.4 reduce-scatter.13
  893.1 21.8 all-gather.26
  1068.7 48.4 reduce-scatter.15
  1119.4 41.1 reduce-scatter.17
  1164.1 273.9 all-reduce.16
  1440.2 43.3 all-reduce.14
  1488.3 76.0 reduce-scatter.21
  1568.7 74.5 reduce-scatter.23
  1648.5 110.3 reduce-scatter.19
  1763.5 111.0 reduce-scatter.25
where the time goes:
time: 1890 us; the launch traced here: 1880 us
  waiting for transfers between devices  1310 us (69%)
  matrix products  266 us (14%)
  blocking collectives  144 us (8%)
  other arithmetic  74.4 us (4%)
  local copies, waits for them, and re-layouts  39.2 us (2%)
  starting transfers between devices  30.7 us (2%)
    psum x1, waiting for transfers between devices, per_device(): lax.psum(grad_gate_w.astype(jnp.bfloat16), 'seq').astype(jnp.float32)  252 us
    reduce_scatter x1, waiting for transfers between devices, per_device(): lax.psum_scatter(contract_cols(grad_gate, w_gate) + contract_cols(grad_up...  162 us
    reduce_scatter x1, waiting for transfers between devices, per_device(): lax.psum_scatter(jnp.dot(hidden, w_down, preferred_element_type=jnp.float...  161 us
    unnamed x2, blocking collectives  127 us
    ppermute x15, waiting for transfers between devices, passed_along(): return lax.ppermute(x, axis, pairs)  126 us
    reduce_scatter x1, waiting for transfers between devices, per_device(): lax.psum_scatter(grad_query_w, ('seq', 'fsdp'), scatter_dimension=0, tile...  116 us
    reduce_scatter x1, waiting for transfers between devices, per_device(): lax.psum_scatter(grad_out_w, ('seq', 'fsdp'), scatter_dimension=1, tiled=...  116 us
    all_gather x1, waiting for transfers between devices, per_device(): ffn_rows = lax.all_gather(ffn_in, ('fsdp', 'tensor'), axis=0, tiled=True)  79.5 us
  transfers between devices with their start and end apart: 35, of which 23 were waited for; matrix products, arithmetic and copies ran while one was open for 8% of the time, Pallas kernels for 0%

commit v1 on v0

v1 whole, which is shorter than its diff:
```python
import functools

import jax
import jax.numpy as jnp
from jax import lax
from jax.experimental import pallas as pl
from jax.experimental.pallas import tpu as pltpu
from jax.sharding import PartitionSpec as P

HEAD = 256
WINDOW = 4096

epsilon = 1e-06
soft_cap = 50.0
rotary_base = 10000.0
low = jnp.bfloat16
wide = jnp.float32


def dot(left, right, left_dim=1, right_dim=0):
    return lax.dot_general(
        left, right, (((left_dim,), (right_dim,)), ((), ())), preferred_element_type=wide
    )


def unit_of(values):
    scale = lax.rsqrt(jnp.mean(values * values, axis=-1, keepdims=True) + epsilon)
    return values * scale, scale


def normalize_back(values, weighted):
    unit, scale = unit_of(values)
    grad = scale * (weighted - unit * jnp.mean(weighted * unit, axis=-1, keepdims=True))
    return grad, unit


def rotary_tables(positions):
    freqs = rotary_base ** (-2.0 * jnp.arange(HEAD // 2, dtype=wide) / HEAD)
    angles = positions.astype(wide)[:, None] * freqs[None, :]
    return jnp.cos(angles), jnp.sin(angles)


def rotate(values, cosine, sine):
    half = values.shape[-1] // 2
    front, back = values[..., :half], values[..., half:]
    return jnp.concatenate([front * cosine - back * sine, back * cosine + front * sine], axis=-1)


def gated_gelu(gate, up):
    return jax.nn.gelu(gate, approximate=True) * up


def flip(x, axis, mask):
    return lax.ppermute(x, axis, [(i, i ^ mask) for i in range(lax.axis_size(axis))])


def other_core(x):
    return flip(x, "seq", 1)


def other_x(x):
    return flip(x, "seq", 2)


def other_y(x):
    return flip(x, "tensor", 1)


PAIR = [(0, 1), (1, 0), (2, 3), (3, 2)]
MIDDLE = [(1, 2), (2, 1)]
OUTWARD = [(1, 0), (2, 3)]
INWARD = [(0, 1), (3, 2)]


def slot_places():
    count, place = lax.axis_size("fsdp"), lax.axis_index("fsdp")
    if count != 4:
        return [jnp.int32(i) for i in range(count)]
    first = place < 2
    return [place, place ^ 1, jnp.where(first, 2, 1), jnp.where(first, 3, 0)]


def own_slot():
    return 0 if lax.axis_size("fsdp") == 4 else None


def gather_slots(piece):
    count = lax.axis_size("fsdp")
    if count != 4:
        whole = lax.all_gather(piece, "fsdp", axis=0, tiled=False)
        return [whole[i] for i in range(count)]
    pair = lax.ppermute(piece, "fsdp", PAIR)
    near = lax.ppermute(piece, "fsdp", MIDDLE)
    near = near + lax.ppermute(near, "fsdp", OUTWARD)
    far = lax.ppermute(pair, "fsdp", MIDDLE)
    far = far + lax.ppermute(far, "fsdp", OUTWARD)
    return [piece, pair, near, far]


def scatter_slots(pieces):
    count = lax.axis_size("fsdp")
    if count != 4:
        return lax.psum_scatter(
            jnp.stack([p.astype(low) for p in pieces]), "fsdp", scatter_dimension=0, tiled=False
        ).astype(wide)
    own, pair, near, far = pieces

    def add(a, b):
        return a.astype(wide) + b.astype(wide)

    far = add(far, lax.ppermute(far.astype(low), "fsdp", INWARD)).astype(low)
    pair = add(pair, lax.ppermute(far, "fsdp", MIDDLE))
    near = add(near, lax.ppermute(near.astype(low), "fsdp", INWARD)).astype(low)
    own = add(own, lax.ppermute(near, "fsdp", MIDDLE))
    return add(own, lax.ppermute(pair.astype(low), "fsdp", PAIR))


def ordered(pieces, place):
    return [lax.select_n(place ^ i, *pieces) for i in range(len(pieces))]


def swap_seq(blocks, place):
    got = [lax.dynamic_index_in_dim(blocks, place, 0, False)]
    for mask in range(1, blocks.shape[0]):
        got.append(flip(lax.dynamic_index_in_dim(blocks, place ^ mask, 0, False), "seq", mask))
    return ordered(got, place)


def sum_everywhere(x):
    x = x + other_core(x)
    x = x + other_x(x)
    x = x + other_y(x)
    step = 1
    while step < lax.axis_size("fsdp"):
        x = x + flip(x, "fsdp", step)
        step *= 2
    return x


def dot_nt(left, right):
    return dot(left, right, 1, 1)


def visible_of(query_doc, key_doc, query_at, key_at, same, windowed):
    seen = query_doc == key_doc
    if same:
        seen = seen & (query_at >= key_at)
    if windowed:
        seen = seen & (query_at - key_at < WINDOW)
    return seen


def tiles(blocks, block_keys, chunk, windowed):
    reach = min(blocks - 1, (WINDOW - 2 + block_keys) // block_keys)
    return [
        [
            (key_block * block_keys + start, key_block == block)
            for key_block in range(max(0, block - reach), block + 1)
            for start in range(0, block_keys, chunk)
        ]
        for block in range(blocks)
    ]


def attend_kernel(
    plan, chunk, windowed, core, query, query_doc, query_at, keyed, key_doc, key_at, out, lse
):
    rows = query.shape[0] // len(plan)
    kind = core[0]
    for block, parts in enumerate(plan):
        here = pl.ds(block * rows, rows)
        q = query[here, :]
        total = jnp.zeros((rows, 1), wide)
        summed = jnp.zeros((rows, HEAD), wide)
        for first, same in parts:
            there = pl.ds(first, chunk)
            scores = dot_nt(q, keyed[kind, there, :])
            weights = jnp.exp(soft_cap * jnp.tanh(scores * (1.0 / soft_cap)))
            seen = visible_of(
                query_doc[here, :], key_doc[:, there], query_at[here, :], key_at[:, there], same, windowed
            )
            weights = jnp.where(seen, weights, 0.0)
            total = total + jnp.sum(weights, axis=1, keepdims=True)
            summed = summed + dot(weights.astype(low), keyed[1 - kind, there, :])
        out[here, :] = summed / total
        lse[here, :] = jnp.log(total)


def attend_back_kernel(
    plan,
    chunk,
    windowed,
    core,
    query,
    query_doc,
    query_at,
    keyed,
    key_doc,
    key_at,
    incoming,
    lse,
    delta,
    grad_query,
    grad_keyed,
    key_total,
    value_total,
):
    rows = query.shape[0] // len(plan)
    kind = core[0]
    seen_by = {}
    for block, parts in enumerate(plan):
        for first, same in parts:
            seen_by.setdefault(first, []).append((block, same))
    grad_query[...] = jnp.zeros_like(grad_query)
    for first in sorted(seen_by):
        there = pl.ds(first, chunk)
        k = keyed[kind, there, :]
        v = keyed[1 - kind, there, :]
        for turn, (block, same) in enumerate(seen_by[first]):
            here = pl.ds(block * rows, rows)
            q = query[here, :]
            d = incoming[here, :]
            bent = jnp.tanh(dot_nt(k, q) * (1.0 / soft_cap))
            weights = jnp.exp(soft_cap * bent - lse[:, here])
            seen = visible_of(
                query_doc[:, here], key_doc[there, :], query_at[:, here], key_at[there, :], same, windowed
            )
            weights = jnp.where(seen, weights, 0.0)
            grads = weights * (dot_nt(v, d) - delta[:, here]) * (1.0 - bent * bent)
            grads = grads.astype(low)
            value_part = dot(weights.astype(low), d)
            key_part = dot(grads, q)
            if turn == 0:
                value_total[...] = value_part
                key_total[...] = key_part
            else:
                value_total[...] += value_part
                key_total[...] += key_part
            grad_query[here, :] += dot(grads, k, 0, 0)
        grad_keyed[kind, there, :] = key_total[...].astype(low)
        grad_keyed[1 - kind, there, :] = value_total[...].astype(low)


def in_vmem(count):
    return [pl.BlockSpec(memory_space=pltpu.SMEM)] + [pl.BlockSpec(memory_space=pltpu.VMEM)] * count


def attend(core, query, docs, ats, keyed, key_docs, key_ats, blocks):
    tokens, keys = query.shape[0], keyed.shape[1]
    chunk = min(1024, keys // blocks)
    windowed = keys > WINDOW
    plan = tiles(blocks, keys // blocks, chunk, windowed)
    count = sum(len(parts) for parts in plan) * (tokens // blocks) * chunk
    return pl.pallas_call(
        functools.partial(attend_kernel, plan, chunk, windowed),
        out_shape=(
            jax.ShapeDtypeStruct((tokens, HEAD), wide),
            jax.ShapeDtypeStruct((tokens, 1), wide),
        ),
        in_specs=in_vmem(6),
        out_specs=(pl.BlockSpec(memory_space=pltpu.VMEM),) * 2,
        compiler_params=pltpu.CompilerParams(vmem_limit_bytes=48 * 1024 * 1024),
        cost_estimate=pl.CostEstimate(
            flops=4 * count * HEAD, bytes_accessed=6 * keys * HEAD, transcendentals=2 * count
        ),
        name="attend",
    )(core, query, docs[:, None], ats[:, None], keyed, key_docs[None, :], key_ats[None, :])


def attend_back(core, query, docs, ats, keyed, key_docs, key_ats, incoming, lse, delta, blocks):
    tokens, keys = query.shape[0], keyed.shape[1]
    chunk = min(1024, keys // blocks)
    windowed = keys > WINDOW
    plan = tiles(blocks, keys // blocks, chunk, windowed)
    count = sum(len(parts) for parts in plan) * (tokens // blocks) * chunk
    return pl.pallas_call(
        functools.partial(attend_back_kernel, plan, chunk, windowed),
        out_shape=(
            jax.ShapeDtypeStruct((tokens, HEAD), wide),
            jax.ShapeDtypeStruct(keyed.shape, low),
        ),
        in_specs=in_vmem(9),
        out_specs=(pl.BlockSpec(memory_space=pltpu.VMEM),) * 2,
        scratch_shapes=[pltpu.VMEM((chunk, HEAD), wide), pltpu.VMEM((chunk, HEAD), wide)],
        compiler_params=pltpu.CompilerParams(vmem_limit_bytes=56 * 1024 * 1024),
        cost_estimate=pl.CostEstimate(
            flops=10 * count * HEAD, bytes_accessed=12 * keys * HEAD, transcendentals=2 * count
        ),
        name="attend_back",
    )(
        core,
        query,
        docs[None, :],
        ats[None, :],
        keyed,
        key_docs[:, None],
        key_ats[:, None],
        incoming,
        lse,
        delta,
    )


def per_device(
    layer_input,
    positions,
    gain_attn_in,
    w_query,
    w_key,
    w_value,
    w_out,
    gain_attn_out,
    gain_ffn_in,
    w_gate,
    w_up,
    w_down,
    gain_ffn_out,
    cotangent,
):
    rows, width = layer_input.shape
    half_rows = cotangent.shape[0]
    blocks = lax.axis_size("seq")
    line = lax.axis_size("fsdp")
    seq_place = lax.axis_index("seq")
    fsdp_place = lax.axis_index("fsdp")
    tensor_place = lax.axis_index("tensor")
    core = seq_place % 2
    side = seq_place // 2
    share = gain_attn_in.shape[0]
    heads = w_query.shape[1] // HEAD
    places = slot_places()
    scale = HEAD ** (-0.5)
    assert blocks == heads == 4 and w_key.shape[1] == 2 * HEAD

    extra = 16
    gain_row = jnp.pad(gain_attn_in[None, :], ((0, extra - 1), (0, HEAD - share)))
    query_blocks = w_query.reshape(share, blocks, HEAD).transpose(1, 0, 2)
    keyed_blocks = jnp.stack(
        [
            jnp.concatenate(
                [(w_key, w_value)[i % 2][:, (i // 2) * HEAD : (i // 2 + 1) * HEAD], gain_row],
                axis=0,
            )
            for i in range(blocks)
        ]
    )

    def assemble(pieces):
        whole = jnp.zeros((blocks, line) + pieces[0].shape[1:], pieces[0].dtype)
        for piece, at in zip(pieces, places):
            whole = lax.dynamic_update_slice(whole, piece[:, None], (0, at, 0, 0))
        return whole.reshape(blocks * line * pieces[0].shape[1], pieces[0].shape[2])

    keyed_slots = gather_slots(jnp.stack(swap_seq(keyed_blocks, seq_place)))
    keyed_w = assemble([piece[:, :share] for piece in keyed_slots])
    gain_one = assemble([piece[:, share : share + 1, :share] for piece in keyed_slots])
    gain_one = gain_one.reshape(width).astype(wide)
    query_w = assemble(gather_slots(jnp.stack(swap_seq(query_blocks, seq_place))))

    from_x = other_x(layer_input)
    from_core = other_core(layer_input)
    from_far = other_core(from_x)
    units = [
        (unit_of(piece.astype(wide))[0] * gain_one).astype(low)
        for piece in (layer_input, from_core, from_x, from_far)
    ]
    normed = jnp.zeros((blocks, rows, width), low)
    for mask, piece in enumerate(units):
        normed = lax.dynamic_update_index_in_dim(normed, piece, seq_place ^ mask, 0)
    normed = normed.reshape(blocks * rows, width)

    place_slots = jnp.stack(gather_slots(positions))
    place_all = jnp.stack(
        ordered([place_slots] + [flip(place_slots, "seq", m) for m in range(1, blocks)], seq_place)
    )
    token_rows = jnp.arange(rows, dtype=jnp.int32)
    block_starts = jnp.arange(blocks, dtype=jnp.int32)[:, None, None] * (line * rows)
    key_at = block_starts + (jnp.stack(places) * rows)[None, :, None] + token_rows
    key_doc = (key_at - place_all).reshape(-1)
    key_at = key_at.reshape(-1)
    own = own_slot()
    own_positions = (
        place_all[:, own]
        if own is not None
        else lax.dynamic_index_in_dim(place_all, fsdp_place, 1, False)
    ).reshape(-1)
    query_at = (block_starts[:, 0] + fsdp_place * rows + token_rows).reshape(-1)
    query_doc = query_at - own_positions
    cosine, sine = rotary_tables(own_positions)
    plain = core == 1

    keyed_raw = dot(normed, keyed_w)
    keyed = jnp.where(plain, keyed_raw, rotate(keyed_raw, cosine, sine)).astype(low)
    keyed_slots = gather_slots(keyed.reshape(blocks, rows, HEAD))
    other_slots = [other_core(piece) for piece in keyed_slots]
    keyed_all = jnp.stack(
        [jnp.stack(keyed_slots, axis=1), jnp.stack(other_slots, axis=1)]
    ).reshape(2, blocks * line * rows, HEAD)
    query_raw = dot(normed, query_w)
    queries = (rotate(query_raw, cosine, sine) * scale).astype(low)
    core_array = core.reshape(1).astype(jnp.int32)

    attend_out, log_total = attend(
        core_array, queries, query_doc, query_at, keyed_all, key_doc, key_at, blocks
    )

    gains = jnp.stack([gain_attn_out, gain_ffn_in, gain_ffn_out])
    gains = jnp.pad(gains, ((0, extra - 3), (0, heads * HEAD - share)))
    out_slots = gather_slots(jnp.concatenate([w_out.T, gains], axis=0))
    out_line = jnp.zeros((line, share + extra, heads * HEAD), low)
    for piece, at in zip(out_slots, places):
        out_line = lax.dynamic_update_index_in_dim(out_line, piece, at, 0)
    out_x = other_x(out_line)
    out_core = other_core(out_line)
    out_far = other_core(out_x)
    out_w = jnp.zeros((blocks, line, share, heads * HEAD), low)
    gain_all = jnp.zeros((blocks, line, 3, share), low)
    for mask, piece in enumerate((out_line, out_core, out_x, out_far)):
        out_w = lax.dynamic_update_index_in_dim(out_w, piece[:, :share], seq_place ^ mask, 0)
        gain_all = lax.dynamic_update_index_in_dim(
            gain_all, piece[:, share : share + 3, :share], seq_place ^ mask, 0
        )
    out_w = out_w.reshape(width, heads * HEAD)
    gain_all = gain_all.transpose(2, 0, 1, 3).reshape(3, width).astype(wide)
    gain_two, gain_three, gain_four = gain_all[0], gain_all[1], gain_all[2]

    attended = jnp.concatenate(
        swap_seq(attend_out.astype(low).reshape(blocks, rows, HEAD), seq_place), axis=1
    )
    away = lax.dynamic_slice_in_dim(attended, (1 - tensor_place) * half_rows, half_rows, 0)
    kept = lax.dynamic_slice_in_dim(attended, tensor_place * half_rows, half_rows, 0)
    branch_away = other_y(dot(away, out_w, 1, 1).astype(low))
    branch = dot(kept, out_w, 1, 1) + branch_away.astype(wide)

    inputs_half = lax.dynamic_slice_in_dim(
        layer_input, tensor_place * half_rows, half_rows, 0
    ).astype(wide)
    middle = inputs_half + unit_of(branch)[0] * gain_two
    ffn_in = (unit_of(middle)[0] * gain_three).astype(low)

    def gather_rows(piece):
        return [jnp.concatenate([p, other_y(p)], axis=0) for p in gather_slots(piece)]

    def scatter_rows(parts):
        sums = [None] * len(parts)
        for i in reversed(range(len(parts))):
            got = other_y(parts[i][half_rows:].astype(low))
            sums[i] = parts[i][:half_rows].astype(wide) + got.astype(wide)
        return scatter_slots(sums)

    ffn_rows = gather_rows(ffn_in)
    gates = [dot(part, w_gate) for part in ffn_rows]
    ups = [dot(part, w_up) for part in ffn_rows]
    hiddens = [gated_gelu(g, u).astype(low) for g, u in zip(gates, ups)]
    ffn_out = scatter_rows([dot(h, w_down) for h in hiddens])
    unit_out, scale_out = unit_of(ffn_out)
    output = middle + unit_out * gain_four

    incoming = cotangent.astype(wide)
    grad_ffn_out, _ = normalize_back(ffn_out, incoming * gain_four)
    gain_four_part = jnp.sum(incoming * unit_out, axis=0)
    ffn_cots = gather_rows(grad_ffn_out.astype(low))
    grad_gates, grad_ups = [], []
    for part, g, u in zip(ffn_cots, gates, ups):
        _, pullback = jax.vjp(gated_gelu, g, u)
        grad_gate, grad_up = pullback(dot(part, w_down, 1, 1))
        grad_gates.append(grad_gate.astype(low))
        grad_ups.append(grad_up.astype(low))
    grad_ffn_in = scatter_rows(
        [dot(g, w_gate, 1, 1) + dot(u, w_up, 1, 1) for g, u in zip(grad_gates, grad_ups)]
    )

    half = width // 2
    rows_all = jnp.concatenate(ffn_rows, axis=0)
    cots_all = jnp.concatenate(ffn_cots, axis=0)
    hidden_all = jnp.concatenate(hiddens, axis=0)
    grad_gate_all = jnp.concatenate(grad_gates, axis=0)
    grad_up_all = jnp.concatenate(grad_ups, axis=0)

    def summed_over_seq(part_of, axis):
        sent = other_core(part_of((1 - core) * half).astype(low))
        mine = (part_of(core * half) + sent.astype(wide)).astype(low)
        mine = (mine.astype(wide) + other_x(mine).astype(wide)).astype(low)
        theirs = other_core(mine)
        first = jnp.where(core == 0, mine, theirs)
        second = jnp.where(core == 0, theirs, mine)
        return jnp.concatenate([first, second], axis=axis).astype(wide)

    def half_of(x, start):
        return lax.dynamic_slice_in_dim(x, start, half, 1)

    grad_down_w = summed_over_seq(lambda at: dot(hidden_all, half_of(cots_all, at), 0, 0), 1)
    grad_gate_w = summed_over_seq(lambda at: dot(half_of(rows_all, at), grad_gate_all, 0, 0), 0)
    grad_up_w = summed_over_seq(lambda at: dot(half_of(rows_all, at), grad_up_all, 0, 0), 0)

    grad_mid_norm, unit_middle = normalize_back(middle, grad_ffn_in * gain_three)
    gain_three_part = jnp.sum(grad_ffn_in * unit_middle, axis=0)
    grad_middle = incoming + grad_mid_norm
    grad_branch, unit_branch = normalize_back(branch, grad_middle * gain_two)
    gain_two_part = jnp.sum(grad_middle * unit_branch, axis=0)
    grad_branch = grad_branch.astype(low)
    branch_other = other_y(grad_branch)
    first = tensor_place == 0
    branch_cot = jnp.concatenate(
        [jnp.where(first, grad_branch, branch_other), jnp.where(first, branch_other, grad_branch)],
        axis=0,
    )
    grad_attended = dot(branch_cot, out_w).astype(low)
    grad_attended = jnp.concatenate(
        swap_seq(grad_attended.reshape(rows, blocks, HEAD).transpose(1, 0, 2), seq_place), axis=0
    )
    delta = jnp.sum(attend_out * grad_attended.astype(wide), axis=1)
    grad_queries, grad_keyed = attend_back(
        core_array,
        queries,
        query_doc,
        query_at,
        keyed_all,
        key_doc,
        key_at,
        grad_attended,
        log_total.reshape(1, -1),
        delta[None, :],
        blocks,
    )

    grad_keyed = grad_keyed.reshape(2, blocks, line, rows, HEAD)
    keyed_got = other_core(grad_keyed[1])
    keyed_sum = grad_keyed[0].astype(wide) + keyed_got.astype(wide)
    keyed_own = scatter_slots([keyed_sum[:, i] for i in range(line)]).reshape(blocks * rows, HEAD)
    grad_keyed_raw = jnp.where(plain, keyed_own, rotate(keyed_own, cosine, -sine)).astype(low)
    grad_query_raw = rotate(grad_queries * scale, cosine, -sine).astype(low)

    def to_rows(grad):
        grad = grad.astype(low).reshape(blocks, line, share, HEAD)
        parts = [lax.dynamic_index_in_dim(grad, at, 1, False) for at in places]
        return [p.astype(wide) for p in swap_seq(scatter_slots(parts).astype(low), seq_place)]

    query_grads = jnp.concatenate(to_rows(dot(normed, grad_query_raw, 0, 0)), axis=1)
    keyed_grads = to_rows(dot(normed, grad_keyed_raw, 0, 0))
    key_grads = jnp.concatenate(keyed_grads[0::2], axis=1)
    value_grads = jnp.concatenate(keyed_grads[1::2], axis=1)
    gain_one_part = (
        jnp.sum(query_grads * w_query.astype(wide), axis=1)
        + jnp.sum(key_grads * w_key.astype(wide), axis=1)
        + jnp.sum(value_grads * w_value.astype(wide), axis=1)
    )
    grad_gain_one = (gain_one_part + other_y(gain_one_part)) / gain_attn_in.astype(wide)

    out_grad = dot(branch_cot, attended, 0, 0).astype(low)
    out_grad = out_grad.reshape(2, 2, line, share, heads * HEAD)
    out_got = other_core(lax.dynamic_index_in_dim(out_grad, 1 - core, 1, False))
    out_sum = (
        lax.dynamic_index_in_dim(out_grad, core, 1, False).astype(wide) + out_got.astype(wide)
    ).astype(low)
    out_got = other_x(lax.dynamic_index_in_dim(out_sum, 1 - side, 0, False))
    out_sum = (
        lax.dynamic_index_in_dim(out_sum, side, 0, False).astype(wide) + out_got.astype(wide)
    ).astype(low)
    grad_out_w = scatter_slots(
        [lax.dynamic_index_in_dim(out_sum, at, 0, False) for at in places]
    ).T

    back = (dot(grad_query_raw, query_w, 1, 1) + dot(grad_keyed_raw, keyed_w, 1, 1)).astype(low)
    back = back.reshape(2, 2, rows, width)
    back_got = other_core(lax.dynamic_index_in_dim(back, 1 - core, 1, False))
    back = (
        lax.dynamic_index_in_dim(back, core, 1, False).astype(wide) + back_got.astype(wide)
    ).astype(low)
    back_got = other_x(lax.dynamic_index_in_dim(back, 1 - side, 0, False))
    back = (
        lax.dynamic_index_in_dim(back, side, 0, False).astype(wide) + back_got.astype(wide)
    ).astype(low)
    back_got = other_y(lax.dynamic_slice_in_dim(back, (1 - tensor_place) * half_rows, half_rows, 0))
    back = lax.dynamic_slice_in_dim(back, tensor_place * half_rows, half_rows, 0).astype(
        wide
    ) + back_got.astype(wide)
    grad_input = grad_middle + normalize_back(inputs_half, back * gain_one)[0]

    gain_sums = sum_everywhere(jnp.stack([gain_two_part, gain_three_part, gain_four_part]))
    gain_sums = lax.dynamic_slice_in_dim(gain_sums, (seq_place * line + fsdp_place) * share, share, 1)

    return (
        output.astype(low),
        grad_input,
        grad_gain_one,
        query_grads,
        key_grads,
        value_grads,
        grad_out_w,
        gain_sums[0],
        gain_sums[1],
        grad_gate_w,
        grad_up_w,
        grad_down_w,
        gain_sums[2],
    )


def solution(mesh):
    by_rows = P(("seq", "fsdp"))
    placed = (
        P(("seq", "fsdp"), None),
        by_rows,
        by_rows,
        P(("seq", "fsdp"), "tensor"),
        P(("seq", "fsdp"), "tensor"),
        P(("seq", "fsdp"), "tensor"),
        P("tensor", ("seq", "fsdp")),
        by_rows,
        by_rows,
        P(None, ("fsdp", "tensor")),
        P(None, ("fsdp", "tensor")),
        P(("fsdp", "tensor"), None),
        by_rows,
        P(("seq", "fsdp", "tensor"), None),
    )
    return jax.shard_map(
        per_device,
        mesh=mesh,
        in_specs=placed,
        out_specs=(
            P(("seq", "fsdp", "tensor"), None),
            P(("seq", "fsdp", "tensor"), None),
            by_rows,
            P(("seq", "fsdp"), "tensor"),
            P(("seq", "fsdp"), "tensor"),
            P(("seq", "fsdp"), "tensor"),
            P("tensor", ("seq", "fsdp")),
            by_rows,
            by_rows,
            P(None, ("fsdp", "tensor")),
            P(None, ("fsdp", "tensor")),
            P(("fsdp", "tensor"), None),
            by_rows,
        ),
        check_vma=False,
    )
```

time: 1890 us -> 905 us (0.48)
  waiting for transfers between devices: 1310 us -> 419 us
  starting transfers between devices: 30.7 us -> 182 us
  blocking collectives: 144 us -> 0 us
  matrix products: 266 us -> 133 us
  Pallas kernels: 0 us -> 22.8 us
    reduce_scatter x9 -> x0, waiting for transfers between devices: 684 us -> none  [the longest x1 162 us: per_device(): lax.psum_scatter(contract_cols(grad_gate, w_gate) + contract_cols(grad_up...]
    ppermute x15 -> x135, waiting for transfers between devices: 126 us -> 419 us  [the longest x70 262 us: flip(): lax.ppermute(x, axis, [(i, i ^ mask) for i in range(lax.axis_size(axis))])]
    psum x2 -> x0, waiting for transfers between devices: 271 us -> none  [the longest x1 252 us: per_device(): lax.psum(grad_gate_w.astype(jnp.bfloat16), 'seq').astype(jnp.float32)]
    all_gather x9 -> x0, waiting for transfers between devices: 227 us -> none  [the longest x1 79.5 us: per_device(): ffn_rows = lax.all_gather(ffn_in, ('fsdp', 'tensor'), axis=0, tiled=True)]
    ppermute x15 -> x135, starting transfers between devices: 29 us -> 182 us  [the longest x70 58.1 us: flip(): lax.ppermute(x, axis, [(i, i ^ mask) for i in range(lax.axis_size(axis))])]
    dot_general x35 -> x40, matrix products: 266 us -> 133 us  [dot(): lax.dot_general(left, right, (((left_dim,), (right_dim,)), ((), ())), pre...]
    unnamed x2 -> x0, blocking collectives: 127 us -> none
    pallas_call x0 -> x2, Pallas kernels: none -> 22.8 us  [the longest x1 16.1 us: attend_back(): pl.pallas_call(functools.partial(attend_back_kernel, plan, chunk, windowe...]
  transfers between devices with their start and end apart: 35 -> 135, of which waited for: 23 -> 55; matrix products, arithmetic and copies ran while one was open for 8% -> 27% of each run, Pallas kernels for 0% -> 3%
where the time goes in v1:
time: 905 us; the launch traced here: 894 us
  waiting for transfers between devices  419 us (46%)
  starting transfers between devices  182 us (20%)
  matrix products  133 us (15%)
  other arithmetic  92.1 us (10%)
  local copies, waits for them, and re-layouts  40.4 us (4%)
  Pallas kernels  22.8 us (3%)
    ppermute x70, waiting for transfers between devices, flip(): lax.ppermute(x, axis, [(i, i ^ mask) for i in range(lax.axis_size(axis))])  262 us
    dot_general x40, matrix products, dot(): lax.dot_general(left, right, (((left_dim,), (right_dim,)), ((), ())), pre...  133 us
    ppermute x70, starting transfers between devices, flip(): lax.ppermute(x, axis, [(i, i ^ mask) for i in range(lax.axis_size(axis))])  58.1 us
    ppermute x7, waiting for transfers between devices, gather_slots(): far = far + lax.ppermute(far, 'fsdp', OUTWARD)  38.2 us
    ppermute x6, waiting for transfers between devices, scatter_slots(): far = add(far, lax.ppermute(far.astype(low), 'fsdp', INWARD)).astype(low)  32.2 us
    ppermute x7, waiting for transfers between devices, gather_slots(): near = near + lax.ppermute(near, 'fsdp', OUTWARD)  27.2 us
    ppermute x6, waiting for transfers between devices, scatter_slots(): near = add(near, lax.ppermute(near.astype(low), 'fsdp', INWARD)).astype(low)  27 us
    ppermute x6, starting transfers between devices, scatter_slots(): return add(own, lax.ppermute(pair.astype(low), 'fsdp', PAIR))  26.8 us
  transfers between devices with their start and end apart: 135, of which 55 were waited for; matrix products, arithmetic and copies ran while one was open for 27% of the time, Pallas kernels for 3%

profile of v1, /device:TPU:0, one launch (start us, length us, event | category | flops | bytes accessed | tf_op | source)
XLA Modules:
  0.0 893.7 jit_solution(3264208844765520254)
XLA Ops:
  63.9 8.1 collective-permute-done.41
  87.2 6.7 collective-permute-done.43
  96.6 10.3 %collective-permute-done.7 = bf16[4,160,256]{2,1,0:T(8,128)(2,1)} collective-permute-done((bf16[4,160,256]{2,1,0:T(8,128)(2,1)}, bf16[4,160,256]{2,1,0:T(8,128)(2,1)}, u32[]{:S(2)}, u32[]{:S(2)}) %collective-permute-start.7) | collective-permute-done | bytes 327712 | tf_op jit(solution)/shard_map/ppermute | solution.py:96
  127.6 11.8 %collective-permute-done.27 = bf16[4,256,256]{2,1,0:T(8,128)(2,1)} collective-permute-done((bf16[4,256,256]{2,1,0:T(8,128)(2,1)}, bf16[4,256,256]{2,1,0:T(8,128)(2,1)}, u32[]{:S(2)}, u32[]{:S(2)}) %collective-permute-start.27) | collective-permute-done | bytes 524320 | tf_op jit(solution)/shard_map/ppermute | solution.py:92
  149.8 9.2 %collective-permute-done.29 = bf16[4,256,256]{2,1,0:T(8,128)(2,1)S(1)} collective-permute-done((bf16[4,256,256]{2,1,0:T(8,128)(2,1)S(1)}, bf16[4,256,256]{2,1,0:T(8,128)(2,1)S(1)}, u32[]{:S(2)}, u32[]{:S(2)}) %collective-permute-start.29) | collective-permute-done | bytes 524320 | tf_op jit(solution)/shard_map/ppermute | solution.py:94
  159.3 11.0 %collective-permute-done.31 = bf16[4,256,256]{2,1,0:T(8,128)(2,1)S(1)} collective-permute-done((bf16[4,256,256]{2,1,0:T(8,128)(2,1)S(1)}, bf16[4,256,256]{2,1,0:T(8,128)(2,1)S(1)}, u32[]{:S(2)}, u32[]{:S(2)}) %collective-permute-start.31) | collective-permute-done | bytes 524320 | tf_op jit(solution)/shard_map/ppermute | solution.py:96
  177.4 6.8 attend.1
  198.9 11.4 %collective-permute-done.47 = bf16[128,2304]{1,0:T(8,128)(2,1)S(1)} collective-permute-done((bf16[128,2304]{1,0:T(8,128)(2,1)S(1)}, bf16[128,2304]{1,0:T(8,128)(2,1)S(1)}, u32[]{:S(2)}, u32[]{:S(2)}) %collective-permute-start.47) | collective-permute-done | bytes 589856 | tf_op jit(solution)/shard_map/ppermute | solution.py:54
  217.6 11.6 %collective-permute-done.48 = bf16[128,2304]{1,0:T(8,128)(2,1)S(1)} collective-permute-done((bf16[128,2304]{1,0:T(8,128)(2,1)S(1)}, bf16[128,2304]{1,0:T(8,128)(2,1)S(1)}, u32[]{:S(2)}, u32[]{:S(2)}) %collective-permute-start.48) | collective-permute-done | bytes 589856 | tf_op jit(solution)/shard_map/ppermute | solution.py:54
  243.5 21.8 %collective-permute-done.57 = bf16[128,2304]{1,0:T(8,128)(2,1)S(1)} collective-permute-done((bf16[128,2304]{1,0:T(8,128)(2,1)S(1)}, bf16[128,2304]{1,0:T(8,128)(2,1)S(1)}, u32[]{:S(2)}, u32[]{:S(2)}) %collective-permute-start.57) | collective-permute-done | bytes 589856 | tf_op jit(solution)/shard_map/ppermute | solution.py:54
  268.9 10.0 %collective-permute-start.60 = (bf16[128,2304]{1,0:T(8,128)(2,1)S(1)}, bf16[128,2304]{1,0:T(8,128)(2,1)S(1)}, u32[]{:S(2)}, u32[]{:S(2)}) collective-permute-start(bf16[128,2304]{1,0:T(8,128)(2,1)S(1)} %collective-permute-done.59), channel_id=1, source_target_pairs={{2,0},{4,6},{3,1},{5,7},{10,8},{12,14},{11,9},{13,15},{18,16},{20,... | collective-permute-start | bytes 1769480 | tf_op jit(solution)/shard_map/ppermute | solution.py:96
  288.0 10.7 %collective-permute-done.61 = bf16[128,2304]{1,0:T(8,128)(2,1)S(1)} collective-permute-done((bf16[128,2304]{1,0:T(8,128)(2,1)S(1)}, bf16[128,2304]{1,0:T(8,128)(2,1)S(1)}, u32[]{:S(2)}, u32[]{:S(2)}) %collective-permute-start.61) | collective-permute-done | bytes 589856 | tf_op jit(solution)/shard_map/ppermute | solution.py:54
  311.7 12.2 %collective-permute-done.62 = bf16[128,2304]{1,0:T(8,128)(2,1)S(1)} collective-permute-done((bf16[128,2304]{1,0:T(8,128)(2,1)S(1)}, bf16[128,2304]{1,0:T(8,128)(2,1)S(1)}, u32[]{:S(2)}, u32[]{:S(2)}) %collective-permute-start.62) | collective-permute-done | bytes 589856 | tf_op jit(solution)/shard_map/ppermute | solution.py:54
  340.9 7.3 collective-permute-done.54
  357.8 8.1 collective-permute-done.65
  401.3 19.8 %collective-permute-done.75 = bf16[128,2304]{1,0:T(8,128)(2,1)S(1)} collective-permute-done((bf16[128,2304]{1,0:T(8,128)(2,1)S(1)}, bf16[128,2304]{1,0:T(8,128)(2,1)S(1)}, u32[]{:S(2)}, u32[]{:S(2)}) %collective-permute-start.75) | collective-permute-done | bytes 589856 | tf_op jit(solution)/shard_map/ppermute | solution.py:54
  436.7 8.4 collective-permute-done.78
  477.2 7.8 collective-permute-done.80
  500.9 7.5 collective-permute-done.72
  509.8 8.2 collective-permute-start.83
  519.0 6.5 convolution_convert_fusion.1
  563.0 7.4 fusion.2
  572.7 16.1 %attend_back.1 = (f32[1024,256]{1,0:T(8,128)}, bf16[2,4096,256]{2,1,0:T(8,128)(2,1)}) custom-call(s32[1]{0:T(128)} %bitcast.core, bf16[1024,256]{1,0:T(8,128)(2,1)} %copy-done, s32[1,1024]{1,0:T(1,128)} %sub.104.query_doc, s32[1,1024]{1,0:T(1,128)} %bitcast.504, bf16[2,4096,256]{2,1,0:T(8,128)(2,1)} %pad_maximum_fusion.keyed, s32[4096,1]{1,0:T(8,128)} %copy.115.key_doc, ...), custom_call_target="tpu_custom_call" | custom-call | flops 6710886400 | bytes 12582912 | tf_op jit(solution)/shard_map/attend_back/pallas_call | solution.py:276
  641.9 7.6 collective-permute-done.89
  649.5 10.8 %collective-permute-done.91 = bf16[4,256,256]{2,1,0:T(8,128)(2,1)S(1)} collective-permute-done((bf16[4,256,256]{2,1,0:T(8,128)(2,1)S(1)}, bf16[4,256,256]{2,1,0:T(8,128)(2,1)S(1)}, u32[]{:S(2)}, u32[]{:S(2)}) %collective-permute-start.91) | collective-permute-done | bytes 524320 | tf_op jit(solution)/shard_map/ppermute | solution.py:111
  661.4 28.6 %collective-permute-done.127 = bf16[1152,1152]{1,0:T(8,128)(2,1)} collective-permute-done((bf16[1152,1152]{1,0:T(8,128)(2,1)S(1)}, bf16[1152,1152]{1,0:T(8,128)(2,1)}, u32[]{:S(2)}, u32[]{:S(2)}) %collective-permute-start.127) | collective-permute-done | bytes 2654240 | tf_op jit(solution)/shard_map/ppermute | solution.py:54
  698.6 48.2 %collective-permute-done.130 = bf16[1152,1152]{1,0:T(8,128)(2,1)S(1)} collective-permute-done((bf16[1152,1152]{1,0:T(8,128)(2,1)S(1)}, bf16[1152,1152]{1,0:T(8,128)(2,1)S(1)}, u32[]{:S(2)}, u32[]{:S(2)}) %collective-permute-start.130) | collective-permute-done | bytes 2654240 | tf_op jit(solution)/shard_map/ppermute | solution.py:54
  747.8 24.3 %collective-permute-done.115 = bf16[4,144,1024]{2,1,0:T(8,128)(2,1)S(1)} collective-permute-done((bf16[4,144,1024]{2,1,0:T(8,128)(2,1)S(1)}, bf16[4,144,1024]{2,1,0:T(8,128)(2,1)S(1)}, u32[]{:S(2)}, u32[]{:S(2)}) %collective-permute-start.115) | collective-permute-done | bytes 1179680 | tf_op jit(solution)/shard_map/ppermute | solution.py:54
  787.3 7.1 collective-permute-done.107
  796.8 7.2 collective-permute-start.118
  858.1 20.4 %collective-permute-done.95 = bf16[256,2304]{1,0:T(8,128)(2,1)S(1)} collective-permute-done((bf16[256,2304]{1,0:T(8,128)(2,1)S(1)}, bf16[256,2304]{1,0:T(8,128)(2,1)S(1)}, u32[]{:S(2)}, u32[]{:S(2)}) %collective-permute-start.95) | collective-permute-done | bytes 1179680 | tf_op jit(solution)/shard_map/ppermute | solution.py:54
  885.0 6.3 collective-permute-done.96
  (736 shorter events, 490.3 us)
Async XLA Ops:
  11.2 35.9 %collective-permute-start.39 = (bf16[160,1024]{1,0:T(8,128)(2,1)}, bf16[160,1024]{1,0:T(8,128)(2,1)}, u32[]{:S(2)}, u32[]{:S(2)}) collective-permute-start(bf16[160,1024]{1,0:T(8,128)(2,1)} %pad_maximum_fusion.31), channel_id=1, source_target_pairs={{0,2},{2,0},{4,6},{6,4},{1,3},{3,1},{5,7},{7,5},{8,10},{10,8},{12,... | collective-permute-start | bytes 983048 | tf_op jit(solution)/shard_map/ppermute | solution.py:92
  11.2 46.6 %collective-permute-start.40 = (bf16[160,1024]{1,0:T(8,128)(2,1)}, bf16[160,1024]{1,0:T(8,128)(2,1)}, u32[]{:S(2)}, u32[]{:S(2)}) collective-permute-start(bf16[160,1024]{1,0:T(8,128)(2,1)} %pad_maximum_fusion.31), channel_id=1, source_target_pairs={{2,4},{4,2},{3,5},{5,3},{10,12},{12,10},{11,13},{13,11},{18,20},{2... | collective-permute-start | bytes 983048 | tf_op jit(solution)/shard_map/ppermute | solution.py:93
  42.4 69.9 %collective-permute-start.9 = (bf16[256,2304]{1,0:T(8,128)(2,1)S(1)}, bf16[256,2304]{1,0:T(8,128)(2,1)}, u32[]{:S(2)}, u32[]{:S(2)}) collective-permute-start(bf16[256,2304]{1,0:T(8,128)(2,1)S(1)} %copy-done.4), channel_id=1, source_target_pairs={{0,16},{8,24},{16,0},{24,8},{1,17},{9,25},{17,1},{25,9},{2,18},{10... | collective-permute-start | bytes 3538952 | tf_op jit(solution)/shard_map/ppermute | solution.py:54
  81.4 29.3 %collective-permute-start.8 = (bf16[256,2304]{1,0:T(8,128)(2,1)S(1)}, bf16[256,2304]{1,0:T(8,128)(2,1)}, u32[]{:S(2)}, u32[]{:S(2)}) collective-permute-start(bf16[256,2304]{1,0:T(8,128)(2,1)S(1)} %copy-done.4), channel_id=1, source_target_pairs={{0,8},{8,0},{16,24},{24,16},{1,9},{9,1},{17,25},{25,17},{2,10},{10... | collective-permute-start | bytes 3538952 | tf_op jit(solution)/shard_map/ppermute | solution.py:54
  95.0 31.7 %collective-permute-start.45 = (bf16[4,160,1024]{2,1,0:T(8,128)(2,1)S(1)}, bf16[4,160,1024]{2,1,0:T(8,128)(2,1)}, u32[]{:S(2)}, u32[]{:S(2)}) collective-permute-start(bf16[4,160,1024]{2,1,0:T(8,128)(2,1)S(1)} %bitcast_dynamic-update-slice_fusion), channel_id=1, source_target_pairs={{0,16},{8,24},{16,0},{24,8},{1,17},{9,25},{17,1},{25,9},{2,18},{10... | collective-permute-start | bytes 3932168 | tf_op jit(solution)/shard_map/ppermute | solution.py:54
  106.9 33.2 %collective-permute-start.44 = (bf16[4,160,1024]{2,1,0:T(8,128)(2,1)S(1)}, bf16[4,160,1024]{2,1,0:T(8,128)(2,1)}, u32[]{:S(2)}, u32[]{:S(2)}) collective-permute-start(bf16[4,160,1024]{2,1,0:T(8,128)(2,1)S(1)} %bitcast_dynamic-update-slice_fusion), channel_id=1, source_target_pairs={{0,8},{8,0},{16,24},{24,16},{1,9},{9,1},{17,25},{25,17},{2,10},{10... | collective-permute-start | bytes 3932168 | tf_op jit(solution)/shard_map/ppermute | solution.py:54
  126.7 59.7 %collective-permute-start.46 = (bf16[4,160,1024]{2,1,0:T(8,128)(2,1)}, bf16[4,160,1024]{2,1,0:T(8,128)(2,1)}, u32[]{:S(2)}, u32[]{:S(2)}) collective-permute-start(bf16[4,160,1024]{2,1,0:T(8,128)(2,1)} %collective-permute-done.45), channel_id=1, source_target_pairs={{0,8},{8,0},{16,24},{24,16},{1,9},{9,1},{17,25},{25,17},{2,10},{10... | collective-permute-start | bytes 3932168 | tf_op jit(solution)/shard_map/ppermute | solution.py:54
  144.3 26.0 %collective-permute-start.31 = (bf16[4,256,256]{2,1,0:T(8,128)(2,1)S(1)}, bf16[4,256,256]{2,1,0:T(8,128)(2,1)S(1)}, u32[]{:S(2)}, u32[]{:S(2)}) collective-permute-start(bf16[4,256,256]{2,1,0:T(8,128)(2,1)S(1)} %collective-permute-done.30), channel_id=1, source_target_pairs={{2,0},{4,6},{3,1},{5,7},{10,8},{12,14},{11,9},{13,15},{18,16},{20,... | collective-permute-start | bytes 1572872 | tf_op jit(solution)/shard_map/ppermute | solution.py:96
  146.6 28.1 %collective-permute-start.32 = (bf16[4,256,256]{2,1,0:T(8,128)(2,1)}, bf16[4,256,256]{2,1,0:T(8,128)(2,1)S(1)}, u32[]{:S(2)}, u32[]{:S(2)}) collective-permute-start(bf16[4,256,256]{2,1,0:T(8,128)(2,1)} %bitcast.57), channel_id=1, source_target_pairs={{0,8},{8,0},{16,24},{24,16},{1,9},{9,1},{17,25},{25,17},{2,10},{10... | collective-permute-start | bytes 1572872 | tf_op jit(solution)/shard_map/ppermute | solution.py:54
  149.3 25.5 %collective-permute-start.33 = (bf16[4,256,256]{2,1,0:T(8,128)(2,1)}, bf16[4,256,256]{2,1,0:T(8,128)(2,1)S(1)}, u32[]{:S(2)}, u32[]{:S(2)}) collective-permute-start(bf16[4,256,256]{2,1,0:T(8,128)(2,1)} %collective-permute-done.27), channel_id=1, source_target_pairs={{0,8},{8,0},{16,24},{24,16},{1,9},{9,1},{17,25},{25,17},{2,10},{10... | collective-permute-start | bytes 1572872 | tf_op jit(solution)/shard_map/ppermute | solution.py:54
  239.3 118.5 %collective-permute-start.49 = (bf16[128,2304]{1,0:T(8,128)(2,1)}, bf16[128,2304]{1,0:T(8,128)(2,1)}, u32[]{:S(2)}, u32[]{:S(2)}) collective-permute-start(bf16[128,2304]{1,0:T(8,128)(2,1)} %slice.427), channel_id=1, source_target_pairs={{0,1},{1,0},{2,3},{3,2},{4,5},{5,4},{6,7},{7,6},{8,9},{9,8},{10,11... | collective-permute-start | bytes 1769480 | tf_op jit(solution)/shard_map/ppermute | solution.py:54
  240.8 28.1 %collective-permute-start.59 = (bf16[128,2304]{1,0:T(8,128)(2,1)S(1)}, bf16[128,2304]{1,0:T(8,128)(2,1)S(1)}, u32[]{:S(2)}, u32[]{:S(2)}) collective-permute-start(bf16[128,2304]{1,0:T(8,128)(2,1)S(1)} %collective-permute-done.56), channel_id=1, source_target_pairs={{2,4},{4,2},{3,5},{5,3},{10,12},{12,10},{11,13},{13,11},{18,20},{2... | collective-permute-start | bytes 1769480 | tf_op jit(solution)/shard_map/ppermute | solution.py:95
  284.7 66.0 %collective-permute-start.58 = (bf16[128,2304]{1,0:T(8,128)(2,1)S(1)}, bf16[128,2304]{1,0:T(8,128)(2,1)S(1)}, u32[]{:S(2)}, u32[]{:S(2)}) collective-permute-start(bf16[128,2304]{1,0:T(8,128)(2,1)S(1)} %slice.425), channel_id=1, source_target_pairs={{0,1},{1,0},{2,3},{3,2},{4,5},{5,4},{6,7},{7,6},{8,9},{9,8},{10,11... | collective-permute-start | bytes 1769480 | tf_op jit(solution)/shard_map/ppermute | solution.py:54
  395.8 129.6 %collective-permute-start.67 = (bf16[128,2304]{1,0:T(8,128)(2,1)S(1)}, bf16[128,2304]{1,0:T(8,128)(2,1)S(1)}, u32[]{:S(2)}, u32[]{:S(2)}) collective-permute-start(bf16[128,2304]{1,0:T(8,128)(2,1)S(1)} %slice.423), channel_id=1, source_target_pairs={{0,1},{1,0},{2,3},{3,2},{4,5},{5,4},{6,7},{7,6},{8,9},{9,8},{10,11... | collective-permute-start | bytes 1769480 | tf_op jit(solution)/shard_map/ppermute | solution.py:54
  396.5 35.7 %collective-permute-start.77 = (bf16[128,2304]{1,0:T(8,128)(2,1)S(1)}, bf16[128,2304]{1,0:T(8,128)(2,1)S(1)}, u32[]{:S(2)}, u32[]{:S(2)}) collective-permute-start(bf16[128,2304]{1,0:T(8,128)(2,1)S(1)} %collective-permute-done.74), channel_id=1, source_target_pairs={{2,4},{4,2},{3,5},{5,3},{10,12},{12,10},{11,13},{13,11},{18,20},{2... | collective-permute-start | bytes 1769480 | tf_op jit(solution)/shard_map/ppermute | solution.py:95
  435.8 73.8 %collective-permute-start.76 = (bf16[128,2304]{1,0:T(8,128)(2,1)S(1)}, bf16[128,2304]{1,0:T(8,128)(2,1)S(1)}, u32[]{:S(2)}, u32[]{:S(2)}) collective-permute-start(bf16[128,2304]{1,0:T(8,128)(2,1)S(1)} %slice.421), channel_id=1, source_target_pairs={{0,1},{1,0},{2,3},{3,2},{4,5},{5,4},{6,7},{7,6},{8,9},{9,8},{10,11... | collective-permute-start | bytes 1769480 | tf_op jit(solution)/shard_map/ppermute | solution.py:54
  535.2 26.2 %collective-permute-start.132 = (bf16[1152,1152]{1,0:T(8,128)(2,1)}, bf16[1152,1152]{1,0:T(8,128)(2,1)}, u32[]{:S(2)}, u32[]{:S(2)}) collective-permute-start(bf16[1152,1152]{1,0:T(8,128)(2,1)} %convolution_convert_fusion), channel_id=1, source_target_pairs={{0,8},{8,0},{16,24},{24,16},{1,9},{9,1},{17,25},{25,17},{2,10},{10... | collective-permute-start | bytes 7962632 | tf_op jit(solution)/shard_map/ppermute | solution.py:54
  551.7 44.7 %collective-permute-start.126 = (bf16[1152,1152]{1,0:T(8,128)(2,1)}, bf16[1152,1152]{1,0:T(8,128)(2,1)}, u32[]{:S(2)}, u32[]{:S(2)}) collective-permute-start(bf16[1152,1152]{1,0:T(8,128)(2,1)} %convolution_convert_fusion.2), channel_id=1, source_target_pairs={{0,8},{8,0},{16,24},{24,16},{1,9},{9,1},{17,25},{25,17},{2,10},{10... | collective-permute-start | bytes 7962632 | tf_op jit(solution)/shard_map/ppermute | solution.py:54
  551.7 63.6 %collective-permute-start.129 = (bf16[1152,1152]{1,0:T(8,128)(2,1)}, bf16[1152,1152]{1,0:T(8,128)(2,1)}, u32[]{:S(2)}, u32[]{:S(2)}) collective-permute-start(bf16[1152,1152]{1,0:T(8,128)(2,1)} %convolution_convert_fusion.1), channel_id=1, source_target_pairs={{0,8},{8,0},{16,24},{24,16},{1,9},{9,1},{17,25},{25,17},{2,10},{10... | collective-permute-start | bytes 7962632 | tf_op jit(solution)/shard_map/ppermute | solution.py:54
  570.4 67.0 %collective-permute-start.133 = (bf16[1152,1152]{1,0:T(8,128)(2,1)}, bf16[1152,1152]{1,0:T(8,128)(2,1)}, u32[]{:S(2)}, u32[]{:S(2)}) collective-permute-start(bf16[1152,1152]{1,0:T(8,128)(2,1)} %fusion.2), channel_id=1, source_target_pairs={{0,16},{8,24},{16,0},{24,8},{1,17},{9,25},{17,1},{25,9},{2,18},{10... | collective-permute-start | bytes 7962632 | tf_op jit(solution)/shard_map/ppermute | solution.py:54
  604.4 30.1 %collective-permute-start.88 = (bf16[4,4,256,256]{3,2,0,1:T(8,128)(2,1)S(1)}, bf16[4,4,256,256]{3,2,0,1:T(8,128)(2,1)S(1)}, u32[]{:S(2)}, u32[]{:S(2)}) collective-permute-start(bf16[4,4,256,256]{3,2,0,1:T(8,128)(2,1)S(1)} %copy.117), channel_id=1, source_target_pairs={{0,8},{8,0},{16,24},{24,16},{1,9},{9,1},{17,25},{25,17},{2,10},{10... | collective-permute-start | bytes 6291464 | tf_op jit(solution)/shard_map/ppermute | solution.py:54
  630.2 59.8 %collective-permute-start.127 = (bf16[1152,1152]{1,0:T(8,128)(2,1)S(1)}, bf16[1152,1152]{1,0:T(8,128)(2,1)}, u32[]{:S(2)}, u32[]{:S(2)}) collective-permute-start(bf16[1152,1152]{1,0:T(8,128)(2,1)S(1)} %fusion), channel_id=1, source_target_pairs={{0,16},{8,24},{16,0},{24,8},{1,17},{9,25},{17,1},{25,9},{2,18},{10... | collective-permute-start | bytes 7962632 | tf_op jit(solution)/shard_map/ppermute | solution.py:54
  632.9 113.8 %collective-permute-start.130 = (bf16[1152,1152]{1,0:T(8,128)(2,1)S(1)}, bf16[1152,1152]{1,0:T(8,128)(2,1)S(1)}, u32[]{:S(2)}, u32[]{:S(2)}) collective-permute-start(bf16[1152,1152]{1,0:T(8,128)(2,1)S(1)} %fusion.1), channel_id=1, source_target_pairs={{0,16},{8,24},{16,0},{24,8},{1,17},{9,25},{17,1},{25,9},{2,18},{10... | collective-permute-start | bytes 7962632 | tf_op jit(solution)/shard_map/ppermute | solution.py:54
  633.5 60.6 %collective-permute-start.114 = (bf16[2,4,144,1024]{3,2,1,0:T(8,128)(2,1)}, bf16[2,4,144,1024]{3,2,1,0:T(8,128)(2,1)}, u32[]{:S(2)}, u32[]{:S(2)}) collective-permute-start(bf16[2,4,144,1024]{3,2,1,0:T(8,128)(2,1)} %dynamic-slice_bitcast_fusion), channel_id=1, source_target_pairs={{0,8},{8,0},{16,24},{24,16},{1,9},{9,1},{17,25},{25,17},{2,10},{10... | collective-permute-start | bytes 7077896 | tf_op jit(solution)/shard_map/ppermute | solution.py:54
  649.5 190.7 %collective-permute-start.134 = (bf16[1152,1152]{1,0:T(8,128)(2,1)S(1)}, bf16[1152,1152]{1,0:T(8,128)(2,1)}, u32[]{:S(2)}, u32[]{:S(2)}) collective-permute-start(bf16[1152,1152]{1,0:T(8,128)(2,1)S(1)} %add_convert_fusion.1), channel_id=1, source_target_pairs={{0,8},{8,0},{16,24},{24,16},{1,9},{9,1},{17,25},{25,17},{2,10},{10... | collective-permute-start | bytes 7962632 | tf_op jit(solution)/shard_map/ppermute | solution.py:54
  660.7 37.0 %collective-permute-start.92 = (bf16[4,256,256]{2,1,0:T(8,128)(2,1)S(1)}, bf16[4,256,256]{2,1,0:T(8,128)(2,1)S(1)}, u32[]{:S(2)}, u32[]{:S(2)}) collective-permute-start(bf16[4,256,256]{2,1,0:T(8,128)(2,1)S(1)} %get-tuple-element.65), channel_id=1, source_target_pairs={{2,4},{4,2},{3,5},{5,3},{10,12},{12,10},{11,13},{13,11},{18,20},{2... | collective-permute-start | bytes 1572872 | tf_op jit(solution)/shard_map/ppermute | solution.py:112
  692.5 155.3 %collective-permute-start.128 = (bf16[1152,1152]{1,0:T(8,128)(2,1)S(1)}, bf16[1152,1152]{1,0:T(8,128)(2,1)}, u32[]{:S(2)}, u32[]{:S(2)}) collective-permute-start(bf16[1152,1152]{1,0:T(8,128)(2,1)S(1)} %add_convert_fusion.3), channel_id=1, source_target_pairs={{0,8},{8,0},{16,24},{24,16},{1,9},{9,1},{17,25},{25,17},{2,10},{10... | collective-permute-start | bytes 7962632 | tf_op jit(solution)/shard_map/ppermute | solution.py:54
  697.0 75.1 %collective-permute-start.115 = (bf16[4,144,1024]{2,1,0:T(8,128)(2,1)S(1)}, bf16[4,144,1024]{2,1,0:T(8,128)(2,1)S(1)}, u32[]{:S(2)}, u32[]{:S(2)}) collective-permute-start(bf16[4,144,1024]{2,1,0:T(8,128)(2,1)S(1)} %dynamic-slice_bitcast_fusion.2), channel_id=1, source_target_pairs={{0,16},{8,24},{16,0},{24,8},{1,17},{9,25},{17,1},{25,9},{2,18},{10... | collective-permute-start | bytes 3538952 | tf_op jit(solution)/shard_map/ppermute | solution.py:54
  697.8 77.3 %collective-permute-start.90 = (bf16[4,256,256]{2,1,0:T(8,128)(2,1)S(1)}, bf16[4,256,256]{2,1,0:T(8,128)(2,1)S(1)}, u32[]{:S(2)}, u32[]{:S(2)}) collective-permute-start(bf16[4,256,256]{2,1,0:T(8,128)(2,1)S(1)} %get-tuple-element.64), channel_id=1, source_target_pairs={{2,4},{4,2},{3,5},{5,3},{10,12},{12,10},{11,13},{13,11},{18,20},{2... | collective-permute-start | bytes 1572872 | tf_op jit(solution)/shard_map/ppermute | solution.py:114
  746.8 28.3 %collective-permute-start.93 = (bf16[4,256,256]{2,1,0:T(8,128)(2,1)S(1)}, bf16[4,256,256]{2,1,0:T(8,128)(2,1)S(1)}, u32[]{:S(2)}, u32[]{:S(2)}) collective-permute-start(bf16[4,256,256]{2,1,0:T(8,128)(2,1)S(1)} %fusion.104), channel_id=1, source_target_pairs={{0,2},{2,0},{4,6},{6,4},{1,3},{3,1},{5,7},{7,5},{8,10},{10,8},{12,... | collective-permute-start | bytes 1572872 | tf_op jit(solution)/shard_map/ppermute | solution.py:115
  772.6 39.9 %collective-permute-start.116 = (bf16[144,1024]{1,0:T(8,128)(2,1)S(1)}, bf16[144,1024]{1,0:T(8,128)(2,1)S(1)}, u32[]{:S(2)}, u32[]{:S(2)}) collective-permute-start(bf16[144,1024]{1,0:T(8,128)(2,1)S(1)} %get-tuple-element.79), channel_id=1, source_target_pairs={{0,2},{6,4},{1,3},{7,5},{8,10},{14,12},{9,11},{15,13},{16,18},{22,... | collective-permute-start | bytes 884744 | tf_op jit(solution)/shard_map/ppermute | solution.py:113
  852.5 26.1 %collective-permute-start.95 = (bf16[256,2304]{1,0:T(8,128)(2,1)S(1)}, bf16[256,2304]{1,0:T(8,128)(2,1)S(1)}, u32[]{:S(2)}, u32[]{:S(2)}) collective-permute-start(bf16[256,2304]{1,0:T(8,128)(2,1)S(1)} %dynamic-slice_bitcast_fusion.3), channel_id=1, source_target_pairs={{0,16},{8,24},{16,0},{24,8},{1,17},{9,25},{17,1},{25,9},{2,18},{10... | collective-permute-start | bytes 3538952 | tf_op jit(solution)/shard_map/ppermute | solution.py:54
  (205 other events, 3515.3 us)

commit v2 on v1

v2 whole, which is shorter than its diff:
```python
import functools

import jax
import jax.numpy as jnp
from jax import lax
from jax.experimental import pallas as pl
from jax.experimental.pallas import tpu as pltpu
from jax.sharding import PartitionSpec as P

HEAD = 256
WINDOW = 4096

epsilon = 1e-06
soft_cap = 50.0
rotary_base = 10000.0
low = jnp.bfloat16
wide = jnp.float32


def dot(left, right, left_dim=1, right_dim=0):
    return lax.dot_general(
        left, right, (((left_dim,), (right_dim,)), ((), ())), preferred_element_type=wide
    )


def unit_of(values):
    scale = lax.rsqrt(jnp.mean(values * values, axis=-1, keepdims=True) + epsilon)
    return values * scale, scale


def normalize_back(values, weighted):
    unit, scale = unit_of(values)
    grad = scale * (weighted - unit * jnp.mean(weighted * unit, axis=-1, keepdims=True))
    return grad, unit


def rotary_tables(positions):
    freqs = rotary_base ** (-2.0 * jnp.arange(HEAD // 2, dtype=wide) / HEAD)
    angles = positions.astype(wide)[:, None] * freqs[None, :]
    return jnp.cos(angles), jnp.sin(angles)


def rotate(values, cosine, sine):
    half = values.shape[-1] // 2
    front, back = values[..., :half], values[..., half:]
    return jnp.concatenate([front * cosine - back * sine, back * cosine + front * sine], axis=-1)


def gated_gelu(gate, up):
    return jax.nn.gelu(gate, approximate=True) * up


def flip(x, axis, mask):
    return lax.ppermute(x, axis, [(i, i ^ mask) for i in range(lax.axis_size(axis))])


def other_core(x):
    return flip(x, "seq", 1)


def other_x(x):
    return flip(x, "seq", 2)


def other_y(x):
    return flip(x, "tensor", 1)


def after(x, *others):
    if not others:
        return x
    nothing = sum(other[(0,) * other.ndim].astype(wide) * 0.0 for other in others)
    return x + nothing.astype(x.dtype)


PAIR = [(0, 1), (1, 0), (2, 3), (3, 2)]
MIDDLE = [(1, 2), (2, 1)]
OUTWARD = [(1, 0), (2, 3)]
INWARD = [(0, 1), (3, 2)]
ENDS = [(0, 3), (3, 0)]
END_TO_NEAR = [(0, 2), (3, 1)]
MIDDLE_TO_FAR = [(1, 3), (2, 0)]


def slot_places():
    count, place = lax.axis_size("fsdp"), lax.axis_index("fsdp")
    if count != 4:
        return [jnp.int32(i) for i in range(count)]
    first = place < 2
    return [place, place ^ 1, jnp.where(first, 2, 1), jnp.where(first, 3, 0)]


def gather_slots(piece):
    count = lax.axis_size("fsdp")
    if count != 4:
        whole = lax.all_gather(piece, "fsdp", axis=0, tiled=False)
        return [whole[i] for i in range(count)]
    pair = lax.ppermute(piece, "fsdp", PAIR)
    near = lax.ppermute(piece, "fsdp", MIDDLE)
    far = lax.ppermute(piece, "fsdp", ENDS) + lax.ppermute(piece, "fsdp", END_TO_NEAR)
    return [piece, pair, near + lax.ppermute(near, "fsdp", OUTWARD), far]


def gather_places(piece):
    count, place = lax.axis_size("fsdp"), lax.axis_index("fsdp")
    if count != 4:
        whole = lax.all_gather(piece, "fsdp", axis=0, tiled=False)
        return [(whole[i], jnp.int32(i)) for i in range(count)]
    got = [(piece, place)]
    for by in range(1, count):
        pairs = [(i, (i + by) % count) for i in range(count)]
        got.append((lax.ppermute(piece, "fsdp", pairs), (place - by) % count))
    return got


def scatter_start(pieces):
    count = lax.axis_size("fsdp")
    pieces = [p.astype(low) for p in pieces]
    if count != 4:
        return [lax.psum_scatter(jnp.stack(pieces), "fsdp", scatter_dimension=0, tiled=False)]
    own, pair, near, far = pieces
    near_in = lax.ppermute(near, "fsdp", INWARD)
    ends = lax.ppermute(far, "fsdp", ENDS)
    middle = lax.ppermute(far, "fsdp", MIDDLE_TO_FAR)
    pair_in = lax.ppermute(pair, "fsdp", PAIR)
    near = (near.astype(wide) + near_in.astype(wide)).astype(low)
    return [own, pair_in, ends, middle, lax.ppermute(near, "fsdp", MIDDLE)]


def scatter_end(got):
    total = got[0].astype(wide)
    for part in got[1:]:
        total = total + part.astype(wide)
    return total


def ordered(pieces, place):
    return [lax.select_n(place ^ i, *pieces) for i in range(len(pieces))]


def swap_masks(blocks, place):
    got = [lax.dynamic_index_in_dim(blocks, place, 0, False)]
    for mask in range(1, blocks.shape[0]):
        got.append(flip(lax.dynamic_index_in_dim(blocks, place ^ mask, 0, False), "seq", mask))
    return got


def swap_seq(blocks, place):
    return ordered(swap_masks(blocks, place), place)


def dot_nt(left, right):
    return dot(left, right, 1, 1)


def visible_of(query_doc, key_doc, query_at, key_at, same, windowed):
    seen = query_doc == key_doc
    if same:
        seen = seen & (query_at >= key_at)
    if windowed:
        seen = seen & (query_at - key_at < WINDOW)
    return seen


def tiles(blocks, line, rows, chunk):
    reach = min(blocks - 1, (WINDOW - 2 + line * rows) // (line * rows))
    return [
        [
            (key_block, slot, key_block == block)
            for key_block in range(max(0, block - reach), block + 1)
            for slot in range(0, line, chunk)
        ]
        for block in range(blocks)
    ]


def chunk_of(keyed, kind, key_block, slot, chunk):
    return jnp.concatenate([keyed[kind, slot + i, key_block] for i in range(chunk)], axis=0)


def attend_kernel(
    plan, chunk, windowed, core, query, query_doc, query_at, keyed, key_doc, key_at, out, lse
):
    line, rows = keyed.shape[1], keyed.shape[3]
    kind = core[0]
    for block, parts in enumerate(plan):
        here = pl.ds(block * rows, rows)
        q = query[here, :]
        total = jnp.zeros((rows, 1), wide)
        summed = jnp.zeros((rows, HEAD), wide)
        for key_block, slot, same in parts:
            there = pl.ds((key_block * line + slot) * rows, chunk * rows)
            scores = dot_nt(q, chunk_of(keyed, kind, key_block, slot, chunk))
            weights = jnp.exp(soft_cap * jnp.tanh(scores * (1.0 / soft_cap)))
            seen = visible_of(
                query_doc[here, :], key_doc[:, there], query_at[here, :], key_at[:, there], same, windowed
            )
            weights = jnp.where(seen, weights, 0.0)
            total = total + jnp.sum(weights, axis=1, keepdims=True)
            summed = summed + dot(
                weights.astype(low), chunk_of(keyed, 1 - kind, key_block, slot, chunk)
            )
        out[here, :] = summed / total
        lse[here, :] = jnp.log(total)


def attend_back_kernel(
    plan,
    chunk,
    windowed,
    core,
    query,
    query_doc,
    query_at,
    keyed,
    key_doc,
    key_at,
    incoming,
    lse,
    delta,
    grad_query,
    grad_keyed,
    key_total,
    value_total,
):
    line, rows = keyed.shape[1], keyed.shape[3]
    kind = core[0]
    seen_by = {}
    for block, parts in enumerate(plan):
        for key_block, slot, same in parts:
            seen_by.setdefault((key_block, slot), []).append((block, same))
    grad_query[...] = jnp.zeros_like(grad_query)
    for key_block, slot in sorted(seen_by):
        there = pl.ds((key_block * line + slot) * rows, chunk * rows)
        k = chunk_of(keyed, kind, key_block, slot, chunk)
        v = chunk_of(keyed, 1 - kind, key_block, slot, chunk)
        for turn, (block, same) in enumerate(seen_by[key_block, slot]):
            here = pl.ds(block * rows, rows)
            q = query[here, :]
            d = incoming[here, :]
            bent = jnp.tanh(dot_nt(k, q) * (1.0 / soft_cap))
            weights = jnp.exp(soft_cap * bent - lse[:, here])
            seen = visible_of(
                query_doc[:, here], key_doc[there, :], query_at[:, here], key_at[there, :], same, windowed
            )
            weights = jnp.where(seen, weights, 0.0)
            grads = weights * (dot_nt(v, d) - delta[:, here]) * (1.0 - bent * bent)
            grads = grads.astype(low)
            value_part = dot(weights.astype(low), d)
            key_part = dot(grads, q)
            if turn == 0:
                value_total[...] = value_part
                key_total[...] = key_part
            else:
                value_total[...] += value_part
                key_total[...] += key_part
            grad_query[here, :] += dot(grads, k, 0, 0)
        for i in range(chunk):
            inside = pl.ds(i * rows, rows)
            grad_keyed[kind, slot + i, key_block] = key_total[inside, :].astype(low)
            grad_keyed[1 - kind, slot + i, key_block] = value_total[inside, :].astype(low)


def in_vmem(count):
    return [pl.BlockSpec(memory_space=pltpu.SMEM)] + [pl.BlockSpec(memory_space=pltpu.VMEM)] * count


def kernel_sizes(keyed):
    _, line, blocks, rows, _ = keyed.shape
    chunk = min(line, max(1, 1024 // rows))
    plan = tiles(blocks, line, rows, chunk)
    count = sum(len(parts) for parts in plan) * rows * rows * chunk
    return plan, chunk, line * blocks * rows > WINDOW, count


def attend(core, query, docs, ats, keyed, key_docs, key_ats):
    tokens = query.shape[0]
    plan, chunk, windowed, count = kernel_sizes(keyed)
    return pl.pallas_call(
        functools.partial(attend_kernel, plan, chunk, windowed),
        out_shape=(
            jax.ShapeDtypeStruct((tokens, HEAD), wide),
            jax.ShapeDtypeStruct((tokens, 1), wide),
        ),
        in_specs=in_vmem(6),
        out_specs=(pl.BlockSpec(memory_space=pltpu.VMEM),) * 2,
        compiler_params=pltpu.CompilerParams(vmem_limit_bytes=48 * 1024 * 1024),
        cost_estimate=pl.CostEstimate(
            flops=4 * count * HEAD, bytes_accessed=2 * keyed.size, transcendentals=2 * count
        ),
        name="attend",
    )(core, query, docs, ats, keyed, key_docs, key_ats)


def attend_back(core, query, docs, ats, keyed, key_docs, key_ats, incoming, lse, delta):
    tokens = query.shape[0]
    plan, chunk, windowed, count = kernel_sizes(keyed)
    total = pltpu.VMEM((chunk * keyed.shape[3], HEAD), wide)
    return pl.pallas_call(
        functools.partial(attend_back_kernel, plan, chunk, windowed),
        out_shape=(
            jax.ShapeDtypeStruct((tokens, HEAD), wide),
            jax.ShapeDtypeStruct(keyed.shape, low),
        ),
        in_specs=in_vmem(9),
        out_specs=(pl.BlockSpec(memory_space=pltpu.VMEM),) * 2,
        scratch_shapes=[total, total],
        compiler_params=pltpu.CompilerParams(vmem_limit_bytes=56 * 1024 * 1024),
        cost_estimate=pl.CostEstimate(
            flops=10 * count * HEAD, bytes_accessed=4 * keyed.size, transcendentals=2 * count
        ),
        name="attend_back",
    )(
        core,
        query,
        docs,
        ats,
        keyed,
        key_docs,
        key_ats,
        incoming,
        lse,
        delta,
    )


def join_kernel(core, mine, theirs, out):
    ours = pl.program_id(0) == core[0]

    @pl.when(ours)
    def _():
        out[...] = mine[...].astype(wide)

    @pl.when(jnp.logical_not(ours))
    def _():
        out[...] = theirs[...].astype(wide)


def join_halves(core, mine, theirs):
    half, width = mine.shape
    rows = next(rows for rows in (288, 144, 72, half) if half % rows == 0)
    steps = half // rows
    return pl.pallas_call(
        join_kernel,
        out_shape=jax.ShapeDtypeStruct((2 * half, width), wide),
        grid_spec=pltpu.PrefetchScalarGridSpec(
            num_scalar_prefetch=1,
            grid=(2, steps),
            in_specs=[
                pl.BlockSpec((rows, width), lambda h, i, c: (jnp.where(h == c[0], i, 0), 0)),
                pl.BlockSpec((rows, width), lambda h, i, c: (jnp.where(h == c[0], 0, i), 0)),
            ],
            out_specs=pl.BlockSpec((rows, width), lambda h, i, c: (h * steps + i, 0)),
        ),
        compiler_params=pltpu.CompilerParams(vmem_limit_bytes=32 * 1024 * 1024),
        cost_estimate=pl.CostEstimate(flops=0, bytes_accessed=14 * half * width, transcendentals=0),
        name="join_halves",
    )(core, mine, theirs)


def per_device(
    layer_input,
    positions,
    gain_attn_in,
    w_query,
    w_key,
    w_value,
    w_out,
    gain_attn_out,
    gain_ffn_in,
    w_gate,
    w_up,
    w_down,
    gain_ffn_out,
    cotangent,
):
    rows, width = layer_input.shape
    half_rows = cotangent.shape[0]
    blocks = lax.axis_size("seq")
    line = lax.axis_size("fsdp")
    seq_place = lax.axis_index("seq")
    fsdp_place = lax.axis_index("fsdp")
    tensor_place = lax.axis_index("tensor")
    core = seq_place % 2
    side = seq_place // 2
    share = gain_attn_in.shape[0]
    heads = w_query.shape[1] // HEAD
    places = slot_places()
    scale = HEAD ** (-0.5)
    assert blocks == heads == 4 and w_key.shape[1] == 2 * HEAD

    query_blocks = w_query.reshape(share, blocks, HEAD).transpose(1, 0, 2)
    keyed_blocks = jnp.stack(
        [(w_key, w_value)[i % 2][:, (i // 2) * HEAD : (i // 2 + 1) * HEAD] for i in range(blocks)]
    )

    def assemble(pieces):
        whole = jnp.zeros((blocks, line, share, HEAD), low)
        for piece, at in pieces:
            whole = lax.dynamic_update_slice(whole, piece[:, None], (0, at, 0, 0))
        return whole.reshape(width, HEAD)

    from_x = other_x(layer_input)

    small = jnp.concatenate(
        [positions.astype(wide)]
        + [g.astype(wide) for g in (gain_attn_in, gain_attn_out, gain_ffn_in, gain_ffn_out)]
    )
    small = jnp.pad(small, (0, -small.shape[0] % 1024)).reshape(-1, 128)
    small_line = jnp.zeros((line,) + small.shape, wide)
    for piece, at in gather_places(small):
        small_line = lax.dynamic_update_index_in_dim(small_line, piece, at, 0)
    small_all = jnp.stack(
        ordered([small_line] + [flip(small_line, "seq", m) for m in range(1, blocks)], seq_place)
    ).reshape(blocks, line, -1)
    gain_one, gain_two, gain_three, gain_four = [
        small_all[:, :, rows + i * share : rows + (i + 1) * share].reshape(width) for i in range(4)
    ]
    place_all = small_all[:, :, :rows].astype(jnp.int32)

    keyed_piece = after(jnp.stack(swap_seq(keyed_blocks, seq_place)), from_x, gain_one)
    from_core = other_core(layer_input)
    from_far = other_core(from_x)

    keyed_w = assemble(gather_places(keyed_piece))
    query_piece = jnp.stack(swap_seq(query_blocks, seq_place))
    query_w = lax.all_gather(after(query_piece, keyed_w), "fsdp", axis=1, tiled=False).reshape(width, HEAD)

    out_w = lax.all_gather(after(w_out.T, keyed_piece), ("seq", "fsdp"), axis=0, tiled=True)

    normed = jnp.zeros((blocks, rows, width), low)
    for mask, piece in enumerate((layer_input, from_core, from_x, from_far)):
        unit = unit_of(piece.astype(wide))[0]
        normed = lax.dynamic_update_index_in_dim(
            normed, (unit * gain_one).astype(low), seq_place ^ mask, 0
        )
    normed = normed.reshape(blocks * rows, width)
    keyed_raw = dot(normed, keyed_w)

    token_rows = jnp.arange(rows, dtype=jnp.int32)
    block_starts = jnp.arange(blocks, dtype=jnp.int32)[:, None, None] * (line * rows)
    key_at = block_starts + (jnp.stack(places) * rows)[None, :, None] + token_rows
    key_places = jnp.stack(
        [lax.dynamic_index_in_dim(place_all, at, 1, False) for at in places], axis=1
    )
    key_doc = (key_at - key_places).reshape(-1)
    key_at = key_at.reshape(-1)
    own_positions = lax.dynamic_index_in_dim(place_all, fsdp_place, 1, False).reshape(-1)
    query_at = (block_starts[:, 0] + fsdp_place * rows + token_rows).reshape(-1)
    query_doc = query_at - own_positions
    cosine, sine = rotary_tables(own_positions)
    plain = core == 1

    keyed = jnp.where(plain, keyed_raw, rotate(keyed_raw, cosine, sine)).astype(low)
    keyed_slots = gather_slots(keyed.reshape(blocks, rows, HEAD))
    other_slots = [other_core(piece) for piece in keyed_slots]
    keyed_all = jnp.stack(keyed_slots + other_slots).reshape(2, line, blocks, rows, HEAD)
    query_raw = dot(normed, query_w)
    queries = (rotate(query_raw, cosine, sine) * scale).astype(low)
    core_array = core.reshape(1).astype(jnp.int32)

    attend_out, log_total = attend(
        core_array,
        queries,
        query_doc[:, None],
        query_at[:, None],
        keyed_all,
        key_doc[None, :],
        key_at[None, :],
    )
    back_marks = (query_doc[None, :], query_at[None, :], key_doc[:, None], key_at[:, None])
    log_total = log_total.reshape(1, -1)

    attended = jnp.concatenate(
        swap_seq(attend_out.astype(low).reshape(blocks, rows, HEAD), seq_place), axis=1
    )
    away = lax.dynamic_slice_in_dim(attended, (1 - tensor_place) * half_rows, half_rows, 0)
    kept = lax.dynamic_slice_in_dim(attended, tensor_place * half_rows, half_rows, 0)
    branch_away = other_y(dot(away, out_w, 1, 1).astype(low))
    branch = dot(kept, out_w, 1, 1) + branch_away.astype(wide)

    both_w = after(jnp.concatenate([query_w, keyed_w], axis=1), attended)
    both_all = lax.all_gather(both_w, "seq", axis=0, tiled=False)

    inputs_half = lax.dynamic_slice_in_dim(
        layer_input, tensor_place * half_rows, half_rows, 0
    ).astype(wide)
    middle = inputs_half + unit_of(branch)[0] * gain_two
    ffn_in = (unit_of(middle)[0] * gain_three).astype(low)

    def through(piece, work):
        if line != 4:
            parts = [
                work(jnp.concatenate([slot, other_y(slot)], axis=0)) for slot in gather_slots(piece)
            ]
            kept = [part[0] for part in parts]
            sums = [
                p[:half_rows] + other_y(p[half_rows:].astype(low)).astype(wide) for _, p in parts
            ]
            return kept, scatter_end(scatter_start(sums))

        def joined(one, two, *others):
            return after(jnp.concatenate([one, two], axis=0), *others)

        pair = lax.ppermute(piece, "fsdp", PAIR)
        near_middle = lax.ppermute(piece, "fsdp", MIDDLE)
        own_y = other_y(piece)
        pair_y = other_y(pair)
        far_middle = lax.ppermute(pair, "fsdp", MIDDLE)
        near_end = lax.ppermute(near_middle, "fsdp", OUTWARD)
        own_kept, own_part = work(joined(piece, own_y, pair, near_middle))
        near = near_middle + near_end
        near_y = other_y(near)
        far = far_middle + lax.ppermute(far_middle, "fsdp", OUTWARD)
        pair_kept, pair_part = work(joined(pair, pair_y, near, far_middle))
        far_y = other_y(far)
        near_kept, near_part = work(joined(near, near_y, far))
        far_kept, far_part = work(joined(far, far_y, near_part))
        kept = (own_kept, pair_kept, near_kept, far_kept)

        def sent(part, *others):
            return other_y(after(part[half_rows:].astype(low), *others))

        def added(part, got, *others):
            return after(part[:half_rows] + got.astype(wide), *others).astype(low)

        near_got = sent(near_part)
        far_got = sent(far_part)
        pair_got = sent(pair_part, far_part, near_got)
        own_got = sent(own_part, far_got)
        near_sum = added(near_part, near_got)
        near_in = lax.ppermute(near_sum, "fsdp", INWARD)
        far_sum = added(far_part, far_got)
        far_ends = lax.ppermute(far_sum, "fsdp", ENDS)
        far_middle = lax.ppermute(far_sum, "fsdp", MIDDLE_TO_FAR)
        near_sum = (near_sum.astype(wide) + near_in.astype(wide)).astype(low)
        near_middle = lax.ppermute(near_sum, "fsdp", MIDDLE)
        pair_sum = added(pair_part, pair_got)
        pair_in = lax.ppermute(pair_sum, "fsdp", PAIR)
        total = own_part[:half_rows]
        for part in (own_got, near_middle, far_ends, far_middle, pair_in):
            total = total + part.astype(wide)
        return kept, total

    def forward(part):
        gate, up = dot(part, w_gate), dot(part, w_up)
        hidden = gated_gelu(gate, up).astype(low)
        return (part, gate, up, hidden), dot(hidden, w_down)

    forward_kept, ffn_out = through(ffn_in, forward)
    ffn_out = after(ffn_out, both_all)
    unit_out, _ = unit_of(ffn_out)
    output = middle + unit_out * gain_four

    incoming = cotangent.astype(wide)
    grad_ffn_out, _ = normalize_back(ffn_out, incoming * gain_four)
    gain_four_part = jnp.sum(incoming * unit_out, axis=0)
    still = list(forward_kept)

    def backward(part):
        _, gate, up, _ = still.pop(0)
        _, pullback = jax.vjp(gated_gelu, gate, up)
        grad_gate, grad_up = pullback(dot(part, w_down, 1, 1))
        grad_gate, grad_up = grad_gate.astype(low), grad_up.astype(low)
        return (part, grad_gate, grad_up), dot(grad_gate, w_gate, 1, 1) + dot(grad_up, w_up, 1, 1)

    rows_all = jnp.concatenate([k[0] for k in forward_kept], axis=0)
    hidden_all = jnp.concatenate([k[3] for k in forward_kept], axis=0)

    def rows_product(left, rights, *others):
        return dot(left, after(jnp.concatenate(rights, axis=0), *others), 0, 0).astype(low)

    def core_half(grad):
        half = grad.shape[0] // 2
        sent = lax.dynamic_slice_in_dim(grad, (1 - core) * half, half, 0)
        kept = lax.dynamic_slice_in_dim(grad, core * half, half, 0)
        return (kept.astype(wide) + other_core(sent).astype(wide)).astype(low)

    def over_x(mine):
        return lax.psum(mine, "seq", axis_index_groups=[[0, 2], [1, 3]])

    def both_halves(mine, *hold):
        mine = after(mine, *hold)
        return join_halves(core_array, mine, other_core(mine))

    backward_kept, grad_ffn_in = through(grad_ffn_out.astype(low), backward)

    grad_mid_norm, unit_middle = normalize_back(middle, grad_ffn_in * gain_three)
    gain_three_part = jnp.sum(grad_ffn_in * unit_middle, axis=0)
    grad_middle = incoming + grad_mid_norm
    grad_branch, unit_branch = normalize_back(branch, grad_middle * gain_two)
    gain_two_part = jnp.sum(grad_middle * unit_branch, axis=0)
    grad_branch = grad_branch.astype(low)
    gain_parts = jnp.stack([gain_two_part, gain_three_part, gain_four_part])
    branch_other = other_y(grad_branch)

    down_mine = core_half(rows_product(hidden_all, [k[0] for k in backward_kept], branch_other))
    gate_mine = core_half(rows_product(rows_all, [k[1] for k in backward_kept], grad_branch))
    up_mine = core_half(rows_product(rows_all, [k[2] for k in backward_kept], branch_other))
    down_sum, gate_sum, up_sum = over_x((down_mine, gate_mine, up_mine))

    always = positions[0] >= 0

    def stretch(work):
        shapes = jax.eval_shape(work)
        return lax.cond(
            always, work, lambda: jax.tree.map(lambda x: jnp.zeros(x.shape, x.dtype), shapes)
        )

    def attention_back():
        gains = gain_parts + other_y(gain_parts)
        first = tensor_place == 0
        branch_cot = jnp.concatenate(
            [
                jnp.where(first, grad_branch, branch_other),
                jnp.where(first, branch_other, grad_branch),
            ],
            axis=0,
        )
        grad_attended = dot(branch_cot, out_w).astype(low)
        grad_attended = jnp.concatenate(
            swap_seq(grad_attended.reshape(rows, blocks, HEAD).transpose(1, 0, 2), seq_place), axis=0
        )
        delta = jnp.sum(attend_out * grad_attended.astype(wide), axis=1)
        grad_queries, grad_keyed = attend_back(
            core_array,
            queries,
            *back_marks[:2],
            keyed_all,
            *back_marks[2:],
            grad_attended,
            log_total,
            delta[None, :],
        )
        keyed_got = other_core(grad_keyed[1])
        keyed_started = scatter_start(
            [grad_keyed[0, i].astype(wide) + keyed_got[i].astype(wide) for i in range(line)]
        )
        grad_query_raw = rotate(grad_queries * scale, cosine, -sine).astype(low)

        extra = 16
        gain_rows = gains.reshape(3, 2, 2, line, share).transpose(2, 3, 1, 0, 4)
        gain_rows = gain_rows.reshape(2, line, 2, 1, 3 * share).astype(low)
        gain_rows = jnp.pad(
            gain_rows, ((0, 0),) * 3 + ((0, extra - 1), (0, heads * HEAD - 3 * share))
        )
        out_grad = dot(after(branch_cot, grad_queries), attended, 0, 0).astype(low)
        out_grad = out_grad.reshape(2, 2, line, share, heads * HEAD).transpose(1, 2, 0, 3, 4)
        out_grad = jnp.concatenate([out_grad, gain_rows], axis=3)
        out_got = other_core(lax.dynamic_index_in_dim(out_grad, 1 - core, 0, False))
        out_sum = lax.dynamic_index_in_dim(out_grad, core, 0, False).astype(wide)
        out_sum = (out_sum + out_got.astype(wide)).astype(low)

        keyed_own = scatter_end(keyed_started).reshape(blocks * rows, HEAD)
        grad_keyed_raw = jnp.where(plain, keyed_own, rotate(keyed_own, cosine, -sine)).astype(low)
        return jnp.concatenate([grad_query_raw, grad_keyed_raw], axis=1), out_sum

    grad_raw, out_sum = stretch(attention_back)

    weight_grad = dot(normed, grad_raw, 0, 0).astype(low).reshape(blocks, line, share, 2 * HEAD)
    weight_started = scatter_start(
        [lax.dynamic_index_in_dim(weight_grad, at, 1, False) for at in places]
    )

    raw_mine = swap_seq(grad_raw.reshape(blocks, rows, 2 * HEAD), seq_place)
    back = sum(dot(part, both_all[i], 1, 1) for i, part in enumerate(raw_mine))
    back_got = other_y(
        lax.dynamic_slice_in_dim(back, (1 - tensor_place) * half_rows, half_rows, 0).astype(low)
    )
    back = lax.dynamic_slice_in_dim(back, tensor_place * half_rows, half_rows, 0)
    back = back + back_got.astype(wide)
    grad_input = grad_middle + normalize_back(inputs_half, back * gain_one)[0]

    out_parts = after(out_sum, weight_grad)
    out_started = scatter_start(
        [lax.dynamic_index_in_dim(out_parts, at, 0, False) for at in places]
    )
    weight_sum = scatter_end(weight_started).astype(low)
    out_sum = scatter_end(out_started)
    out_got = other_x(lax.dynamic_index_in_dim(out_sum, 1 - side, 0, False).astype(low))
    weight_grads = [part.astype(wide) for part in swap_seq(weight_sum, seq_place)]
    query_grads = jnp.concatenate([part[:, :HEAD] for part in weight_grads], axis=1)
    key_grads = jnp.concatenate([part[:, HEAD:] for part in weight_grads[0::2]], axis=1)
    value_grads = jnp.concatenate([part[:, HEAD:] for part in weight_grads[1::2]], axis=1)
    gain_one_part = (
        jnp.sum(query_grads * w_query.astype(wide), axis=1)
        + jnp.sum(key_grads * w_key.astype(wide), axis=1)
        + jnp.sum(value_grads * w_value.astype(wide), axis=1)
    )
    grad_gain_one = (gain_one_part + other_y(gain_one_part)) / gain_attn_in.astype(wide)
    out_sum = lax.dynamic_index_in_dim(out_sum, side, 0, False) + out_got.astype(wide)
    gain_sums = out_sum[share, : 3 * share].reshape(3, share)

    return (
        output.astype(low),
        grad_input,
        grad_gain_one,
        query_grads,
        key_grads,
        value_grads,
        out_sum[:share].T,
        gain_sums[0],
        gain_sums[1],
        both_halves(gate_sum, weight_started[:3][-1]),
        both_halves(up_sum, weight_started[:3][-1]),
        both_halves(down_sum, weight_started[:3][-1]),
        gain_sums[2],
    )


def solution(mesh):
    by_rows = P(("seq", "fsdp"))
    placed = (
        P(("seq", "fsdp"), None),
        by_rows,
        by_rows,
        P(("seq", "fsdp"), "tensor"),
        P(("seq", "fsdp"), "tensor"),
        P(("seq", "fsdp"), "tensor"),
        P("tensor", ("seq", "fsdp")),
        by_rows,
        by_rows,
        P(None, ("fsdp", "tensor")),
        P(None, ("fsdp", "tensor")),
        P(("fsdp", "tensor"), None),
        by_rows,
        P(("seq", "fsdp", "tensor"), None),
    )
    return jax.shard_map(
        per_device,
        mesh=mesh,
        in_specs=placed,
        out_specs=(
            P(("seq", "fsdp", "tensor"), None),
            P(("seq", "fsdp", "tensor"), None),
            by_rows,
            P(("seq", "fsdp"), "tensor"),
            P(("seq", "fsdp"), "tensor"),
            P(("seq", "fsdp"), "tensor"),
            P("tensor", ("seq", "fsdp")),
            by_rows,
            by_rows,
            P(None, ("fsdp", "tensor")),
            P(None, ("fsdp", "tensor")),
            P(("fsdp", "tensor"), None),
            by_rows,
        ),
        check_vma=False,
    )
```

time: 905 us -> 823 us (0.909)
  waiting for transfers between devices: 419 us -> 339 us
  starting transfers between devices: 182 us -> 129 us
  local copies, waits for them, and re-layouts: 40.4 us -> 76.9 us
  between operations: 4.26 us -> 36.4 us
  matrix products: 133 us -> 103 us
  Pallas kernels: 22.8 us -> 37.3 us
    ppermute x70 -> x58, waiting for transfers between devices: 262 us -> 135 us  [flip(): lax.ppermute(x, axis, [(i, i ^ mask) for i in range(lax.axis_size(axis))])]
    ppermute x51 -> x44, waiting for transfers between devices: 143 us -> 202 us  [the longest x3 48.5 us: scatter_start(): pair_in = lax.ppermute(pair, 'fsdp', PAIR)]
    dot_general x40 -> x38, matrix products: 133 us -> 103 us  [dot(): lax.dot_general(left, right, (((left_dim,), (right_dim,)), ((), ())), pre...]
    ppermute x51 -> x44, starting transfers between devices: 105 us -> 84.9 us  [the longest x2 11.8 us: through(): far = far_middle + lax.ppermute(far_middle, 'fsdp', OUTWARD)]
    slice x12 -> x39, local copies, waits for them, and re-layouts: 2.78 us -> 21.6 us  [the longest x29 17 us: after(): other[(0,) * other.ndim].astype(wide) * 0.0]
    ppermute x70 -> x58, starting transfers between devices: 58.1 us -> 41.4 us  [flip(): lax.ppermute(x, axis, [(i, i ^ mask) for i in range(lax.axis_size(axis))])]
    unnamed x219 -> x286, local copies, waits for them, and re-layouts: 5.86 us -> 21.3 us
    pallas_call x0 -> x3, Pallas kernels: none -> 14.3 us  [join_halves(): pl.pallas_call(join_kernel, out_shape=jax.ShapeDtypeStruct((2 * half, wid...]
  transfers between devices with their start and end apart: 135 -> 108, of which waited for: 55 -> 42; matrix products, arithmetic and copies ran while one was open for 27% -> 28% of each run, Pallas kernels for 3% -> 4%
where the time goes in v2:
time: 823 us; the launch traced here: 807 us
  waiting for transfers between devices  339 us (41%)
  starting transfers between devices  129 us (16%)
  matrix products  103 us (13%)
  other arithmetic  84.9 us (10%)
  local copies, waits for them, and re-layouts  76.9 us (9%)
  Pallas kernels  37.3 us (5%)
  between operations  36.4 us (4%)
    ppermute x58, waiting for transfers between devices, flip(): lax.ppermute(x, axis, [(i, i ^ mask) for i in range(lax.axis_size(axis))])  135 us
    dot_general x38, matrix products, dot(): lax.dot_general(left, right, (((left_dim,), (right_dim,)), ((), ())), pre...  103 us
    ppermute x3, waiting for transfers between devices, scatter_start(): pair_in = lax.ppermute(pair, 'fsdp', PAIR)  48.5 us
    ppermute x58, starting transfers between devices, flip(): lax.ppermute(x, axis, [(i, i ^ mask) for i in range(lax.axis_size(axis))])  41.4 us
    ppermute x1, waiting for transfers between devices, gather_slots(): return [piece, pair, near + lax.ppermute(near, 'fsdp', OUTWARD), far]  26.1 us
    ppermute x3, waiting for transfers between devices, scatter_start(): near_in = lax.ppermute(near, 'fsdp', INWARD)  25.2 us
    ppermute x6, waiting for transfers between devices, gather_places(): got.append((lax.ppermute(piece, 'fsdp', pairs), (place - by) % count))  24.5 us
    ppermute x2, waiting for transfers between devices, through(): pair = lax.ppermute(piece, 'fsdp', PAIR)  21.8 us
  transfers between devices with their start and end apart: 108, of which 42 were waited for; matrix products, arithmetic and copies ran while one was open for 28% of the time, Pallas kernels for 4%

profile of v2, /device:TPU:0, one launch (start us, length us, event | category | flops | bytes accessed | tf_op | source)
XLA Modules:
  0.0 807.4 jit_solution(12001076810931066031)
XLA Ops:
  23.7 19.7 %collective-permute-done.16 = f32[4,8,128]{2,1,0:T(8,128)S(1)} collective-permute-done((f32[4,8,128]{2,1,0:T(8,128)S(1)}, f32[4,8,128]{2,1,0:T(8,128)S(1)}, u32[]{:S(2)}, u32[]{:S(2)}) %collective-permute-start.16) | collective-permute-done | bytes 16416 | tf_op jit(solution)/shard_map/ppermute | solution.py:54
  60.3 7.3 collective-permute-done.26
  67.7 17.2 %collective-permute-done.27 = bf16[4,144,256]{2,1,0:T(8,128)(2,1)S(1)} collective-permute-done((bf16[4,144,256]{2,1,0:T(8,128)(2,1)S(1)}, bf16[4,144,256]{2,1,0:T(8,128)(2,1)S(1)}, u32[]{:S(2)}, u32[]{:S(2)}) %collective-permute-start.27) | collective-permute-done | bytes 294944 | tf_op jit(solution)/shard_map/ppermute | solution.py:112
  135.8 26.1 %collective-permute-done.31 = bf16[4,256,256]{2,1,0:T(8,128)(2,1)} collective-permute-done((bf16[4,256,256]{2,1,0:T(8,128)(2,1)}, bf16[4,256,256]{2,1,0:T(8,128)(2,1)}, u32[]{:S(2)}, u32[]{:S(2)}) %collective-permute-start.31) | collective-permute-done | bytes 524320 | tf_op jit(solution)/shard_map/ppermute | solution.py:101
  172.2 7.5 attend.1
  202.4 8.8 %collective-permute-done.41 = bf16[128,2304]{1,0:T(8,128)(2,1)} collective-permute-done((bf16[128,2304]{1,0:T(8,128)(2,1)}, bf16[128,2304]{1,0:T(8,128)(2,1)}, u32[]{:S(2)}, u32[]{:S(2)}) %collective-permute-start.41) | collective-permute-done | bytes 589856 | tf_op jit(solution)/shard_map/ppermute | solution.py:54
  223.1 10.5 %collective-permute-done.43 = bf16[128,2304]{1,0:T(8,128)(2,1)S(1)} collective-permute-done((bf16[128,2304]{1,0:T(8,128)(2,1)S(1)}, bf16[128,2304]{1,0:T(8,128)(2,1)S(1)}, u32[]{:S(2)}, u32[]{:S(2)}) %collective-permute-start.43) | collective-permute-done | bytes 589856 | tf_op jit(solution)/shard_map/ppermute | solution.py:505
  254.8 10.0 %collective-permute-start.46 = (bf16[128,2304]{1,0:T(8,128)(2,1)S(1)}, bf16[128,2304]{1,0:T(8,128)(2,1)S(1)}, u32[]{:S(2)}, u32[]{:S(2)}) collective-permute-start(bf16[128,2304]{1,0:T(8,128)(2,1)S(1)} %collective-permute-done.45), channel_id=1, source_target_pairs={{2,0},{4,6},{3,1},{5,7},{10,8},{12,14},{11,9},{13,15},{18,16},{20,... | collective-permute-start | bytes 1769480 | tf_op jit(solution)/shard_map/ppermute | solution.py:514
  282.4 5.9 collective-permute-done.47
  305.9 14.1 %collective-permute-done.50 = bf16[128,2304]{1,0:T(8,128)(2,1)S(1)} collective-permute-done((bf16[128,2304]{1,0:T(8,128)(2,1)S(1)}, bf16[128,2304]{1,0:T(8,128)(2,1)S(1)}, u32[]{:S(2)}, u32[]{:S(2)}) %collective-permute-start.50) | collective-permute-done | bytes 589856 | tf_op jit(solution)/shard_map/ppermute | solution.py:54
  337.6 9.0 %collective-permute-done.56 = bf16[128,2304]{1,0:T(8,128)(2,1)} collective-permute-done((bf16[128,2304]{1,0:T(8,128)(2,1)}, bf16[128,2304]{1,0:T(8,128)(2,1)}, u32[]{:S(2)}, u32[]{:S(2)}) %collective-permute-start.56) | collective-permute-done | bytes 589856 | tf_op jit(solution)/shard_map/ppermute | solution.py:535
  346.6 9.6 %collective-permute-done.59 = bf16[128,2304]{1,0:T(8,128)(2,1)} collective-permute-done((bf16[128,2304]{1,0:T(8,128)(2,1)}, bf16[128,2304]{1,0:T(8,128)(2,1)}, u32[]{:S(2)}, u32[]{:S(2)}) %collective-permute-start.59) | collective-permute-done | bytes 589856 | tf_op jit(solution)/shard_map/ppermute | solution.py:539
  366.3 11.3 %collective-permute-done.61 = bf16[128,2304]{1,0:T(8,128)(2,1)S(1)} collective-permute-done((bf16[128,2304]{1,0:T(8,128)(2,1)S(1)}, bf16[128,2304]{1,0:T(8,128)(2,1)S(1)}, u32[]{:S(2)}, u32[]{:S(2)}) %collective-permute-start.61) | collective-permute-done | bytes 589856 | tf_op jit(solution)/shard_map/ppermute | solution.py:505
  387.7 10.4 %collective-permute-done.66 = bf16[128,2304]{1,0:T(8,128)(2,1)S(1)} collective-permute-done((bf16[128,2304]{1,0:T(8,128)(2,1)S(1)}, bf16[128,2304]{1,0:T(8,128)(2,1)S(1)}, u32[]{:S(2)}, u32[]{:S(2)}) %collective-permute-start.66) | collective-permute-done | bytes 589856 | tf_op jit(solution)/shard_map/ppermute | solution.py:510
  408.4 10.3 %collective-permute-done.64 = bf16[128,2304]{1,0:T(8,128)(2,1)S(1)} collective-permute-done((bf16[128,2304]{1,0:T(8,128)(2,1)S(1)}, bf16[128,2304]{1,0:T(8,128)(2,1)S(1)}, u32[]{:S(2)}, u32[]{:S(2)}) %collective-permute-start.64) | collective-permute-done | bytes 589856 | tf_op jit(solution)/shard_map/ppermute | solution.py:514
  429.5 5.8 collective-permute-done.65
  450.0 14.1 %collective-permute-done.68 = bf16[128,2304]{1,0:T(8,128)(2,1)S(1)} collective-permute-done((bf16[128,2304]{1,0:T(8,128)(2,1)S(1)}, bf16[128,2304]{1,0:T(8,128)(2,1)S(1)}, u32[]{:S(2)}, u32[]{:S(2)}) %collective-permute-start.68) | collective-permute-done | bytes 589856 | tf_op jit(solution)/shard_map/ppermute | solution.py:54
  478.9 5.9 collective-permute-done.69
  484.9 5.9 collective-permute-done.74
  490.8 8.7 %collective-permute-done.77 = bf16[128,2304]{1,0:T(8,128)(2,1)} collective-permute-done((bf16[128,2304]{1,0:T(8,128)(2,1)}, bf16[128,2304]{1,0:T(8,128)(2,1)}, u32[]{:S(2)}, u32[]{:S(2)}) %collective-permute-start.77) | collective-permute-done | bytes 589856 | tf_op jit(solution)/shard_map/ppermute | solution.py:539
  506.2 6.4 convolution_convert_fusion.4
  521.1 6.9 convolution_convert_fusion.3
  557.4 99.5 %conditional.1 = (bf16[1024,512]{1,0:T(8,128)(2,1)S(1)}, bf16[4,256,512]{2,1,0:T(8,128)(2,1)S(1)}, bf16[4,2,160,1024]{3,2,1,0:T(8,128)(2,1)S(1)}) conditional(s32[]{:T(128)} %bitcast.108, () %tuple.18, (s32[4,256]{1,0:T(4,128)S(1)}, s32[4,256]{1,0:T(4,128)S(1)}, s32[4,1,256]{2,1,0:T(1,128)S(1)}, s32[4,4,256]{2,1,0:T(4,128)S(1)}, ...), branch_computations={%region_14.15_spmd, %region_15.17_spmd} | conditional | flops 9181550592 | bytes 198138048 | solution.py:606
  574.1 6.0 collective-permute-done.1
  582.4 15.5 %attend_back.1 = (f32[1024,256]{1,0:T(8,128)}, bf16[2,4,4,256,256]{4,3,2,1,0:T(8,128)(2,1)}) custom-call(s32[1]{0:T(128)} %get-tuple-element.58.core, bf16[1024,256]{1,0:T(8,128)(2,1)S(1)} %copy-done.74, s32[1,1024]{1,0:T(1,128)} %sub.79.query_doc, s32[1,1024]{1,0:T(1,128)} %bitcast.461, bf16[2,4,4,256,256]{4,3,2,1,0:T(8,128)(2,1)} %get-tuple-element.63.keyed, ...), custom_call_target="tpu_custom_call" | custom-call | flops 6710886400 | bytes 8388608 | tf_op jit(solution)/shard_map/cond/branch_1_fun/attend_back/pallas_call | solution.py:299
  618.6 7.3 collective-permute-done.7
  630.3 24.0 %collective-permute-done.4 = bf16[4,256,256]{2,1,0:T(8,128)(2,1)S(1)} collective-permute-done((bf16[4,256,256]{2,1,0:T(8,128)(2,1)}, bf16[4,256,256]{2,1,0:T(8,128)(2,1)S(1)}, u32[]{:S(2)}, u32[]{:S(2)}) %collective-permute-start.4) | collective-permute-done | bytes 524320 | tf_op jit(solution)/shard_map/cond/branch_1_fun/ppermute | solution.py:125
  658.8 6.1 convolution_convert_fusion.5
  672.1 11.1 %collective-permute-done.81 = bf16[256,512]{1,0:T(8,128)(2,1)S(1)} collective-permute-done((bf16[256,512]{1,0:T(8,128)(2,1)S(1)}, bf16[256,512]{1,0:T(8,128)(2,1)S(1)}, u32[]{:S(2)}, u32[]{:S(2)}) %collective-permute-start.81) | collective-permute-done | bytes 262176 | tf_op jit(solution)/shard_map/ppermute | solution.py:54
  683.3 11.4 %collective-permute-done.80 = bf16[256,512]{1,0:T(8,128)(2,1)S(1)} collective-permute-done((bf16[256,512]{1,0:T(8,128)(2,1)S(1)}, bf16[256,512]{1,0:T(8,128)(2,1)S(1)}, u32[]{:S(2)}, u32[]{:S(2)}) %collective-permute-start.80) | collective-permute-done | bytes 262176 | tf_op jit(solution)/shard_map/ppermute | solution.py:54
  711.2 12.2 %collective-permute-done.95 = bf16[2,160,1024]{2,1,0:T(8,128)(2,1)S(1)} collective-permute-done((bf16[2,160,1024]{2,1,0:T(8,128)(2,1)S(1)}, bf16[2,160,1024]{2,1,0:T(8,128)(2,1)S(1)}, u32[]{:S(2)}, u32[]{:S(2)}) %collective-permute-start.95) | collective-permute-done | bytes 655392 | tf_op jit(solution)/shard_map/ppermute | solution.py:122
  734.2 24.5 %collective-permute-done.92 = bf16[2,160,1024]{2,1,0:T(8,128)(2,1)S(1)} collective-permute-done((bf16[2,160,1024]{2,1,0:T(8,128)(2,1)S(1)}, bf16[2,160,1024]{2,1,0:T(8,128)(2,1)S(1)}, u32[]{:S(2)}, u32[]{:S(2)}) %collective-permute-start.92) | collective-permute-done | bytes 655392 | tf_op jit(solution)/shard_map/ppermute | solution.py:125
  (784 shorter events, 419.8 us)
Async XLA Ops:
  7.2 121.2 %all-gather.4.cloned.1.call-start = ((), (), s32[]{:S(2)}) async-start(), calls=%async_computation | async-start | bytes 1474560 | tf_op jit(solution)/shard_map/all_gather | solution.py:427
  16.8 37.7 %collective-permute-start.18 = (bf16[256,2304]{1,0:T(8,128)(2,1)}, bf16[256,2304]{1,0:T(8,128)(2,1)S(1)}, u32[]{:S(2)}, u32[]{:S(2)}) collective-permute-start(bf16[256,2304]{1,0:T(8,128)(2,1)} %param.16), channel_id=1, source_target_pairs={{0,16},{8,24},{16,0},{24,8},{1,17},{9,25},{17,1},{25,9},{2,18},{10... | collective-permute-start | bytes 3538952 | tf_op jit(solution)/shard_map/ppermute | solution.py:54
  18.3 76.6 %collective-permute-start.17 = (bf16[256,2304]{1,0:T(8,128)(2,1)}, bf16[256,2304]{1,0:T(8,128)(2,1)}, u32[]{:S(2)}, u32[]{:S(2)}) collective-permute-start(bf16[256,2304]{1,0:T(8,128)(2,1)} %param.16), channel_id=1, source_target_pairs={{0,8},{8,0},{16,24},{24,16},{1,9},{9,1},{17,25},{25,17},{2,10},{10... | collective-permute-start | bytes 3538952 | tf_op jit(solution)/shard_map/ppermute | solution.py:54
  58.4 26.5 %collective-permute-start.28 = (bf16[4,144,256]{2,1,0:T(8,128)(2,1)S(1)}, bf16[4,144,256]{2,1,0:T(8,128)(2,1)S(1)}, u32[]{:S(2)}, u32[]{:S(2)}) collective-permute-start(bf16[4,144,256]{2,1,0:T(8,128)(2,1)S(1)} %maximum_add_fusion.17), channel_id=1, source_target_pairs={{0,6},{2,0},{4,2},{6,4},{1,7},{3,1},{5,3},{7,5},{8,14},{10,8},{12,... | collective-permute-start | bytes 884744 | tf_op jit(solution)/shard_map/ppermute | solution.py:112
  86.9 103.8 %all-gather.6.cloned.1.call-start = ((), (), s32[]{:S(2)}) async-start(), calls=%async_computation.1 | async-start | bytes 5013504 | tf_op jit(solution)/shard_map/all_gather | solution.py:429
  94.0 241.8 %all-gather.8.cloned.1.call-start = ((), (), s32[]{:S(2)}) async-start(), calls=%async_computation.2 | async-start | bytes 11796480 | tf_op jit(solution)/shard_map/all_gather | solution.py:483
  112.8 53.9 %collective-permute-start.34 = (bf16[4,256,256]{2,1,0:T(8,128)(2,1)}, bf16[4,256,256]{2,1,0:T(8,128)(2,1)}, u32[]{:S(2)}, u32[]{:S(2)}) collective-permute-start(bf16[4,256,256]{2,1,0:T(8,128)(2,1)} %bitcast.72), channel_id=1, source_target_pairs={{0,8},{8,0},{16,24},{24,16},{1,9},{9,1},{17,25},{25,17},{2,10},{10... | collective-permute-start | bytes 1572872 | tf_op jit(solution)/shard_map/ppermute | solution.py:54
  112.9 51.1 %collective-permute-start.33 = (bf16[4,256,256]{2,1,0:T(8,128)(2,1)}, bf16[4,256,256]{2,1,0:T(8,128)(2,1)}, u32[]{:S(2)}, u32[]{:S(2)}) collective-permute-start(bf16[4,256,256]{2,1,0:T(8,128)(2,1)} %bitcast.72), channel_id=1, source_target_pairs={{0,4},{6,2},{1,5},{7,3},{8,12},{14,10},{9,13},{15,11},{16,20},{22,... | collective-permute-start | bytes 1572872 | tf_op jit(solution)/shard_map/ppermute | solution.py:100
  117.1 46.9 %collective-permute-start.32 = (bf16[4,256,256]{2,1,0:T(8,128)(2,1)}, bf16[4,256,256]{2,1,0:T(8,128)(2,1)}, u32[]{:S(2)}, u32[]{:S(2)}) collective-permute-start(bf16[4,256,256]{2,1,0:T(8,128)(2,1)} %bitcast.72), channel_id=1, source_target_pairs={{0,6},{6,0},{1,7},{7,1},{8,14},{14,8},{9,15},{15,9},{16,22},{22,16... | collective-permute-start | bytes 1572872 | tf_op jit(solution)/shard_map/ppermute | solution.py:100
  123.3 38.5 %collective-permute-start.31 = (bf16[4,256,256]{2,1,0:T(8,128)(2,1)}, bf16[4,256,256]{2,1,0:T(8,128)(2,1)}, u32[]{:S(2)}, u32[]{:S(2)}) collective-permute-start(bf16[4,256,256]{2,1,0:T(8,128)(2,1)} %collective-permute-done.30), channel_id=1, source_target_pairs={{2,0},{4,6},{3,1},{5,7},{10,8},{12,14},{11,9},{13,15},{18,16},{20,... | collective-permute-start | bytes 1572872 | tf_op jit(solution)/shard_map/ppermute | solution.py:101
  126.5 42.1 %collective-permute-start.35 = (bf16[4,256,256]{2,1,0:T(8,128)(2,1)}, bf16[4,256,256]{2,1,0:T(8,128)(2,1)}, u32[]{:S(2)}, u32[]{:S(2)}) collective-permute-start(bf16[4,256,256]{2,1,0:T(8,128)(2,1)} %collective-permute-done.29), channel_id=1, source_target_pairs={{0,8},{8,0},{16,24},{24,16},{1,9},{9,1},{17,25},{25,17},{2,10},{10... | collective-permute-start | bytes 1572872 | tf_op jit(solution)/shard_map/ppermute | solution.py:54
  202.4 566.6 %all-reduce.5.cloned.1.call-start = ((), (), s32[]{:S(2)}) async-start(), calls=%async_computation.3 | async-start | bytes 15925248 | tf_op jit(solution)/shard_map/psum | solution.py:580
  236.7 28.2 %collective-permute-start.57 = (bf16[128,2304]{1,0:T(8,128)(2,1)S(1)}, bf16[128,2304]{1,0:T(8,128)(2,1)S(1)}, u32[]{:S(2)}, u32[]{:S(2)}) collective-permute-start(bf16[128,2304]{1,0:T(8,128)(2,1)S(1)} %collective-permute-done.43), channel_id=1, source_target_pairs={{0,1},{1,0},{2,3},{3,2},{4,5},{5,4},{6,7},{7,6},{8,9},{9,8},{10,11... | collective-permute-start | bytes 1769480 | tf_op jit(solution)/shard_map/ppermute | solution.py:54
  297.3 29.0 %collective-permute-start.53 = (bf16[128,2304]{1,0:T(8,128)(2,1)S(1)}, bf16[128,2304]{1,0:T(8,128)(2,1)S(1)}, u32[]{:S(2)}, u32[]{:S(2)}) collective-permute-start(bf16[128,2304]{1,0:T(8,128)(2,1)S(1)} %fusion.117), channel_id=1, source_target_pairs={{0,2},{6,4},{1,3},{7,5},{8,10},{14,12},{9,11},{15,13},{16,18},{22,... | collective-permute-start | bytes 1769480 | tf_op jit(solution)/shard_map/ppermute | solution.py:532
  305.3 27.3 %collective-permute-start.58 = (bf16[128,2304]{1,0:T(8,128)(2,1)S(1)}, bf16[128,2304]{1,0:T(8,128)(2,1)S(1)}, u32[]{:S(2)}, u32[]{:S(2)}) collective-permute-start(bf16[128,2304]{1,0:T(8,128)(2,1)S(1)} %fusion.140), channel_id=1, source_target_pairs={{0,1},{1,0},{2,3},{3,2},{4,5},{5,4},{6,7},{7,6},{8,9},{9,8},{10,11... | collective-permute-start | bytes 1769480 | tf_op jit(solution)/shard_map/ppermute | solution.py:54
  320.9 25.7 %collective-permute-start.56 = (bf16[128,2304]{1,0:T(8,128)(2,1)}, bf16[128,2304]{1,0:T(8,128)(2,1)}, u32[]{:S(2)}, u32[]{:S(2)}) collective-permute-start(bf16[128,2304]{1,0:T(8,128)(2,1)} %fusion.116), channel_id=1, source_target_pairs={{2,6},{4,0},{3,7},{5,1},{10,14},{12,8},{11,15},{13,9},{18,22},{20,... | collective-permute-start | bytes 1769480 | tf_op jit(solution)/shard_map/ppermute | solution.py:535
  449.1 27.7 %collective-permute-start.76 = (bf16[128,2304]{1,0:T(8,128)(2,1)S(1)}, bf16[128,2304]{1,0:T(8,128)(2,1)S(1)}, u32[]{:S(2)}, u32[]{:S(2)}) collective-permute-start(bf16[128,2304]{1,0:T(8,128)(2,1)S(1)} %fusion.142), channel_id=1, source_target_pairs={{0,1},{1,0},{2,3},{3,2},{4,5},{5,4},{6,7},{7,6},{8,9},{9,8},{10,11... | collective-permute-start | bytes 1769480 | tf_op jit(solution)/shard_map/ppermute | solution.py:54
  514.5 27.8 %collective-permute-start.98 = (bf16[1152,1152]{1,0:T(8,128)(2,1)}, bf16[1152,1152]{1,0:T(8,128)(2,1)}, u32[]{:S(2)}, u32[]{:S(2)}) collective-permute-start(bf16[1152,1152]{1,0:T(8,128)(2,1)} %constant_dynamic-slice_fusion.6), channel_id=1, source_target_pairs={{0,8},{8,0},{16,24},{24,16},{1,9},{9,1},{17,25},{25,17},{2,10},{10... | collective-permute-start | bytes 7962632 | tf_op jit(solution)/shard_map/ppermute | solution.py:54
  615.1 39.2 %collective-permute-start.6 = (bf16[4,256,256]{2,1,0:T(8,128)(2,1)}, bf16[4,256,256]{2,1,0:T(8,128)(2,1)S(1)}, u32[]{:S(2)}, u32[]{:S(2)}) collective-permute-start(bf16[4,256,256]{2,1,0:T(8,128)(2,1)} %get-tuple-element.249), channel_id=1, source_target_pairs={{2,6},{4,0},{3,7},{5,1},{10,14},{12,8},{11,15},{13,9},{18,22},{20,... | collective-permute-start | bytes 1572872 | tf_op jit(solution)/shard_map/cond/branch_1_fun/ppermute | solution.py:124
  616.6 37.7 %collective-permute-start.5 = (bf16[4,256,256]{2,1,0:T(8,128)(2,1)}, bf16[4,256,256]{2,1,0:T(8,128)(2,1)S(1)}, u32[]{:S(2)}, u32[]{:S(2)}) collective-permute-start(bf16[4,256,256]{2,1,0:T(8,128)(2,1)} %get-tuple-element.249), channel_id=1, source_target_pairs={{0,6},{6,0},{1,7},{7,1},{8,14},{14,8},{9,15},{15,9},{16,22},{22,16... | collective-permute-start | bytes 1572872 | tf_op jit(solution)/shard_map/cond/branch_1_fun/ppermute | solution.py:123
  618.5 35.8 %collective-permute-start.4 = (bf16[4,256,256]{2,1,0:T(8,128)(2,1)}, bf16[4,256,256]{2,1,0:T(8,128)(2,1)S(1)}, u32[]{:S(2)}, u32[]{:S(2)}) collective-permute-start(bf16[4,256,256]{2,1,0:T(8,128)(2,1)} %get-tuple-element.247), channel_id=1, source_target_pairs={{0,2},{2,0},{4,6},{6,4},{1,3},{3,1},{5,7},{7,5},{8,10},{10,8},{12,... | collective-permute-start | bytes 1572872 | tf_op jit(solution)/shard_map/cond/branch_1_fun/ppermute | solution.py:125
  626.0 28.3 %collective-permute-start.8 = (bf16[4,256,256]{2,1,0:T(8,128)(2,1)S(1)}, bf16[4,256,256]{2,1,0:T(8,128)(2,1)S(1)}, u32[]{:S(2)}, u32[]{:S(2)}) collective-permute-start(bf16[4,256,256]{2,1,0:T(8,128)(2,1)S(1)} %add_convert_fusion), channel_id=1, source_target_pairs={{2,4},{4,2},{3,5},{5,3},{10,12},{12,10},{11,13},{13,11},{18,20},{2... | collective-permute-start | bytes 1572872 | tf_op jit(solution)/shard_map/cond/branch_1_fun/ppermute | solution.py:127
  665.6 64.5 %collective-permute-start.85 = (bf16[4,144,512]{2,1,0:T(8,128)(2,1)S(1)}, bf16[4,144,512]{2,1,0:T(8,128)(2,1)S(1)}, u32[]{:S(2)}, u32[]{:S(2)}) collective-permute-start(bf16[4,144,512]{2,1,0:T(8,128)(2,1)S(1)} %get-tuple-element.268), channel_id=1, source_target_pairs={{2,6},{4,0},{3,7},{5,1},{10,14},{12,8},{11,15},{13,9},{18,22},{20,... | collective-permute-start | bytes 1769480 | tf_op jit(solution)/shard_map/ppermute | solution.py:124
  667.1 34.0 %collective-permute-start.84 = (bf16[4,144,512]{2,1,0:T(8,128)(2,1)S(1)}, bf16[4,144,512]{2,1,0:T(8,128)(2,1)S(1)}, u32[]{:S(2)}, u32[]{:S(2)}) collective-permute-start(bf16[4,144,512]{2,1,0:T(8,128)(2,1)S(1)} %get-tuple-element.268), channel_id=1, source_target_pairs={{0,6},{6,0},{1,7},{7,1},{8,14},{14,8},{9,15},{15,9},{16,22},{22,16... | collective-permute-start | bytes 1769480 | tf_op jit(solution)/shard_map/ppermute | solution.py:123
  683.3 41.1 %collective-permute-start.83 = (bf16[4,144,512]{2,1,0:T(8,128)(2,1)S(1)}, bf16[4,144,512]{2,1,0:T(8,128)(2,1)S(1)}, u32[]{:S(2)}, u32[]{:S(2)}) collective-permute-start(bf16[4,144,512]{2,1,0:T(8,128)(2,1)S(1)} %get-tuple-element.266), channel_id=1, source_target_pairs={{0,2},{2,0},{4,6},{6,4},{1,3},{3,1},{5,7},{7,5},{8,10},{10,8},{12,... | collective-permute-start | bytes 1769480 | tf_op jit(solution)/shard_map/ppermute | solution.py:125
  696.0 27.4 %collective-permute-start.95 = (bf16[2,160,1024]{2,1,0:T(8,128)(2,1)S(1)}, bf16[2,160,1024]{2,1,0:T(8,128)(2,1)S(1)}, u32[]{:S(2)}, u32[]{:S(2)}) collective-permute-start(bf16[2,160,1024]{2,1,0:T(8,128)(2,1)S(1)} %get-tuple-element.264), channel_id=1, source_target_pairs={{0,2},{6,4},{1,3},{7,5},{8,10},{14,12},{9,11},{15,13},{16,18},{22,... | collective-permute-start | bytes 1966088 | tf_op jit(solution)/shard_map/ppermute | solution.py:122
  701.1 30.7 %collective-permute-start.82 = (bf16[128,2304]{1,0:T(8,128)(2,1)S(1)}, bf16[128,2304]{1,0:T(8,128)(2,1)S(1)}, u32[]{:S(2)}, u32[]{:S(2)}) collective-permute-start(bf16[128,2304]{1,0:T(8,128)(2,1)S(1)} %dynamic-slice_convert_fusion), channel_id=1, source_target_pairs={{0,1},{1,0},{2,3},{3,2},{4,5},{5,4},{6,7},{7,6},{8,9},{9,8},{10,11... | collective-permute-start | bytes 1769480 | tf_op jit(solution)/shard_map/ppermute | solution.py:54
  709.8 50.0 %collective-permute-start.94 = (bf16[2,160,1024]{2,1,0:T(8,128)(2,1)S(1)}, bf16[2,160,1024]{2,1,0:T(8,128)(2,1)S(1)}, u32[]{:S(2)}, u32[]{:S(2)}) collective-permute-start(bf16[2,160,1024]{2,1,0:T(8,128)(2,1)S(1)} %get-tuple-element.265), channel_id=1, source_target_pairs={{2,6},{4,0},{3,7},{5,1},{10,14},{12,8},{11,15},{13,9},{18,22},{20,... | collective-permute-start | bytes 1966088 | tf_op jit(solution)/shard_map/ppermute | solution.py:124
  724.4 35.4 %collective-permute-start.93 = (bf16[2,160,1024]{2,1,0:T(8,128)(2,1)S(1)}, bf16[2,160,1024]{2,1,0:T(8,128)(2,1)S(1)}, u32[]{:S(2)}, u32[]{:S(2)}) collective-permute-start(bf16[2,160,1024]{2,1,0:T(8,128)(2,1)S(1)} %get-tuple-element.265), channel_id=1, source_target_pairs={{0,6},{6,0},{1,7},{7,1},{8,14},{14,8},{9,15},{15,9},{16,22},{22,16... | collective-permute-start | bytes 1966088 | tf_op jit(solution)/shard_map/ppermute | solution.py:123
  730.1 28.5 %collective-permute-start.92 = (bf16[2,160,1024]{2,1,0:T(8,128)(2,1)S(1)}, bf16[2,160,1024]{2,1,0:T(8,128)(2,1)S(1)}, u32[]{:S(2)}, u32[]{:S(2)}) collective-permute-start(bf16[2,160,1024]{2,1,0:T(8,128)(2,1)S(1)} %get-tuple-element.263), channel_id=1, source_target_pairs={{0,2},{2,0},{4,6},{6,4},{1,3},{3,1},{5,7},{7,5},{8,10},{10,8},{12,... | collective-permute-start | bytes 1966088 | tf_op jit(solution)/shard_map/ppermute | solution.py:125
  731.8 28.0 %collective-permute-start.96 = (bf16[2,160,1024]{2,1,0:T(8,128)(2,1)S(1)}, bf16[2,160,1024]{2,1,0:T(8,128)(2,1)S(1)}, u32[]{:S(2)}, u32[]{:S(2)}) collective-permute-start(bf16[2,160,1024]{2,1,0:T(8,128)(2,1)S(1)} %add_convert_fusion.6), channel_id=1, source_target_pairs={{2,4},{4,2},{3,5},{5,3},{10,12},{12,10},{11,13},{13,11},{18,20},{2... | collective-permute-start | bytes 1966088 | tf_op jit(solution)/shard_map/ppermute | solution.py:127
  734.1 28.0 %collective-permute-start.90 = (bf16[144,512]{1,0:T(8,128)(2,1)S(1)}, bf16[144,512]{1,0:T(8,128)(2,1)S(1)}, u32[]{:S(2)}, u32[]{:S(2)}) collective-permute-start(bf16[144,512]{1,0:T(8,128)(2,1)S(1)} %get-tuple-element.298), channel_id=1, source_target_pairs={{0,24},{8,16},{16,8},{24,0},{1,25},{9,17},{17,9},{25,1},{2,26},{10... | collective-permute-start | bytes 442376 | tf_op jit(solution)/shard_map/ppermute | solution.py:54
  (225 other events, 2298.3 us)
Sparse Core Ops, SparseCore 0:
  87.0 30.0 all-gather.3
  120.0 69.7 all-gather.5
  202.5 62.2 all-gather.7
  555.4 208.1 all-reduce.4

commit v3 on v2

--- a/solution.py
+++ b/solution.py
@@ -576,12 +576,9 @@
         kept = lax.dynamic_slice_in_dim(grad, core * half, half, 0)
         return (kept.astype(wide) + other_core(sent).astype(wide)).astype(low)
 
-    def over_x(mine):
-        return lax.psum(mine, "seq", axis_index_groups=[[0, 2], [1, 3]])
-
-    def both_halves(mine, *hold):
-        mine = after(mine, *hold)
-        return join_halves(core_array, mine, other_core(mine))
+    def over_x(mine, sides=((0, 2), (1, 3))):
+        return lax.psum(mine, "seq", axis_index_groups=[list(side) for side in sides])
+
 
     backward_kept, grad_ffn_in = through(grad_ffn_out.astype(low), backward)
 
@@ -597,7 +594,7 @@
     down_mine = core_half(rows_product(hidden_all, [k[0] for k in backward_kept], branch_other))
     gate_mine = core_half(rows_product(rows_all, [k[1] for k in backward_kept], grad_branch))
     up_mine = core_half(rows_product(rows_all, [k[2] for k in backward_kept], branch_other))
-    down_sum, gate_sum, up_sum = over_x((down_mine, gate_mine, up_mine))
+    down_sum, gate_sum = over_x((down_mine, gate_mine))
 
     always = positions[0] >= 0
 
@@ -662,13 +659,18 @@
         [lax.dynamic_index_in_dim(weight_grad, at, 1, False) for at in places]
     )
 
+    up_sum = over_x(after(up_mine, weight_started[:2][-1]), ((1, 3), (0, 2)))
+    grad_gate_w, grad_down_w = [
+        join_halves(core_array, mine, other_core(mine)) for mine in (gate_sum, down_sum)
+    ]
+
     raw_mine = swap_seq(grad_raw.reshape(blocks, rows, 2 * HEAD), seq_place)
     back = sum(dot(part, both_all[i], 1, 1) for i, part in enumerate(raw_mine))
     back_got = other_y(
         lax.dynamic_slice_in_dim(back, (1 - tensor_place) * half_rows, half_rows, 0).astype(low)
     )
     back = lax.dynamic_slice_in_dim(back, tensor_place * half_rows, half_rows, 0)
-    back = back + back_got.astype(wide)
+    back = after(back, grad_gate_w, grad_down_w) + back_got.astype(wide)
     grad_input = grad_middle + normalize_back(inputs_half, back * gain_one)[0]
 
     out_parts = after(out_sum, weight_grad)
@@ -701,9 +703,9 @@
         out_sum[:share].T,
         gain_sums[0],
         gain_sums[1],
-        both_halves(gate_sum, weight_started[:3][-1]),
-        both_halves(up_sum, weight_started[:3][-1]),
-        both_halves(down_sum, weight_started[:3][-1]),
+        grad_gate_w,
+        join_halves(core_array, up_sum, other_core(up_sum)),
+        grad_down_w,
         gain_sums[2],
     )
 

time: 823 us -> 945 us (1.15)
  waiting for transfers between devices: 339 us -> 436 us
  matrix products: 103 us -> 113 us
    psum x1 -> x2, waiting for transfers between devices: 0.01 us -> 132 us  [over_x(): lax.psum(mine, 'seq', axis_index_groups=[list(side) for side in sides])]
    ppermute x3, waiting for transfers between devices: 25.2 us -> 8.52 us  [scatter_start(): near_in = lax.ppermute(near, 'fsdp', INWARD)]
    ppermute x58, waiting for transfers between devices: 135 us -> 119 us  [flip(): lax.ppermute(x, axis, [(i, i ^ mask) for i in range(lax.axis_size(axis))])]
    dot_general x38, matrix products: 103 us -> 113 us  [dot(): lax.dot_general(left, right, (((left_dim,), (right_dim,)), ((), ())), pre...]
    slice x29 -> x31, local copies, waits for them, and re-layouts: 17 us -> 20 us  [after(): other[(0,) * other.ndim].astype(wide) * 0.0]
    unnamed x286 -> x254, local copies, waits for them, and re-layouts: 21.3 us -> 22.7 us
  transfers between devices with their start and end apart: 108 -> 109, of which waited for: 42 -> 40; matrix products, arithmetic and copies ran while one was open for 28% -> 24% of each run, Pallas kernels for 4% -> 2%
where the time goes in v3:
time: 945 us; the launch traced here: 935 us
  waiting for transfers between devices  436 us (46%)
  starting transfers between devices  138 us (15%)
  matrix products  113 us (12%)
  local copies, waits for them, and re-layouts  85 us (9%)
  other arithmetic  84.3 us (9%)
  Pallas kernels  37.7 us (4%)
  between operations  37.3 us (4%)
    psum x2, waiting for transfers between devices, over_x(): lax.psum(mine, 'seq', axis_index_groups=[list(side) for side in sides])  132 us
    ppermute x58, waiting for transfers between devices, flip(): lax.ppermute(x, axis, [(i, i ^ mask) for i in range(lax.axis_size(axis))])  119 us
    dot_general x38, matrix products, dot(): lax.dot_general(left, right, (((left_dim,), (right_dim,)), ((), ())), pre...  113 us
    ppermute x3, waiting for transfers between devices, scatter_start(): pair_in = lax.ppermute(pair, 'fsdp', PAIR)  45.3 us
    ppermute x58, starting transfers between devices, flip(): lax.ppermute(x, axis, [(i, i ^ mask) for i in range(lax.axis_size(axis))])  45 us
    ppermute x1, waiting for transfers between devices, gather_slots(): return [piece, pair, near + lax.ppermute(near, 'fsdp', OUTWARD), far]  26.1 us
    ppermute x6, waiting for transfers between devices, gather_places(): got.append((lax.ppermute(piece, 'fsdp', pairs), (place - by) % count))  24.5 us
    unnamed x254, local copies, waits for them, and re-layouts  22.7 us
  transfers between devices with their start and end apart: 109, of which 40 were waited for; matrix products, arithmetic and copies ran while one was open for 24% of the time, Pallas kernels for 2%

profile of v3, /device:TPU:0, one launch (start us, length us, event | category | flops | bytes accessed | tf_op | source)
XLA Modules:
  0.0 935.3 jit_solution(12540547920101288992)
XLA Ops:
  23.7 19.7 %collective-permute-done.16 = f32[4,8,128]{2,1,0:T(8,128)S(1)} collective-permute-done((f32[4,8,128]{2,1,0:T(8,128)S(1)}, f32[4,8,128]{2,1,0:T(8,128)S(1)}, u32[]{:S(2)}, u32[]{:S(2)}) %collective-permute-start.16) | collective-permute-done | bytes 16416 | tf_op jit(solution)/shard_map/ppermute | solution.py:54
  60.3 7.3 collective-permute-done.26
  67.7 17.2 %collective-permute-done.27 = bf16[4,144,256]{2,1,0:T(8,128)(2,1)S(1)} collective-permute-done((bf16[4,144,256]{2,1,0:T(8,128)(2,1)S(1)}, bf16[4,144,256]{2,1,0:T(8,128)(2,1)S(1)}, u32[]{:S(2)}, u32[]{:S(2)}) %collective-permute-start.27) | collective-permute-done | bytes 294944 | tf_op jit(solution)/shard_map/ppermute | solution.py:112
  135.8 26.1 %collective-permute-done.31 = bf16[4,256,256]{2,1,0:T(8,128)(2,1)} collective-permute-done((bf16[4,256,256]{2,1,0:T(8,128)(2,1)}, bf16[4,256,256]{2,1,0:T(8,128)(2,1)}, u32[]{:S(2)}, u32[]{:S(2)}) %collective-permute-start.31) | collective-permute-done | bytes 524320 | tf_op jit(solution)/shard_map/ppermute | solution.py:101
  172.1 7.5 attend.1
  202.1 8.8 collective-permute-done.41
  223.2 10.4 %collective-permute-done.43 = bf16[128,2304]{1,0:T(8,128)(2,1)S(1)} collective-permute-done((bf16[128,2304]{1,0:T(8,128)(2,1)S(1)}, bf16[128,2304]{1,0:T(8,128)(2,1)S(1)}, u32[]{:S(2)}, u32[]{:S(2)}) %collective-permute-start.43) | collective-permute-done | bytes 589856 | tf_op jit(solution)/shard_map/ppermute | solution.py:505
  254.8 10.0 %collective-permute-start.46 = (bf16[128,2304]{1,0:T(8,128)(2,1)S(1)}, bf16[128,2304]{1,0:T(8,128)(2,1)S(1)}, u32[]{:S(2)}, u32[]{:S(2)}) collective-permute-start(bf16[128,2304]{1,0:T(8,128)(2,1)S(1)} %collective-permute-done.45), channel_id=1, source_target_pairs={{2,0},{4,6},{3,1},{5,7},{10,8},{12,14},{11,9},{13,15},{18,16},{20,... | collective-permute-start | bytes 1769480 | tf_op jit(solution)/shard_map/ppermute | solution.py:514
  282.4 5.9 collective-permute-done.47
  306.3 14.1 %collective-permute-done.50 = bf16[128,2304]{1,0:T(8,128)(2,1)S(1)} collective-permute-done((bf16[128,2304]{1,0:T(8,128)(2,1)S(1)}, bf16[128,2304]{1,0:T(8,128)(2,1)S(1)}, u32[]{:S(2)}, u32[]{:S(2)}) %collective-permute-start.50) | collective-permute-done | bytes 589856 | tf_op jit(solution)/shard_map/ppermute | solution.py:54
  338.0 9.0 collective-permute-done.56
  347.1 9.4 %collective-permute-done.59 = bf16[128,2304]{1,0:T(8,128)(2,1)} collective-permute-done((bf16[128,2304]{1,0:T(8,128)(2,1)}, bf16[128,2304]{1,0:T(8,128)(2,1)}, u32[]{:S(2)}, u32[]{:S(2)}) %collective-permute-start.59) | collective-permute-done | bytes 589856 | tf_op jit(solution)/shard_map/ppermute | solution.py:539
  366.6 11.3 %collective-permute-done.61 = bf16[128,2304]{1,0:T(8,128)(2,1)S(1)} collective-permute-done((bf16[128,2304]{1,0:T(8,128)(2,1)S(1)}, bf16[128,2304]{1,0:T(8,128)(2,1)S(1)}, u32[]{:S(2)}, u32[]{:S(2)}) %collective-permute-start.61) | collective-permute-done | bytes 589856 | tf_op jit(solution)/shard_map/ppermute | solution.py:505
  387.9 10.6 %collective-permute-done.66 = bf16[128,2304]{1,0:T(8,128)(2,1)S(1)} collective-permute-done((bf16[128,2304]{1,0:T(8,128)(2,1)S(1)}, bf16[128,2304]{1,0:T(8,128)(2,1)S(1)}, u32[]{:S(2)}, u32[]{:S(2)}) %collective-permute-start.66) | collective-permute-done | bytes 589856 | tf_op jit(solution)/shard_map/ppermute | solution.py:510
  410.6 10.6 %collective-permute-done.64 = bf16[128,2304]{1,0:T(8,128)(2,1)S(1)} collective-permute-done((bf16[128,2304]{1,0:T(8,128)(2,1)S(1)}, bf16[128,2304]{1,0:T(8,128)(2,1)S(1)}, u32[]{:S(2)}, u32[]{:S(2)}) %collective-permute-start.64) | collective-permute-done | bytes 589856 | tf_op jit(solution)/shard_map/ppermute | solution.py:514
  452.7 14.1 %collective-permute-done.68 = bf16[128,2304]{1,0:T(8,128)(2,1)S(1)} collective-permute-done((bf16[128,2304]{1,0:T(8,128)(2,1)S(1)}, bf16[128,2304]{1,0:T(8,128)(2,1)S(1)}, u32[]{:S(2)}, u32[]{:S(2)}) %collective-permute-start.68) | collective-permute-done | bytes 589856 | tf_op jit(solution)/shard_map/ppermute | solution.py:54
  488.8 5.6 collective-permute-done.74
  494.4 10.2 %collective-permute-done.77 = bf16[128,2304]{1,0:T(8,128)(2,1)} collective-permute-done((bf16[128,2304]{1,0:T(8,128)(2,1)}, bf16[128,2304]{1,0:T(8,128)(2,1)}, u32[]{:S(2)}, u32[]{:S(2)}) %collective-permute-start.77) | collective-permute-done | bytes 589856 | tf_op jit(solution)/shard_map/ppermute | solution.py:539
  511.9 8.8 convolution_convert_fusion.4
  526.4 6.7 convolution_convert_fusion.2
  536.4 97.4 %conditional.1 = (bf16[1024,512]{1,0:T(8,128)(2,1)}, bf16[4,256,512]{2,1,0:T(8,128)(2,1)}, bf16[4,2,160,1024]{3,2,1,0:T(8,128)(2,1)S(1)}) conditional(s32[]{:T(128)} %bitcast.108, () %tuple.18, (s32[4,256]{1,0:T(4,128)S(1)}, s32[4,256]{1,0:T(4,128)S(1)}, s32[4,1,256]{2,1,0:T(1,128)S(1)}, s32[4,4,256]{2,1,0:T(4,128)S(1)}, ...), branch_computations={%region_14.15_spmd, %region_15.17_spmd} | conditional | flops 9181550592 | bytes 198138048 | solution.py:603
  557.8 15.7 %attend_back.1 = (f32[1024,256]{1,0:T(8,128)}, bf16[2,4,4,256,256]{4,3,2,1,0:T(8,128)(2,1)}) custom-call(s32[1]{0:T(128)} %get-tuple-element.58.core, bf16[1024,256]{1,0:T(8,128)(2,1)S(1)} %copy-done.67, s32[1,1024]{1,0:T(1,128)} %sub.79.query_doc, s32[1,1024]{1,0:T(1,128)} %bitcast.460, bf16[2,4,4,256,256]{4,3,2,1,0:T(8,128)(2,1)} %get-tuple-element.63.keyed, ...), custom_call_target="tpu_custom_call" | custom-call | flops 6710886400 | bytes 8388608 | tf_op jit(solution)/shard_map/cond/branch_1_fun/attend_back/pallas_call | solution.py:299
  593.5 7.3 collective-permute-done.7
  605.2 24.2 %collective-permute-done.4 = bf16[4,256,256]{2,1,0:T(8,128)(2,1)S(1)} collective-permute-done((bf16[4,256,256]{2,1,0:T(8,128)(2,1)}, bf16[4,256,256]{2,1,0:T(8,128)(2,1)S(1)}, u32[]{:S(2)}, u32[]{:S(2)}) %collective-permute-start.4) | collective-permute-done | bytes 524320 | tf_op jit(solution)/shard_map/cond/branch_1_fun/ppermute | solution.py:125
  638.0 5.4 convolution_convert_fusion.5
  646.6 7.9 convolution_convert_fusion.3
  683.8 11.3 %collective-permute-done.81 = bf16[256,512]{1,0:T(8,128)(2,1)S(1)} collective-permute-done((bf16[256,512]{1,0:T(8,128)(2,1)S(1)}, bf16[256,512]{1,0:T(8,128)(2,1)S(1)}, u32[]{:S(2)}, u32[]{:S(2)}) %collective-permute-start.81) | collective-permute-done | bytes 262176 | tf_op jit(solution)/shard_map/ppermute | solution.py:54
  696.6 8.0 collective-permute-done.80
  714.9 5.7 collective-permute-start.97
  722.9 6.4 collective-permute-start.96
  736.6 18.3 %collective-permute-done.96 = bf16[2,160,1024]{2,1,0:T(8,128)(2,1)S(1)} collective-permute-done((bf16[2,160,1024]{2,1,0:T(8,128)(2,1)S(1)}, bf16[2,160,1024]{2,1,0:T(8,128)(2,1)S(1)}, u32[]{:S(2)}, u32[]{:S(2)}) %collective-permute-start.96) | collective-permute-done | bytes 655392 | tf_op jit(solution)/shard_map/ppermute | solution.py:125
  763.7 131.9 %all-reduce.8.cloned.1.call-done = (bf16[1152,1152]{1,0:T(8,128)(2,1)}, bf16[576,2304]{1,0:T(8,128)(2,1)}) async-done(((bf16[1152,1152]{1,0:T(8,128)(2,1)}, bf16[576,2304]{1,0:T(8,128)(2,1)}), (bf16[1152,1152]{1,0:T(8,128)(2,1)}, bf16[576,2304]{1,0:T(8,128)(2,1)})) %all-reduce.8.cloned.1.call-update) | async-done | bytes 5308432 | tf_op jit(solution)/shard_map/psum | solution.py:580
  (753 shorter events, 429.1 us)
Async XLA Ops:
  7.2 121.2 %all-gather.4.cloned.1.call-start = ((), (), s32[]{:S(2)}) async-start(), calls=%async_computation | async-start | bytes 1474560 | tf_op jit(solution)/shard_map/all_gather | solution.py:427
  16.8 37.7 %collective-permute-start.18 = (bf16[256,2304]{1,0:T(8,128)(2,1)}, bf16[256,2304]{1,0:T(8,128)(2,1)S(1)}, u32[]{:S(2)}, u32[]{:S(2)}) collective-permute-start(bf16[256,2304]{1,0:T(8,128)(2,1)} %param.16), channel_id=1, source_target_pairs={{0,16},{8,24},{16,0},{24,8},{1,17},{9,25},{17,1},{25,9},{2,18},{10... | collective-permute-start | bytes 3538952 | tf_op jit(solution)/shard_map/ppermute | solution.py:54
  18.3 76.6 %collective-permute-start.17 = (bf16[256,2304]{1,0:T(8,128)(2,1)}, bf16[256,2304]{1,0:T(8,128)(2,1)}, u32[]{:S(2)}, u32[]{:S(2)}) collective-permute-start(bf16[256,2304]{1,0:T(8,128)(2,1)} %param.16), channel_id=1, source_target_pairs={{0,8},{8,0},{16,24},{24,16},{1,9},{9,1},{17,25},{25,17},{2,10},{10... | collective-permute-start | bytes 3538952 | tf_op jit(solution)/shard_map/ppermute | solution.py:54
  58.4 26.5 %collective-permute-start.28 = (bf16[4,144,256]{2,1,0:T(8,128)(2,1)S(1)}, bf16[4,144,256]{2,1,0:T(8,128)(2,1)S(1)}, u32[]{:S(2)}, u32[]{:S(2)}) collective-permute-start(bf16[4,144,256]{2,1,0:T(8,128)(2,1)S(1)} %maximum_add_fusion.17), channel_id=1, source_target_pairs={{0,6},{2,0},{4,2},{6,4},{1,7},{3,1},{5,3},{7,5},{8,14},{10,8},{12,... | collective-permute-start | bytes 884744 | tf_op jit(solution)/shard_map/ppermute | solution.py:112
  86.9 103.6 %all-gather.6.cloned.1.call-start = ((), (), s32[]{:S(2)}) async-start(), calls=%async_computation.1 | async-start | bytes 5013504 | tf_op jit(solution)/shard_map/all_gather | solution.py:429
  94.0 242.2 %all-gather.8.cloned.1.call-start = ((), (), s32[]{:S(2)}) async-start(), calls=%async_computation.2 | async-start | bytes 11796480 | tf_op jit(solution)/shard_map/all_gather | solution.py:483
  112.8 53.9 %collective-permute-start.34 = (bf16[4,256,256]{2,1,0:T(8,128)(2,1)}, bf16[4,256,256]{2,1,0:T(8,128)(2,1)}, u32[]{:S(2)}, u32[]{:S(2)}) collective-permute-start(bf16[4,256,256]{2,1,0:T(8,128)(2,1)} %bitcast.72), channel_id=1, source_target_pairs={{0,8},{8,0},{16,24},{24,16},{1,9},{9,1},{17,25},{25,17},{2,10},{10... | collective-permute-start | bytes 1572872 | tf_op jit(solution)/shard_map/ppermute | solution.py:54
  112.8 51.1 %collective-permute-start.33 = (bf16[4,256,256]{2,1,0:T(8,128)(2,1)}, bf16[4,256,256]{2,1,0:T(8,128)(2,1)}, u32[]{:S(2)}, u32[]{:S(2)}) collective-permute-start(bf16[4,256,256]{2,1,0:T(8,128)(2,1)} %bitcast.72), channel_id=1, source_target_pairs={{0,4},{6,2},{1,5},{7,3},{8,12},{14,10},{9,13},{15,11},{16,20},{22,... | collective-permute-start | bytes 1572872 | tf_op jit(solution)/shard_map/ppermute | solution.py:100
  117.1 46.9 %collective-permute-start.32 = (bf16[4,256,256]{2,1,0:T(8,128)(2,1)}, bf16[4,256,256]{2,1,0:T(8,128)(2,1)}, u32[]{:S(2)}, u32[]{:S(2)}) collective-permute-start(bf16[4,256,256]{2,1,0:T(8,128)(2,1)} %bitcast.72), channel_id=1, source_target_pairs={{0,6},{6,0},{1,7},{7,1},{8,14},{14,8},{9,15},{15,9},{16,22},{22,16... | collective-permute-start | bytes 1572872 | tf_op jit(solution)/shard_map/ppermute | solution.py:100
  123.3 38.5 %collective-permute-start.31 = (bf16[4,256,256]{2,1,0:T(8,128)(2,1)}, bf16[4,256,256]{2,1,0:T(8,128)(2,1)}, u32[]{:S(2)}, u32[]{:S(2)}) collective-permute-start(bf16[4,256,256]{2,1,0:T(8,128)(2,1)} %collective-permute-done.30), channel_id=1, source_target_pairs={{2,0},{4,6},{3,1},{5,7},{10,8},{12,14},{11,9},{13,15},{18,16},{20,... | collective-permute-start | bytes 1572872 | tf_op jit(solution)/shard_map/ppermute | solution.py:101
  126.5 42.0 %collective-permute-start.35 = (bf16[4,256,256]{2,1,0:T(8,128)(2,1)}, bf16[4,256,256]{2,1,0:T(8,128)(2,1)}, u32[]{:S(2)}, u32[]{:S(2)}) collective-permute-start(bf16[4,256,256]{2,1,0:T(8,128)(2,1)} %collective-permute-done.29), channel_id=1, source_target_pairs={{0,8},{8,0},{16,24},{24,16},{1,9},{9,1},{17,25},{25,17},{2,10},{10... | collective-permute-start | bytes 1572872 | tf_op jit(solution)/shard_map/ppermute | solution.py:54
  202.1 561.6 %all-reduce.6.cloned.1.call-start = ((), (), s32[]{:S(2)}) async-start(), calls=%async_computation.3 | async-start | bytes 5308416 | tf_op jit(solution)/shard_map/psum | solution.py:580
  236.7 28.2 %collective-permute-start.57 = (bf16[128,2304]{1,0:T(8,128)(2,1)S(1)}, bf16[128,2304]{1,0:T(8,128)(2,1)S(1)}, u32[]{:S(2)}, u32[]{:S(2)}) collective-permute-start(bf16[128,2304]{1,0:T(8,128)(2,1)S(1)} %collective-permute-done.43), channel_id=1, source_target_pairs={{0,1},{1,0},{2,3},{3,2},{4,5},{5,4},{6,7},{7,6},{8,9},{9,8},{10,11... | collective-permute-start | bytes 1769480 | tf_op jit(solution)/shard_map/ppermute | solution.py:54
  297.3 29.3 %collective-permute-start.53 = (bf16[128,2304]{1,0:T(8,128)(2,1)S(1)}, bf16[128,2304]{1,0:T(8,128)(2,1)S(1)}, u32[]{:S(2)}, u32[]{:S(2)}) collective-permute-start(bf16[128,2304]{1,0:T(8,128)(2,1)S(1)} %fusion.118), channel_id=1, source_target_pairs={{0,2},{6,4},{1,3},{7,5},{8,10},{14,12},{9,11},{15,13},{16,18},{22,... | collective-permute-start | bytes 1769480 | tf_op jit(solution)/shard_map/ppermute | solution.py:532
  305.6 27.4 %collective-permute-start.58 = (bf16[128,2304]{1,0:T(8,128)(2,1)S(1)}, bf16[128,2304]{1,0:T(8,128)(2,1)S(1)}, u32[]{:S(2)}, u32[]{:S(2)}) collective-permute-start(bf16[128,2304]{1,0:T(8,128)(2,1)S(1)} %fusion.141), channel_id=1, source_target_pairs={{0,1},{1,0},{2,3},{3,2},{4,5},{5,4},{6,7},{7,6},{8,9},{9,8},{10,11... | collective-permute-start | bytes 1769480 | tf_op jit(solution)/shard_map/ppermute | solution.py:54
  451.7 27.7 %collective-permute-start.76 = (bf16[128,2304]{1,0:T(8,128)(2,1)S(1)}, bf16[128,2304]{1,0:T(8,128)(2,1)S(1)}, u32[]{:S(2)}, u32[]{:S(2)}) collective-permute-start(bf16[128,2304]{1,0:T(8,128)(2,1)S(1)} %fusion.143), channel_id=1, source_target_pairs={{0,1},{1,0},{2,3},{3,2},{4,5},{5,4},{6,7},{7,6},{8,9},{9,8},{10,11... | collective-permute-start | bytes 1769480 | tf_op jit(solution)/shard_map/ppermute | solution.py:54
  467.7 26.8 %collective-permute-start.74 = (bf16[128,2304]{1,0:T(8,128)(2,1)}, bf16[128,2304]{1,0:T(8,128)(2,1)}, u32[]{:S(2)}, u32[]{:S(2)}) collective-permute-start(bf16[128,2304]{1,0:T(8,128)(2,1)} %fusion.110), channel_id=1, source_target_pairs={{2,6},{4,0},{3,7},{5,1},{10,14},{12,8},{11,15},{13,9},{18,22},{20,... | collective-permute-start | bytes 1769480 | tf_op jit(solution)/shard_map/ppermute | solution.py:535
  590.1 39.3 %collective-permute-start.6 = (bf16[4,256,256]{2,1,0:T(8,128)(2,1)}, bf16[4,256,256]{2,1,0:T(8,128)(2,1)S(1)}, u32[]{:S(2)}, u32[]{:S(2)}) collective-permute-start(bf16[4,256,256]{2,1,0:T(8,128)(2,1)} %get-tuple-element.248), channel_id=1, source_target_pairs={{2,6},{4,0},{3,7},{5,1},{10,14},{12,8},{11,15},{13,9},{18,22},{20,... | collective-permute-start | bytes 1572872 | tf_op jit(solution)/shard_map/cond/branch_1_fun/ppermute | solution.py:124
  591.5 37.9 %collective-permute-start.5 = (bf16[4,256,256]{2,1,0:T(8,128)(2,1)}, bf16[4,256,256]{2,1,0:T(8,128)(2,1)S(1)}, u32[]{:S(2)}, u32[]{:S(2)}) collective-permute-start(bf16[4,256,256]{2,1,0:T(8,128)(2,1)} %get-tuple-element.248), channel_id=1, source_target_pairs={{0,6},{6,0},{1,7},{7,1},{8,14},{14,8},{9,15},{15,9},{16,22},{22,16... | collective-permute-start | bytes 1572872 | tf_op jit(solution)/shard_map/cond/branch_1_fun/ppermute | solution.py:123
  593.4 35.9 %collective-permute-start.4 = (bf16[4,256,256]{2,1,0:T(8,128)(2,1)}, bf16[4,256,256]{2,1,0:T(8,128)(2,1)S(1)}, u32[]{:S(2)}, u32[]{:S(2)}) collective-permute-start(bf16[4,256,256]{2,1,0:T(8,128)(2,1)} %get-tuple-element.246), channel_id=1, source_target_pairs={{0,2},{2,0},{4,6},{6,4},{1,3},{3,1},{5,7},{7,5},{8,10},{10,8},{12,... | collective-permute-start | bytes 1572872 | tf_op jit(solution)/shard_map/cond/branch_1_fun/ppermute | solution.py:125
  601.0 28.4 %collective-permute-start.8 = (bf16[4,256,256]{2,1,0:T(8,128)(2,1)S(1)}, bf16[4,256,256]{2,1,0:T(8,128)(2,1)S(1)}, u32[]{:S(2)}, u32[]{:S(2)}) collective-permute-start(bf16[4,256,256]{2,1,0:T(8,128)(2,1)S(1)} %add_convert_fusion), channel_id=1, source_target_pairs={{2,4},{4,2},{3,5},{5,3},{10,12},{12,10},{11,13},{13,11},{18,20},{2... | collective-permute-start | bytes 1572872 | tf_op jit(solution)/shard_map/cond/branch_1_fun/ppermute | solution.py:127
  633.9 28.0 %collective-permute-start.102 = (bf16[1152,1152]{1,0:T(8,128)(2,1)}, bf16[1152,1152]{1,0:T(8,128)(2,1)S(1)}, u32[]{:S(2)}, u32[]{:S(2)}) collective-permute-start(bf16[1152,1152]{1,0:T(8,128)(2,1)} %constant_dynamic-slice_fusion.4), channel_id=1, source_target_pairs={{0,8},{8,0},{16,24},{24,16},{1,9},{9,1},{17,25},{25,17},{2,10},{10... | collective-permute-start | bytes 7962632 | tf_op jit(solution)/shard_map/ppermute | solution.py:54
  637.5 26.9 %collective-permute-start.82 = (bf16[1152,1152]{1,0:T(8,128)(2,1)}, bf16[1152,1152]{1,0:T(8,128)(2,1)}, u32[]{:S(2)}, u32[]{:S(2)}) collective-permute-start(bf16[1152,1152]{1,0:T(8,128)(2,1)} %constant_dynamic-slice_fusion.6), channel_id=1, source_target_pairs={{0,8},{8,0},{16,24},{24,16},{1,9},{9,1},{17,25},{25,17},{2,10},{10... | collective-permute-start | bytes 7962632 | tf_op jit(solution)/shard_map/ppermute | solution.py:54
  664.3 231.3 %all-reduce.8.cloned.1.call-start = ((), (), s32[]{:S(2)}) async-start(), calls=%async_computation.4 | async-start | bytes 10616832 | tf_op jit(solution)/shard_map/psum | solution.py:580
  676.2 46.8 %collective-permute-start.89 = (bf16[4,144,512]{2,1,0:T(8,128)(2,1)}, bf16[4,144,512]{2,1,0:T(8,128)(2,1)S(1)}, u32[]{:S(2)}, u32[]{:S(2)}) collective-permute-start(bf16[4,144,512]{2,1,0:T(8,128)(2,1)} %get-tuple-element.267), channel_id=1, source_target_pairs={{2,6},{4,0},{3,7},{5,1},{10,14},{12,8},{11,15},{13,9},{18,22},{20,... | collective-permute-start | bytes 1769480 | tf_op jit(solution)/shard_map/ppermute | solution.py:124
  677.4 51.9 %collective-permute-start.88 = (bf16[4,144,512]{2,1,0:T(8,128)(2,1)}, bf16[4,144,512]{2,1,0:T(8,128)(2,1)S(1)}, u32[]{:S(2)}, u32[]{:S(2)}) collective-permute-start(bf16[4,144,512]{2,1,0:T(8,128)(2,1)} %get-tuple-element.267), channel_id=1, source_target_pairs={{0,6},{6,0},{1,7},{7,1},{8,14},{14,8},{9,15},{15,9},{16,22},{22,16... | collective-permute-start | bytes 1769480 | tf_op jit(solution)/shard_map/ppermute | solution.py:123
  706.3 50.0 %collective-permute-start.98 = (bf16[2,160,1024]{2,1,0:T(8,128)(2,1)S(1)}, bf16[2,160,1024]{2,1,0:T(8,128)(2,1)S(1)}, u32[]{:S(2)}, u32[]{:S(2)}) collective-permute-start(bf16[2,160,1024]{2,1,0:T(8,128)(2,1)S(1)} %get-tuple-element.264), channel_id=1, source_target_pairs={{2,6},{4,0},{3,7},{5,1},{10,14},{12,8},{11,15},{13,9},{18,22},{20,... | collective-permute-start | bytes 1966088 | tf_op jit(solution)/shard_map/ppermute | solution.py:124
  714.9 41.4 %collective-permute-start.97 = (bf16[2,160,1024]{2,1,0:T(8,128)(2,1)S(1)}, bf16[2,160,1024]{2,1,0:T(8,128)(2,1)S(1)}, u32[]{:S(2)}, u32[]{:S(2)}) collective-permute-start(bf16[2,160,1024]{2,1,0:T(8,128)(2,1)S(1)} %get-tuple-element.264), channel_id=1, source_target_pairs={{0,6},{6,0},{1,7},{7,1},{8,14},{14,8},{9,15},{15,9},{16,22},{22,16... | collective-permute-start | bytes 1966088 | tf_op jit(solution)/shard_map/ppermute | solution.py:123
  722.9 32.0 %collective-permute-start.96 = (bf16[2,160,1024]{2,1,0:T(8,128)(2,1)S(1)}, bf16[2,160,1024]{2,1,0:T(8,128)(2,1)S(1)}, u32[]{:S(2)}, u32[]{:S(2)}) collective-permute-start(bf16[2,160,1024]{2,1,0:T(8,128)(2,1)S(1)} %get-tuple-element.262), channel_id=1, source_target_pairs={{0,2},{2,0},{4,6},{6,4},{1,3},{3,1},{5,7},{7,5},{8,10},{10,8},{12,... | collective-permute-start | bytes 1966088 | tf_op jit(solution)/shard_map/ppermute | solution.py:125
  729.3 26.9 %collective-permute-start.100 = (bf16[2,160,1024]{2,1,0:T(8,128)(2,1)S(1)}, bf16[2,160,1024]{2,1,0:T(8,128)(2,1)S(1)}, u32[]{:S(2)}, u32[]{:S(2)}) collective-permute-start(bf16[2,160,1024]{2,1,0:T(8,128)(2,1)S(1)} %add_convert_fusion.6), channel_id=1, source_target_pairs={{2,4},{4,2},{3,5},{5,3},{10,12},{12,10},{11,13},{13,11},{18,20},{2... | collective-permute-start | bytes 1966088 | tf_op jit(solution)/shard_map/ppermute | solution.py:127
  757.8 146.9 %collective-permute-start.101 = (bf16[160,1024]{1,0:T(8,128)(2,1)}, bf16[160,1024]{1,0:T(8,128)(2,1)}, u32[]{:S(2)}, u32[]{:S(2)}) collective-permute-start(bf16[160,1024]{1,0:T(8,128)(2,1)} %fusion.148), channel_id=1, source_target_pairs={{0,16},{8,24},{16,0},{24,8},{1,17},{9,25},{17,1},{25,9},{2,18},{10... | collective-permute-start | bytes 983048 | tf_op jit(solution)/shard_map/ppermute | solution.py:54
  763.7 143.6 %collective-permute-start.103 = (bf16[1152,1152]{1,0:T(8,128)(2,1)}, bf16[1152,1152]{1,0:T(8,128)(2,1)S(1)}, u32[]{:S(2)}, u32[]{:S(2)}) collective-permute-start(bf16[1152,1152]{1,0:T(8,128)(2,1)} %all-reduce.6.cloned.1.call-done.mine), channel_id=1, source_target_pairs={{0,8},{8,0},{16,24},{24,16},{1,9},{9,1},{17,25},{25,17},{2,10},{10... | collective-permute-start | bytes 7962632 | tf_op jit(solution)/shard_map/ppermute | solution.py:54
  (210 other events, 2249.7 us)
Sparse Core Ops, SparseCore 0:
  87.0 30.0 all-gather.3
  120.0 69.7 all-gather.5
  202.2 62.1 all-gather.7
  664.5 85.9 all-reduce.5
  753.4 142.1 all-reduce.7
